TPU v7x, 256 devices: a whole 4x4x8 slice. The times are simulated.
256 devices in a mesh: row: 32 (over z, x), col: 8 (over y, core).
Axes of the slice: x: 4, y: 4, z: 8, core: 2. Of those that a mesh axis runs over, the one named last changes fastest.
Arguments:
- panel: float32 [32768, 2048], P('row', 'col')
- rhs: float32 [32768, 2048], P('row', 'col'), may hold values from -6 to 6
Outputs:
- trailing: float32 [32768, 2048], P('row', 'col')
- solution: float32 [2048, 2048], P(None, 'col')
Inputs may be any that keep to these rules, and one draw needn't show every extreme that they name: The blocks L0 and L1 are lower triangular with diagonal entries between 1 and 2; P[0, 0] is zero in the columns of block 1.
All inputs are finite; a program needn't handle non-finite values.
Results may differ from a plain program's by a relative error of at most 0.000094.
Values sent between devices are 32-bit elements; how exact they have to be, the bound alone decides.
No kernel may reach another device: no remote copies, remote signals or barrier semaphores. Data moves between devices by JAX's collectives and lax.ppermute only.
A program may use at most 128 MiB of HBM per device.

v0:
```python
import jax
import jax.numpy as jnp
from jax import lax
from jax.sharding import PartitionSpec as P

NB = 1024


exact = lax.Precision.HIGHEST


def spread(shard, axis, root):
    mine = lax.axis_index(axis) == root
    return lax.psum(jnp.where(mine, shard, jnp.zeros_like(shard)), axis)


def tri_solve(matrix, targets):
    return jax.scipy.linalg.solve_triangular(matrix, targets, lower=True)


def body(panel, rhs):
    rows_dev = panel.shape[0]
    grid_row = lax.axis_index("row")
    gathered = lax.all_gather(panel, "col", axis=1, tiled=True)

    def update(stacked):
        return jnp.dot(gathered, stacked, precision=exact, preferred_element_type=jnp.float32)

    def solve(block, current):
        triangle = gathered[:, block * NB : (block + 1) * NB]
        triangle = jnp.where(grid_row == block, triangle, jnp.eye(NB, dtype=jnp.float32))
        solved = tri_solve(triangle, current)
        return spread(solved, "row", block)

    nothing = jnp.zeros((NB, rhs.shape[1]), jnp.float32)
    solved_one = solve(0, rhs)
    updated = rhs - update(jnp.concatenate([solved_one, nothing], axis=0))
    solved_two = solve(1, updated)
    updated = updated - update(jnp.concatenate([nothing, solved_two], axis=0))
    keep_rows = (jnp.arange(rows_dev, dtype=jnp.int32) >= NB) | (grid_row >= 2)
    updated = jnp.where(keep_rows[:, None], updated, jnp.float32(0.0))
    return (updated, jnp.concatenate([solved_one, solved_two], axis=0))


def solution(mesh):
    placed = (P("row", "col"), P("row", "col"))
    return jax.shard_map(
        body,
        mesh=mesh,
        in_specs=placed,
        out_specs=(P("row", "col"), P(None, "col")),
        check_vma=False,
    )
```

profile of v0, /device:TPU:6, one launch (start us, length us, event | category | flops | bytes accessed | tf_op | source)
XLA Modules:
  0.0 526.6 jit_solution(10572802646873156275)
XLA Ops:
  7.2 0.7 all-gather.2.cloned.1.call-update
  8.0 57.1 %all-gather.2.cloned.1.call-done = f32[1024,2048]{1,0:T(8,128)} async-done(((f32[1024,256]{1,0:T(8,128)}), f32[1024,2048]{1,0:T(8,128)}) %all-gather.2.cloned.1.call-update) | async-done | bytes 8388624 | tf_op jit(solution)/shard_map/all_gather | solution.py:24
  65.1 8.2 %fusion.1 = (f32[1024,1024]{1,0:T(8,128)}, f32[1024,1024]{1,0:T(8,128)}) fusion(f32[1024,2048]{1,0:T(8,128)} %all-gather.2.cloned.1.call-done, pred[]{:T(512)S(6)} %eq.16, pred[]{:T(512)S(6)} %eq.14), kind=kLoop, calls=%fused_computation.7 | loop fusion | flops 7340032 | bytes 16777218 | tf_op jit(solution)/shard_map/jit(_solve_triangular)/triangular_solve | solution.py:18
  73.3 23.6 %while.4 = (s32[]{:T(128)}, f32[1024,1024]{1,0:T(8,128)}, s32[8,2]{0,1:T(2,128)S(1)}, f32[8,128,128]{2,1,0:T(8,128)S(1)}, s32[]{:T(128)}) while((s32[]{:T(128)}, f32[1024,1024]{1,0:T(8,128)}, s32[8,2]{0,1:T(2,128)S(1)}, f32[8,128,128]{2,1,0:T(8,128)S(1)}, s32[]{:T(128)}) %tuple.84), condition=%wide.while_cond, body=%wide.while_body.sunk | while | flops 2 | bytes 131181 | solution.py:18
  73.4 0.6 fusion.118
  74.0 2.3 bitcast_dynamic-update-slice_fusion.4
  76.3 0.6 fusion.118
  76.9 2.3 bitcast_dynamic-update-slice_fusion.4
  79.3 0.6 fusion.118
  79.9 2.3 bitcast_dynamic-update-slice_fusion.4
  82.3 0.6 fusion.118
  82.9 2.3 bitcast_dynamic-update-slice_fusion.4
  85.2 0.6 fusion.118
  85.8 2.3 bitcast_dynamic-update-slice_fusion.4
  88.2 0.6 fusion.118
  88.8 2.3 bitcast_dynamic-update-slice_fusion.4
  91.1 0.6 fusion.118
  91.7 2.3 bitcast_dynamic-update-slice_fusion.4
  94.1 0.6 fusion.118
  94.7 2.2 bitcast_dynamic-update-slice_fusion.4
  96.9 78.6 %custom-call.4 = f32[8,128,128]{1,2,0:T(8,128)S(1)} custom-call(f32[8,128,128]{2,1,0:T(8,128)S(1)} %get-tuple-element.17), custom_call_target="InvertDiagBlocksLowerTriangular" | custom-call | tf_op jit(solution)/shard_map/jit(_solve_triangular)/triangular_solve | solution.py:18
  175.8 1.1 convolution_subtract_fusion.11
  177.3 1.2 convolution_subtract_fusion.7
  178.5 0.3 constant_dynamic-update-slice_fusion.15
  178.8 1.3 convolution_subtract_fusion.6
  180.1 0.3 constant_dynamic-update-slice_fusion.14
  180.4 1.4 convolution_subtract_fusion.5
  182.1 1.5 convolution_subtract_fusion.4
  183.9 1.5 convolution_subtract_fusion.10
  185.8 1.6 convolution_subtract_fusion.13
  187.7 1.0 broadcast_select_fusion.1
  189.1 22.7 %while.5 = (s32[]{:T(128)}, f32[1024,1024]{1,0:T(8,128)}, s32[8,2]{0,1:T(2,128)S(1)}, f32[8,128,128]{2,1,0:T(8,128)S(1)}, s32[]{:T(128)}) while((s32[]{:T(128)}, f32[1024,1024]{1,0:T(8,128)}, s32[8,2]{0,1:T(2,128)S(1)}, f32[8,128,128]{2,1,0:T(8,128)S(1)}, s32[]{:T(128)}) %tuple.96), condition=%wide.while_cond.clone, body=%wide.while_body.clone.sunk | while | flops 2 | bytes 131181 | solution.py:18
  189.1 0.5 fusion.119
  189.7 2.2 bitcast_dynamic-update-slice_fusion.5
  192.0 0.5 fusion.119
  192.5 2.2 bitcast_dynamic-update-slice_fusion.5
  194.8 0.5 fusion.119
  195.4 2.2 bitcast_dynamic-update-slice_fusion.5
  197.7 0.5 fusion.119
  198.2 2.2 bitcast_dynamic-update-slice_fusion.5
  200.5 0.5 fusion.119
  201.0 2.2 bitcast_dynamic-update-slice_fusion.5
  203.3 0.5 fusion.119
  203.9 2.2 bitcast_dynamic-update-slice_fusion.5
  206.2 0.5 fusion.119
  206.7 2.2 bitcast_dynamic-update-slice_fusion.5
  209.0 0.5 fusion.119
  209.6 2.1 bitcast_dynamic-update-slice_fusion.5
  211.7 78.6 %custom-call.5 = f32[8,128,128]{1,2,0:T(8,128)S(1)} custom-call(f32[8,128,128]{2,1,0:T(8,128)S(1)} %get-tuple-element.18), custom_call_target="InvertDiagBlocksLowerTriangular" | custom-call | tf_op jit(solution)/shard_map/jit(_solve_triangular)/triangular_solve | solution.py:18
  290.3 47.4 %all-reduce.5.cloned.1.call-done = f32[1024,256]{1,0:T(8,128)} async-done(((f32[1024,256]{1,0:T(8,128)}), f32[1024,256]{1,0:T(8,128)}) %all-reduce.5.cloned.1.call-update) | async-done | bytes 1048592 | tf_op jit(solution)/shard_map/psum | solution.py:14
  337.7 9.4 %fusion.18 = f32[1024,256]{1,0:T(8,128)S(1)} fusion(f32[1024,256]{1,0:T(8,128)S(1)} %copy-done.2, f32[1024,2048]{1,0:T(8,128)} %all-gather.2.cloned.1.call-done, f32[1024,256]{1,0:T(8,128)} %all-reduce.5.cloned.1.call-done), kind=kOutput, calls=%fused_computation.19 | convolution fusion | flops 6442713088 | bytes 11534336 | tf_op jit(solution)/shard_map/dot_general | solution.py:27
  347.5 1.1 convolution_subtract_fusion.9
  348.6 0.3 constant_dynamic-update-slice_fusion.41
  348.9 1.2 convolution_subtract_fusion.3
  350.1 0.3 constant_dynamic-update-slice_fusion.40
  350.4 1.3 convolution_subtract_fusion.2
  352.1 1.4 convolution_subtract_fusion.1
  353.8 1.6 convolution_subtract_fusion
  355.7 1.5 convolution_subtract_fusion.8
  357.5 1.6 convolution_subtract_fusion.12
  359.5 1.0 broadcast_select_fusion
  360.5 146.9 %all-reduce.7.cloned.1.call-done = f32[1024,256]{1,0:T(8,128)} async-done(((f32[1024,256]{1,0:T(8,128)}), f32[1024,256]{1,0:T(8,128)}) %all-reduce.7.cloned.1.call-update) | async-done | bytes 1048592 | tf_op jit(solution)/shard_map/psum | solution.py:14
  507.4 2.8 pad_maximum_fusion
  510.2 9.9 %fusion.15 = f32[1024,256]{1,0:T(8,128)} fusion(f32[1024,256]{1,0:T(8,128)S(1)} %fusion.18, f32[1024,2048]{1,0:T(8,128)} %all-gather.2.cloned.1.call-done, f32[1024,256]{1,0:T(8,128)S(1)} %copy-done, pred[1024]{0:T(1024)(128)(4,1)S(1)} %fusion.81), kind=kOutput, calls=%fused_computation.18 | convolution fusion | flops 6442975232 | bytes 11535360 | tf_op jit(solution)/shard_map/dot_general | solution.py:27
  (44 shorter events, 5.4 us)
Async XLA Ops:
  7.2 57.9 %all-gather.2.cloned.1.call-start = ((), (), s32[]{:S(2)}) async-start(), calls=%async_computation | async-start | bytes 9437184 | tf_op jit(solution)/shard_map/all_gather | solution.py:24
  7.9 329.8 %all-reduce.5.cloned.1.call-start = ((), (), s32[]{:S(2)}) async-start(), calls=%async_computation.1 | async-start | bytes 2097152 | tf_op jit(solution)/shard_map/psum | solution.py:14
  8.0 167.5 %copy-start.2 = (f32[1024,256]{1,0:T(8,128)S(1)}, f32[1024,256]{1,0:T(8,128)}, u32[]{:S(2)}) copy-start(f32[1024,256]{1,0:T(8,128)} %param.5) | copy-start | bytes 3145732
  188.8 318.6 %all-reduce.7.cloned.1.call-start = ((), (), s32[]{:S(2)}) async-start(), calls=%async_computation.2 | async-start | bytes 2097152 | tf_op jit(solution)/shard_map/psum | solution.py:14
  353.8 153.6 %copy-start.1 = (f32[1024,256]{1,0:T(8,128)S(1)}, f32[1024,256]{1,0:T(8,128)}, u32[]{:S(2)}) copy-start(f32[1024,256]{1,0:T(8,128)} %all-reduce.5.cloned.1.call-done) | copy-start | bytes 3145732
  507.4 2.8 copy-start
Sparse Core Ops, SparseCore 0:
  9.8 55.1 all-gather.1
  188.9 148.7 all-reduce.4
  360.6 146.7 all-reduce.6
where the time goes:
time: 529 us; the launch traced here: 527 us
  waiting for transfers between devices  252 us (48%)
  other arithmetic  170 us (32%)
  local copies, waits for them, and re-layouts  46 us (9%)
  matrix products  43.7 us (8%)
  between operations  14.1 us (3%)
    psum x2, waiting for transfers between devices, spread(): return lax.psum(jnp.where(mine, shard, jnp.zeros_like(shard)), axis)  194 us
    another operation x4, other arithmetic, tri_solve(): return jax.scipy.linalg.solve_triangular(matrix, targets, lower=True)  165 us
    all_gather x1, waiting for transfers between devices, body(): gathered = lax.all_gather(panel, 'col', axis=1, tiled=True)  57.1 us
    another operation x51, local copies, waits for them, and re-layouts, tri_solve(): return jax.scipy.linalg.solve_triangular(matrix, targets, lower=True)  46 us
    another operation x30, matrix products, tri_solve(): return jax.scipy.linalg.solve_triangular(matrix, targets, lower=True)  24.3 us
    dot_general x2, matrix products, update(): jnp.dot(gathered, stacked, precision=exact, preferred_element_type=jnp.fl...  19.4 us
  transfers between devices with their start and end apart: 3, of which 3 were waited for; matrix products, arithmetic and copies ran while one was open for 19% of the time, Pallas kernels for 0%

commit v1 on v0

v1 whole, which is shorter than its diff:
```python
import functools

import jax
import jax.numpy as jnp
from jax import lax
from jax.experimental import pallas as pl
from jax.experimental.pallas import tpu as pltpu
from jax.sharding import PartitionSpec as P

NB = 1024
Q = 256
PARTS = 4
XS = 4
ZS = 8
COLS = 8
F32 = jnp.float32
BF16 = jnp.bfloat16


def halves(value):
    high = value.astype(BF16)
    return high, (value - high.astype(F32)).astype(BF16)


def product(left, right):
    dot = functools.partial(jnp.dot, preferred_element_type=F32)
    return dot(left[0], right[0]) + (dot(left[0], right[1]) + dot(left[1], right[0]))


def invert_kernel(flag_ref, block_ref, out_ref):
    @pl.when(flag_ref[0] == 1)
    def _():
        rows = lax.broadcasted_iota(jnp.int32, (Q, Q), 0)
        cols = lax.broadcasted_iota(jnp.int32, (Q, Q), 1)
        block = block_ref[...]
        inverse = jnp.where(rows == cols, 1.0 / jnp.where(rows == cols, block, 1.0), 0.0)
        level = 0
        while (1 << level) < Q:
            pair = (rows >> (level + 1)) == (cols >> (level + 1))
            below = pair & (((rows >> level) & 1) == 1) & (((cols >> level) & 1) == 0)
            parts = halves(inverse)
            inner = product(halves(jnp.where(below, block, 0.0)), parts)
            inverse = inverse - product(parts, halves(inner))
            level += 1
        out_ref[...] = inverse


def invert(flag, block):
    return pl.pallas_call(
        invert_kernel,
        out_shape=jax.ShapeDtypeStruct((Q, Q), F32),
        in_specs=[pl.BlockSpec(memory_space=pltpu.SMEM), pl.BlockSpec(memory_space=pltpu.VMEM)],
        out_specs=pl.BlockSpec(memory_space=pltpu.VMEM),
        compiler_params=pltpu.CompilerParams(vmem_limit_bytes=32 << 20),
        name="invert",
    )(flag, block)


def solve_kernel(block, flag_ref, gathered, inverses, rhs, *rest):
    if block:
        first, out, panel_buf, inv_buf, rhs_buf, first_buf, sems = rest
    else:
        out, panel_buf, inv_buf, rhs_buf, sems = rest

    @pl.when(flag_ref[0] == 1)
    def _():
        if block:
            moves = [(first, first_buf), (gathered, panel_buf), (inverses, inv_buf), (rhs, rhs_buf)]
        else:
            moves = [(gathered.at[:, pl.ds(0, NB)], panel_buf), (inverses, inv_buf), (rhs, rhs_buf)]
        copies = [pltpu.make_async_copy(a, b, sems.at[i]) for i, (a, b) in enumerate(moves)]
        for copy in copies:
            copy.start()
        for copy in copies:
            copy.wait()
        base = block * NB
        targets = [rhs_buf[pl.ds(i * Q, Q), :] for i in range(PARTS)]
        if block:
            known = [halves(first_buf[pl.ds(j * Q, Q), :]) for j in range(PARTS)]
            for i in range(PARTS):
                for j in range(PARTS):
                    part = panel_buf[pl.ds(i * Q, Q), pl.ds(j * Q, Q)]
                    targets[i] = targets[i] - product(halves(part), known[j])
        for i in range(PARTS):
            inv = halves(inv_buf[pl.ds(i * Q, Q), :])
            value = product(inv, halves(targets[i]))
            out[pl.ds(i * Q, Q), :] = value
            parts = halves(value)
            for k in range(i + 1, PARTS):
                part = panel_buf[pl.ds(k * Q, Q), pl.ds(base + i * Q, Q)]
                targets[k] = targets[k] - product(halves(part), parts)


def solve(block, flag, gathered, inverses, rhs, *first):
    width = rhs.shape[1]
    buffers = [
        pltpu.VMEM((NB, (1 + block) * NB), F32),
        pltpu.VMEM((NB, Q), F32),
        pltpu.VMEM((NB, width), F32),
    ]
    if block:
        buffers.append(pltpu.VMEM((NB, width), F32))
    return pl.pallas_call(
        functools.partial(solve_kernel, block),
        out_shape=jax.ShapeDtypeStruct((NB, width), F32),
        in_specs=[pl.BlockSpec(memory_space=pltpu.SMEM)] + [pl.BlockSpec(memory_space=pl.ANY)] * (3 + block),
        out_specs=pl.BlockSpec(memory_space=pltpu.VMEM),
        scratch_shapes=buffers + [pltpu.SemaphoreType.DMA((4,))],
        compiler_params=pltpu.CompilerParams(vmem_limit_bytes=48 << 20),
        name="solve%d" % block,
    )(flag, gathered, inverses, rhs, *first)


def split_kernel(value_ref, high_ref, low_ref):
    high, low = halves(value_ref[...])
    high_ref[...] = high
    low_ref[...] = low


def split(value):
    rows, cols = value.shape
    step = 128
    spec = pl.BlockSpec((step, cols), lambda i: (i, 0))
    return pl.pallas_call(
        split_kernel,
        grid=(rows // step,),
        out_shape=[jax.ShapeDtypeStruct(value.shape, BF16)] * 2,
        in_specs=[spec],
        out_specs=[spec, spec],
        compiler_params=pltpu.CompilerParams(vmem_limit_bytes=32 << 20),
        name="split",
    )(value)


def update_kernel(last, place_ref, high_ref, low_ref, target_ref, *rest):
    if last:
        pieces, before, (out, whole, solved_high, solved_low) = rest[:5], rest[5], rest[6:]
    else:
        pieces, (out, whole, solved_high, solved_low) = rest[:5], rest[5:]

    @pl.when(pl.program_id(0) == 0)
    def _():
        if last:
            whole[pl.ds(0, NB), :] = before[...]
        turn = place_ref[0]
        lengths = (Q, Q, Q // 2, Q // 2, Q)
        slots = (0, 1, 2, 2, 3)
        shifts = (0, 0, 0, Q // 2, 0)
        for piece, length, slot, shift in zip(pieces, lengths, slots, shifts):
            start = pl.multiple_of(((slot + turn) & 3) * Q + shift, Q // 2)
            value = piece[...]
            high, low = halves(value)
            solved_high[pl.ds(start, length), :] = high
            solved_low[pl.ds(start, length), :] = low
            whole[pl.ds(start + (NB if last else 0), length), :] = value

    result = target_ref[...] - product((high_ref[...], low_ref[...]), (solved_high[...], solved_low[...]))
    if last:
        out[...] = jnp.where(place_ref[1] >= 2, result, 0.0)
    else:
        out[...] = result


def update(last, place, parts, target, pieces, *before):
    rows, width = target.shape
    step = Q
    panel_spec = pl.BlockSpec((step, NB), lambda i: (i, int(last)))
    target_spec = pl.BlockSpec((step, width), lambda i: (i, 0))

    def fixed(length):
        return pl.BlockSpec((length, width), lambda i: (0, 0))

    held = 2 * NB if last else NB
    return pl.pallas_call(
        functools.partial(update_kernel, last),
        grid=(rows // step,),
        out_shape=[jax.ShapeDtypeStruct((rows, width), F32), jax.ShapeDtypeStruct((held, width), F32)],
        in_specs=[pl.BlockSpec(memory_space=pltpu.SMEM), panel_spec, panel_spec, target_spec]
        + [fixed(piece.shape[0]) for piece in pieces]
        + [fixed(NB)] * len(before),
        out_specs=[target_spec, fixed(held)],
        scratch_shapes=[pltpu.VMEM((NB, width), BF16)] * 2,
        compiler_params=pltpu.CompilerParams(vmem_limit_bytes=48 << 20),
        name="update%d" % int(last),
    )(place, *parts, target, *pieces, *before)


def share_inverses(inverse, row, col):
    y, core = col // 2, col % 2

    def pairs(moves):
        return [(r * COLS + 2 * a + k, r * COLS + 2 * b + k) for r in (0, 1) for a, b in moves[r] for k in (0, 1)]

    both = ("row", "col")
    swap = lax.ppermute(inverse, both, pairs([[(0, 1), (1, 0)], [(2, 3), (3, 2)]]))
    out = lax.ppermute(inverse, both, pairs([[(0, 3), (1, 2)], [(2, 1), (3, 0)]]))
    relay = lax.ppermute(out, both, pairs([[(3, 2), (2, 3)], [(1, 0), (0, 1)]]))
    is_low = y == jnp.where(row == 0, 0, 2)
    is_high = y == jnp.where(row == 0, 1, 3)
    got_low = y == jnp.where(row == 0, 3, 1)
    low = jnp.where(is_low, inverse, jnp.where(is_high, swap, jnp.where(got_low, out, relay)))
    high = jnp.where(is_low, swap, jnp.where(is_high, inverse, jnp.where(got_low, relay, out)))
    mine = jnp.stack([low, high])
    cores = [(r * COLS + c, r * COLS + (c ^ 1)) for r in (0, 1) for c in range(COLS)]
    theirs = lax.ppermute(mine, both, cores)
    first = jnp.where(core == 0, mine, theirs)
    second = jnp.where(core == 0, theirs, mine)
    return jnp.stack([first, second], axis=1).reshape(PARTS * Q, Q)


def spread(solved, root, row, ahead=None):
    z = row // XS

    def piece(i, value=solved):
        return value[i * Q : (i + 1) * Q]

    sent = [i for i in range(1, PARTS) if ahead is None or i != 1]
    mine = jnp.zeros_like(piece(0))
    for i in sent:
        mine = mine + lax.ppermute(piece(i), "row", [(root, (root + i) % XS)])
    if ahead is not None:
        mine = jnp.where(row == root + 1, piece(1, ahead), mine)
    mine = jnp.where(row == root, piece(0), mine)

    def along_z(moves):
        return [(a * XS + x, b * XS + x) for a, b in moves for x in range(XS)]

    near = lax.ppermute(mine, "row", along_z([(0, 3)]))
    far = lax.ppermute(mine, "row", along_z([(0, 5)]))
    mine = jnp.where(z == 0, mine, near + far)
    up = lax.ppermute(mine, "row", along_z([(0, 1), (3, 4), (5, 6)]))
    down = lax.ppermute(mine, "row", along_z([(0, 7), (3, 2)]))
    mine = jnp.where((z == 0) | (z == 3) | (z == 5), mine, up + down)

    to_next = [(r, r // XS * XS + (r + 1) % XS) for r in range(ZS * XS)]
    to_last = [(b, a) for a, b in to_next]
    after = lax.ppermute(mine, "row", to_last)
    before = lax.ppermute(mine, "row", to_next)
    over_top = lax.ppermute(after[: Q // 2], "row", to_last)
    over_rest = lax.ppermute(before[Q // 2 :], "row", to_next)
    return mine, after, over_top, over_rest, before


def body(panel, rhs):
    row = lax.axis_index("row")
    col = lax.axis_index("col")
    gathered = lax.all_gather(panel, "col", axis=1, tiled=True)

    holds = ((row == 0) & (col < PARTS)) | ((row == 1) & (col >= PARTS))
    diagonal = lax.dynamic_slice(panel, ((col % PARTS) * Q, 0), (Q, Q))
    inverse = invert(holds.astype(jnp.int32)[None], diagonal)
    inverses = share_inverses(inverse, row, col)
    parts = split(gathered)

    def flag(r):
        return (row == r).astype(jnp.int32)[None]

    def place(root):
        return jnp.stack([(row - root) % XS, row])

    one = solve(0, flag(0), gathered, inverses, rhs)
    ahead = lax.ppermute(one, "row", [(0, 1)])
    two = solve(1, flag(1), gathered, inverses, rhs, ahead)
    pieces_one = spread(one, 0, row, ahead)
    pieces_two = spread(two, 1, row)
    updated, solved_one = update(False, place(0), parts, rhs, pieces_one)
    return tuple(update(True, place(1), parts, updated, pieces_two, solved_one))


def solution(mesh):
    placed = (P("row", "col"), P("row", "col"))
    return jax.shard_map(
        body,
        mesh=mesh,
        in_specs=placed,
        out_specs=(P("row", "col"), P(None, "col")),
        check_vma=False,
    )
```

time: 529 us -> 180 us (0.34)
  the two profiles are of different devices: /device:TPU:6 before, /device:TPU:48 now
where the time goes in v1:
time: 180 us; the launch traced here: 179 us
  waiting for transfers between devices  112 us (62%)
  starting transfers between devices  29 us (16%)
  between operations  14.6 us (8%)
  Pallas kernels  11.4 us (6%)
  local copies, waits for them, and re-layouts  9.99 us (6%)
  other arithmetic  1.8 us (1%)
    ppermute x2, waiting for transfers between devices, spread(): up = lax.ppermute(mine, 'row', along_z([(0, 1), (3, 4), (5, 6)]))  57 us
    all_gather x1, waiting for transfers between devices, body(): gathered = lax.all_gather(panel, 'col', axis=1, tiled=True)  51.2 us
    pallas_call x2, Pallas kernels, update(): pl.pallas_call(functools.partial(update_kernel, last), grid=(rows // step...  10.1 us
    unnamed x8, local copies, waits for them, and re-layouts  7.37 us
    ppermute x2, starting transfers between devices, spread(): over_top = lax.ppermute(after[:Q // 2], 'row', to_last)  6.73 us
    ppermute x2, starting transfers between devices, spread(): after = lax.ppermute(mine, 'row', to_last)  6.45 us
    ppermute x5, starting transfers between devices, spread(): mine = mine + lax.ppermute(piece(i), 'row', [(root, (root + i) % XS)])  4.06 us
  transfers between devices with their start and end apart: 27, of which 5 were waited for; matrix products, arithmetic and copies ran while one was open for 2% of the time, Pallas kernels for 3%

profile of v1, /device:TPU:48, one launch (start us, length us, event | category | flops | bytes accessed | tf_op | source)
XLA Modules:
  0.0 178.9 jit_solution(9279002440568356609)
XLA Ops:
  7.2 0.0 all-gather.2.cloned.1.call-start
  7.2 0.7 all-gather.2.cloned.1.call-update
  7.9 1.0 constant_dynamic-slice_fusion.block_ref
  8.9 0.7 collective-permute-start.1
  9.6 0.7 collective-permute-start
  10.3 0.7 collective-permute-start.2
  11.0 0.0 copy-start.3
  11.0 0.0 collective-permute-done
  11.1 0.1 select_bitcast_fusion.3
  11.2 0.8 collective-permute-start.3
  12.0 0.0 collective-permute-done.3
  12.0 0.1 select_bitcast_fusion.1
  12.1 0.1 pad_maximum_fusion
  12.2 0.1 copy.4
  12.3 51.2 %all-gather.2.cloned.1.call-done.value_ref.gathered = f32[1024,2048]{1,0:T(8,128)} async-done(((f32[1024,256]{1,0:T(8,128)}), f32[1024,2048]{1,0:T(8,128)}) %all-gather.2.cloned.1.call-update) | async-done | bytes 8388624 | tf_op jit(solution)/shard_map/all_gather | solution.py:247
  63.5 1.7 collective-permute-start.4
  65.2 0.8 fusion.2
  66.0 0.7 collective-permute-start.6
  66.7 1.4 collective-permute-start.5
  68.1 0.0 collective-permute-done.4.rest_0_
  68.1 0.1 fusion.1
  68.2 0.7 collective-permute-start.16
  68.9 0.7 collective-permute-start.17
  69.5 0.7 collective-permute-start.15
  70.2 0.0 collective-permute-done.6
  70.3 1.1 fusion
  71.4 0.7 collective-permute-start.8
  72.0 0.7 collective-permute-start.7
  72.7 0.0 collective-permute-done.16
  72.7 0.0 collective-permute-done.15
  72.8 0.1 slice_select_fusion
  72.8 0.7 collective-permute-start.19
  73.5 0.7 collective-permute-start.18
  74.2 0.0 collective-permute-done.7
  74.2 0.1 add_select_fusion.3
  74.3 0.7 collective-permute-start.10
  75.0 1.3 collective-permute-start.9
  76.3 0.0 collective-permute-done.18
  76.3 0.1 add_select_fusion.1
  76.4 0.7 collective-permute-start.21
  77.1 1.3 collective-permute-start.20
  78.4 0.0 collective-permute-done.10
  78.4 56.7 %collective-permute-done.9 = f32[256,256]{1,0:T(8,128)S(1)} collective-permute-done((f32[256,256]{1,0:T(8,128)S(1)}, f32[256,256]{1,0:T(8,128)S(1)}, u32[]{:S(2)}, u32[]{:S(2)}) %collective-permute-start.9) | collective-permute-done | bytes 262176 | tf_op jit(solution)/shard_map/ppermute | solution.py:231
  135.1 0.1 collective-permute-start.13
  135.2 3.2 %collective-permute-start.11 = (f32[256,256]{1,0:T(8,128)S(1)}, f32[256,256]{1,0:T(8,128)S(1)}, u32[]{:S(2)}, u32[]{:S(2)}) collective-permute-start(f32[256,256]{1,0:T(8,128)S(1)} %add_select_fusion.2.rest_0_), channel_id=1, source_target_pairs={{8,0},{16,8},{24,16},{0,24},{40,32},{48,40},{56,48},{32,56},{72,64... | collective-permute-start | bytes 786440 | tf_op jit(solution)/shard_map/ppermute | solution.py:237
  138.4 0.0 collective-permute-done.21
  138.4 0.3 collective-permute-done.20
  138.8 0.3 collective-permute-start.24
  139.0 3.2 %collective-permute-start.22 = (f32[256,256]{1,0:T(8,128)S(1)}, f32[256,256]{1,0:T(8,128)S(1)}, u32[]{:S(2)}, u32[]{:S(2)}) collective-permute-start(f32[256,256]{1,0:T(8,128)S(1)} %add_select_fusion.rest_0_), channel_id=1, source_target_pairs={{8,0},{16,8},{24,16},{0,24},{40,32},{48,40},{56,48},{32,56},{72,64... | collective-permute-start | bytes 786440 | tf_op jit(solution)/shard_map/ppermute | solution.py:237
  142.3 2.3 %collective-permute-done.13.rest_4_ = f32[256,256]{1,0:T(8,128)S(1)} collective-permute-done((f32[256,256]{1,0:T(8,128)S(1)}, f32[256,256]{1,0:T(8,128)S(1)}, u32[]{:S(2)}, u32[]{:S(2)}) %collective-permute-start.13) | collective-permute-done | bytes 262176 | tf_op jit(solution)/shard_map/ppermute | solution.py:238
  144.6 0.1 collective-permute-start.14
  144.7 0.7 slice.52
  145.4 3.4 %collective-permute-start.12 = (f32[128,256]{1,0:T(8,128)}, f32[128,256]{1,0:T(8,128)S(1)}, u32[]{:S(2)}, u32[]{:S(2)}) collective-permute-start(f32[128,256]{1,0:T(8,128)} %slice.52), channel_id=1, source_target_pairs={{8,0},{16,8},{24,16},{0,24},{40,32},{48,40},{56,48},{32,56},{72,64... | collective-permute-start | bytes 393224 | tf_op jit(solution)/shard_map/ppermute | solution.py:239
  148.8 1.0 collective-permute-done.24.rest_4_
  149.8 0.1 collective-permute-start.25
  149.9 3.3 %collective-permute-start.23 = (f32[128,256]{1,0:T(8,128)S(1)}, f32[128,256]{1,0:T(8,128)S(1)}, u32[]{:S(2)}, u32[]{:S(2)}) collective-permute-start(f32[128,256]{1,0:T(8,128)S(1)} %slice.58), channel_id=1, source_target_pairs={{8,0},{16,8},{24,16},{0,24},{40,32},{48,40},{56,48},{32,56},{72,64... | collective-permute-start | bytes 393224 | tf_op jit(solution)/shard_map/ppermute | solution.py:239
  153.2 0.1 pad_add_fusion.place_ref
  153.3 0.1 pad_add_fusion.1.place_ref
  153.4 3.4 %copy-done = f32[1024,2048]{1,0:T(8,128)S(1)} copy-done((f32[1024,2048]{1,0:T(8,128)S(1)}, f32[1024,2048]{1,0:T(8,128)}, u32[]{:S(2)}) %copy-start) | copy-done | bytes 8388632
  156.8 1.2 split.1
  158.0 2.0 %copy-done.1 = bf16[1024,2048]{1,0:T(8,128)(2,1)} copy-done((bf16[1024,2048]{1,0:T(8,128)(2,1)}, bf16[1024,2048]{1,0:T(8,128)(2,1)S(1)}, u32[]{:S(2)}) %copy-start.1) | copy-done | bytes 4194328
  160.0 2.0 %copy-done.2 = bf16[1024,2048]{1,0:T(8,128)(2,1)} copy-done((bf16[1024,2048]{1,0:T(8,128)(2,1)}, bf16[1024,2048]{1,0:T(8,128)(2,1)S(1)}, u32[]{:S(2)}) %copy-start.2) | copy-done | bytes 4194328
  162.0 4.5 %update0.1 = (f32[1024,256]{1,0:T(8,128)S(1)}, f32[1024,256]{1,0:T(8,128)S(1)}) custom-call(s32[2]{0:T(128)S(1)} %pad_add_fusion.1.place_ref, bf16[1024,2048]{1,0:T(8,128)(2,1)} %copy-done.1, bf16[1024,2048]{1,0:T(8,128)(2,1)} %copy-done.2, f32[1024,256]{1,0:T(8,128)S(1)} %copy-done.3, f32[256,256]{1,0:T(8,128)S(1)} %add_select_fusion.2.rest_0_, ...), custom_call_target="tpu_custom_call" | custom-call | tf_op jit(solution)/shard_map/update0/pallas_call | solution.py:174
  166.6 5.5 %update1.1 = (f32[1024,256]{1,0:T(8,128)}, f32[2048,256]{1,0:T(8,128)}) custom-call(s32[2]{0:T(128)S(1)} %pad_add_fusion.place_ref, bf16[1024,2048]{1,0:T(8,128)(2,1)} %copy-done.1, bf16[1024,2048]{1,0:T(8,128)(2,1)} %copy-done.2, f32[1024,256]{1,0:T(8,128)S(1)} %get-tuple-element.8.target_ref, f32[256,256]{1,0:T(8,128)S(1)} %add_select_fusion.rest_0_, ...), custom_call_target="tpu_custom_call" | custom-call | tf_op jit(solution)/shard_map/update1/pallas_call | solution.py:174
  (25 shorter events, 0.3 us)
Async XLA Ops:
  7.2 56.3 %all-gather.2.cloned.1.call-start = ((), (), s32[]{:S(2)}) async-start(), calls=%async_computation | async-start | bytes 9437184 | tf_op jit(solution)/shard_map/all_gather | solution.py:247
  8.9 1.4 collective-permute-start.1
  9.6 1.4 collective-permute-start
  10.3 0.7 collective-permute-start.2
  11.0 52.5 %copy-start.3 = (f32[1024,256]{1,0:T(8,128)S(1)}, f32[1024,256]{1,0:T(8,128)}, u32[]{:S(2)}) copy-start(f32[1024,256]{1,0:T(8,128)} %rhs.3) | copy-start | bytes 3145732
  11.2 0.8 collective-permute-start.3
  63.5 4.5 %collective-permute-start.4 = (f32[1024,256]{1,0:T(8,128)S(1)}, f32[1024,256]{1,0:T(8,128)}, u32[]{:S(2)}, u32[]{:S(2)}) collective-permute-start(f32[1024,256]{1,0:T(8,128)S(1)} %solve0.1), channel_id=1, source_target_pairs={{0,8},{1,9},{2,10},{3,11},{4,12},{5,13},{6,14},{7,15}} | collective-permute-start | bytes 3145736 | tf_op jit(solution)/shard_map/ppermute | solution.py:262
  66.0 4.2 %collective-permute-start.6 = (f32[256,256]{1,0:T(8,128)}, f32[256,256]{1,0:T(8,128)S(1)}, u32[]{:S(2)}, u32[]{:S(2)}) collective-permute-start(f32[256,256]{1,0:T(8,128)} %get-tuple-element.13), channel_id=1, source_target_pairs={{0,24},{1,25},{2,26},{3,27},{4,28},{5,29},{6,30},{7,31}} | collective-permute-start | bytes 786440 | tf_op jit(solution)/shard_map/ppermute | solution.py:220
  66.7 3.5 %collective-permute-start.5 = (f32[256,256]{1,0:T(8,128)}, f32[256,256]{1,0:T(8,128)}, u32[]{:S(2)}, u32[]{:S(2)}) collective-permute-start(f32[256,256]{1,0:T(8,128)} %get-tuple-element.14), channel_id=1, source_target_pairs={{0,16},{1,17},{2,18},{3,19},{4,20},{5,21},{6,22},{7,23}} | collective-permute-start | bytes 786440 | tf_op jit(solution)/shard_map/ppermute | solution.py:220
  68.2 4.6 %collective-permute-start.16 = (f32[256,256]{1,0:T(8,128)S(1)}, f32[256,256]{1,0:T(8,128)S(1)}, u32[]{:S(2)}, u32[]{:S(2)}) collective-permute-start(f32[256,256]{1,0:T(8,128)S(1)} %get-tuple-element.10), channel_id=1, source_target_pairs={{8,24},{9,25},{10,26},{11,27},{12,28},{13,29},{14,30},{15,31}} | collective-permute-start | bytes 786440 | tf_op jit(solution)/shard_map/ppermute | solution.py:220
  68.9 3.9 %collective-permute-start.17 = (f32[256,256]{1,0:T(8,128)S(1)}, f32[256,256]{1,0:T(8,128)S(1)}, u32[]{:S(2)}, u32[]{:S(2)}) collective-permute-start(f32[256,256]{1,0:T(8,128)S(1)} %get-tuple-element.11), channel_id=1, source_target_pairs={{8,0},{9,1},{10,2},{11,3},{12,4},{13,5},{14,6},{15,7}} | collective-permute-start | bytes 786440 | tf_op jit(solution)/shard_map/ppermute | solution.py:220
  69.5 3.2 %collective-permute-start.15 = (f32[256,256]{1,0:T(8,128)S(1)}, f32[256,256]{1,0:T(8,128)S(1)}, u32[]{:S(2)}, u32[]{:S(2)}) collective-permute-start(f32[256,256]{1,0:T(8,128)S(1)} %get-tuple-element.12), channel_id=1, source_target_pairs={{8,16},{9,17},{10,18},{11,19},{12,20},{13,21},{14,22},{15,23}} | collective-permute-start | bytes 786440 | tf_op jit(solution)/shard_map/ppermute | solution.py:220
  71.4 2.9 %collective-permute-start.8 = (f32[256,256]{1,0:T(8,128)S(1)}, f32[256,256]{1,0:T(8,128)S(1)}, u32[]{:S(2)}, u32[]{:S(2)}) collective-permute-start(f32[256,256]{1,0:T(8,128)S(1)} %fusion), channel_id=1, source_target_pairs={{0,160},{8,168},{16,176},{24,184},{1,161},{9,169},{17,177},{25,185... | collective-permute-start | bytes 786440 | tf_op jit(solution)/shard_map/ppermute | solution.py:229
  72.0 2.2 %collective-permute-start.7 = (f32[256,256]{1,0:T(8,128)S(1)}, f32[256,256]{1,0:T(8,128)S(1)}, u32[]{:S(2)}, u32[]{:S(2)}) collective-permute-start(f32[256,256]{1,0:T(8,128)S(1)} %fusion), channel_id=1, source_target_pairs={{0,96},{8,104},{16,112},{24,120},{1,97},{9,105},{17,113},{25,121},... | collective-permute-start | bytes 786440 | tf_op jit(solution)/shard_map/ppermute | solution.py:228
  72.8 3.5 %collective-permute-start.19 = (f32[256,256]{1,0:T(8,128)S(1)}, f32[256,256]{1,0:T(8,128)S(1)}, u32[]{:S(2)}, u32[]{:S(2)}) collective-permute-start(f32[256,256]{1,0:T(8,128)S(1)} %slice_select_fusion), channel_id=1, source_target_pairs={{0,160},{8,168},{16,176},{24,184},{1,161},{9,169},{17,177},{25,185... | collective-permute-start | bytes 786440 | tf_op jit(solution)/shard_map/ppermute | solution.py:229
  73.5 2.8 %collective-permute-start.18 = (f32[256,256]{1,0:T(8,128)S(1)}, f32[256,256]{1,0:T(8,128)S(1)}, u32[]{:S(2)}, u32[]{:S(2)}) collective-permute-start(f32[256,256]{1,0:T(8,128)S(1)} %slice_select_fusion), channel_id=1, source_target_pairs={{0,96},{8,104},{16,112},{24,120},{1,97},{9,105},{17,113},{25,121},... | collective-permute-start | bytes 786440 | tf_op jit(solution)/shard_map/ppermute | solution.py:228
  74.3 4.1 %collective-permute-start.10 = (f32[256,256]{1,0:T(8,128)S(1)}, f32[256,256]{1,0:T(8,128)S(1)}, u32[]{:S(2)}, u32[]{:S(2)}) collective-permute-start(f32[256,256]{1,0:T(8,128)S(1)} %add_select_fusion.3), channel_id=1, source_target_pairs={{0,224},{8,232},{16,240},{24,248},{96,64},{104,72},{112,80},{120,8... | collective-permute-start | bytes 786440 | tf_op jit(solution)/shard_map/ppermute | solution.py:232
  75.0 60.1 %collective-permute-start.9 = (f32[256,256]{1,0:T(8,128)S(1)}, f32[256,256]{1,0:T(8,128)S(1)}, u32[]{:S(2)}, u32[]{:S(2)}) collective-permute-start(f32[256,256]{1,0:T(8,128)S(1)} %add_select_fusion.3), channel_id=1, source_target_pairs={{0,32},{8,40},{16,48},{24,56},{96,128},{104,136},{112,144},{120,15... | collective-permute-start | bytes 786440 | tf_op jit(solution)/shard_map/ppermute | solution.py:231
  76.4 62.1 %collective-permute-start.21 = (f32[256,256]{1,0:T(8,128)S(1)}, f32[256,256]{1,0:T(8,128)S(1)}, u32[]{:S(2)}, u32[]{:S(2)}) collective-permute-start(f32[256,256]{1,0:T(8,128)S(1)} %add_select_fusion.1), channel_id=1, source_target_pairs={{0,224},{8,232},{16,240},{24,248},{96,64},{104,72},{112,80},{120,8... | collective-permute-start | bytes 786440 | tf_op jit(solution)/shard_map/ppermute | solution.py:232
  77.1 61.7 %collective-permute-start.20 = (f32[256,256]{1,0:T(8,128)S(1)}, f32[256,256]{1,0:T(8,128)S(1)}, u32[]{:S(2)}, u32[]{:S(2)}) collective-permute-start(f32[256,256]{1,0:T(8,128)S(1)} %add_select_fusion.1), channel_id=1, source_target_pairs={{0,32},{8,40},{16,48},{24,56},{96,128},{104,136},{112,144},{120,15... | collective-permute-start | bytes 786440 | tf_op jit(solution)/shard_map/ppermute | solution.py:231
  135.1 9.5 %collective-permute-start.13 = (f32[256,256]{1,0:T(8,128)S(1)}, f32[256,256]{1,0:T(8,128)S(1)}, u32[]{:S(2)}, u32[]{:S(2)}) collective-permute-start(f32[256,256]{1,0:T(8,128)S(1)} %add_select_fusion.2.rest_0_), channel_id=1, source_target_pairs={{0,8},{8,16},{16,24},{24,0},{32,40},{40,48},{48,56},{56,32},{64,72... | collective-permute-start | bytes 786440 | tf_op jit(solution)/shard_map/ppermute | solution.py:238
  135.2 9.5 %collective-permute-start.11 = (f32[256,256]{1,0:T(8,128)S(1)}, f32[256,256]{1,0:T(8,128)S(1)}, u32[]{:S(2)}, u32[]{:S(2)}) collective-permute-start(f32[256,256]{1,0:T(8,128)S(1)} %add_select_fusion.2.rest_0_), channel_id=1, source_target_pairs={{8,0},{16,8},{24,16},{0,24},{40,32},{48,40},{56,48},{32,56},{72,64... | collective-permute-start | bytes 786440 | tf_op jit(solution)/shard_map/ppermute | solution.py:237
  138.8 11.0 %collective-permute-start.24 = (f32[256,256]{1,0:T(8,128)S(1)}, f32[256,256]{1,0:T(8,128)S(1)}, u32[]{:S(2)}, u32[]{:S(2)}) collective-permute-start(f32[256,256]{1,0:T(8,128)S(1)} %add_select_fusion.rest_0_), channel_id=1, source_target_pairs={{0,8},{8,16},{16,24},{24,0},{32,40},{40,48},{48,56},{56,32},{64,72... | collective-permute-start | bytes 786440 | tf_op jit(solution)/shard_map/ppermute | solution.py:238
  139.0 10.9 %collective-permute-start.22 = (f32[256,256]{1,0:T(8,128)S(1)}, f32[256,256]{1,0:T(8,128)S(1)}, u32[]{:S(2)}, u32[]{:S(2)}) collective-permute-start(f32[256,256]{1,0:T(8,128)S(1)} %add_select_fusion.rest_0_), channel_id=1, source_target_pairs={{8,0},{16,8},{24,16},{0,24},{40,32},{48,40},{56,48},{32,56},{72,64... | collective-permute-start | bytes 786440 | tf_op jit(solution)/shard_map/ppermute | solution.py:237
  144.6 17.4 %collective-permute-start.14 = (f32[128,256]{1,0:T(8,128)S(1)}, f32[128,256]{1,0:T(8,128)S(1)}, u32[]{:S(2)}, u32[]{:S(2)}) collective-permute-start(f32[128,256]{1,0:T(8,128)S(1)} %slice.53), channel_id=1, source_target_pairs={{0,8},{8,16},{16,24},{24,0},{32,40},{40,48},{48,56},{56,32},{64,72... | collective-permute-start | bytes 393224 | tf_op jit(solution)/shard_map/ppermute | solution.py:240
  145.4 16.6 %collective-permute-start.12 = (f32[128,256]{1,0:T(8,128)}, f32[128,256]{1,0:T(8,128)S(1)}, u32[]{:S(2)}, u32[]{:S(2)}) collective-permute-start(f32[128,256]{1,0:T(8,128)} %slice.52), channel_id=1, source_target_pairs={{8,0},{16,8},{24,16},{0,24},{40,32},{48,40},{56,48},{32,56},{72,64... | collective-permute-start | bytes 393224 | tf_op jit(solution)/shard_map/ppermute | solution.py:239
  149.8 16.7 %collective-permute-start.25 = (f32[128,256]{1,0:T(8,128)S(1)}, f32[128,256]{1,0:T(8,128)S(1)}, u32[]{:S(2)}, u32[]{:S(2)}) collective-permute-start(f32[128,256]{1,0:T(8,128)S(1)} %slice.59), channel_id=1, source_target_pairs={{0,8},{8,16},{16,24},{24,0},{32,40},{40,48},{48,56},{56,32},{64,72... | collective-permute-start | bytes 393224 | tf_op jit(solution)/shard_map/ppermute | solution.py:240
  149.9 16.6 %collective-permute-start.23 = (f32[128,256]{1,0:T(8,128)S(1)}, f32[128,256]{1,0:T(8,128)S(1)}, u32[]{:S(2)}, u32[]{:S(2)}) collective-permute-start(f32[128,256]{1,0:T(8,128)S(1)} %slice.58), channel_id=1, source_target_pairs={{8,0},{16,8},{24,16},{0,24},{40,32},{48,40},{56,48},{32,56},{72,64... | collective-permute-start | bytes 393224 | tf_op jit(solution)/shard_map/ppermute | solution.py:239
  153.4 3.4 %copy-start = (f32[1024,2048]{1,0:T(8,128)S(1)}, f32[1024,2048]{1,0:T(8,128)}, u32[]{:S(2)}) copy-start(f32[1024,2048]{1,0:T(8,128)} %all-gather.2.cloned.1.call-done.value_ref.gathered) | copy-start | bytes 25165828
  158.0 2.0 %copy-start.1 = (bf16[1024,2048]{1,0:T(8,128)(2,1)}, bf16[1024,2048]{1,0:T(8,128)(2,1)S(1)}, u32[]{:S(2)}) copy-start(bf16[1024,2048]{1,0:T(8,128)(2,1)S(1)} %get-tuple-element.6.high_ref) | copy-start | bytes 12582916
  160.0 2.0 %copy-start.2 = (bf16[1024,2048]{1,0:T(8,128)(2,1)}, bf16[1024,2048]{1,0:T(8,128)(2,1)S(1)}, u32[]{:S(2)}) copy-start(bf16[1024,2048]{1,0:T(8,128)(2,1)S(1)} %get-tuple-element.7.low_ref) | copy-start | bytes 12582916
Sparse Core Ops, SparseCore 0:
  9.8 53.6 all-gather.1

commit v2 on v0

v2 whole, which is shorter than its diff:
```python
import functools

import jax
import jax.numpy as jnp
from jax import lax
from jax.experimental import pallas as pl
from jax.experimental.pallas import tpu as pltpu
from jax.sharding import PartitionSpec as P

NB = 1024
HALF = NB // 2
Q = 256
PARTS = 4
XS = 4
YS = 4
ZS = 8
ROWS = XS * ZS
COLS = 2 * YS
F32 = jnp.float32
BF16 = jnp.bfloat16
BOTH = ("row", "col")


def halves(value):
    high = value.astype(BF16)
    return high, (value - high.astype(F32)).astype(BF16)


def product(left, right):
    dot = functools.partial(jnp.dot, preferred_element_type=F32)
    return dot(left[0], right[0]) + (dot(left[0], right[1]) + dot(left[1], right[0]))


def call(kernel, name, shapes, scratch, operands, in_specs=None, out_specs=None, vmem=24, **options):
    operands = [pltpu.with_memory_space_constraint(x, pltpu.HBM) if x.ndim == 3 else x for x in operands]
    return pl.pallas_call(
        kernel,
        out_shape=[(pltpu.HBM if len(shape) == 3 else jax.ShapeDtypeStruct)(shape, dtype) for shape, dtype in shapes],
        in_specs=[pl.BlockSpec(memory_space=pltpu.SMEM)]
        + (in_specs or [pl.BlockSpec(memory_space=pl.ANY)] * (len(operands) - 1)),
        out_specs=out_specs or [pl.BlockSpec(memory_space=pltpu.VMEM)] * len(shapes),
        scratch_shapes=scratch,
        compiler_params=pltpu.CompilerParams(vmem_limit_bytes=vmem << 20),
        cost_estimate=pl.CostEstimate(flops=2 * NB * NB * Q, bytes_accessed=8 << 20, transcendentals=0),
        name=name,
        **options,
    )(*operands)


ROW, PLACE_Y, CORE, TURN = range(4)


def payload_kernel(place, panel_ref, top_ref, bottom_ref):
    top_ref[...] = panel_ref[pl.ds(0, HALF), :]
    bottom_ref[...] = panel_ref[pl.ds(HALF, HALF), :]
    col = 2 * place[PLACE_Y] + place[CORE]
    number = col & (PARTS - 1)

    @pl.when(((place[ROW] == 0) & (col < PARTS)) | ((place[ROW] == 1) & (col >= PARTS)))
    def _():
        rows = lax.broadcasted_iota(jnp.int32, (Q, Q), 0)
        cols = lax.broadcasted_iota(jnp.int32, (Q, Q), 1)
        block = panel_ref[pl.ds(pl.multiple_of(number * Q, Q), Q), :]
        inverse = jnp.where(rows == cols, 1.0 / jnp.where(rows == cols, block, 1.0), 0.0)
        level = 0
        while (1 << level) < Q:
            pair = (rows >> (level + 1)) == (cols >> (level + 1))
            below = pair & (((rows >> level) & 1) == 1) & (((cols >> level) & 1) == 0)
            parts = halves(inverse)
            inner = product(halves(jnp.where(below, block, 0.0)), parts)
            inverse = inverse - product(parts, halves(inner))
            level += 1
        for i in range(PARTS):

            @pl.when(number == i)
            def _():
                half = (top_ref, bottom_ref)[i // 2]
                half[pl.ds((i % 2) * Q, Q), :] = inverse


def payload(place, panel):
    vmem = [pl.BlockSpec(memory_space=pltpu.VMEM)]
    return call(payload_kernel, "payload", [((HALF, Q), F32)] * 2, [], (place, panel), in_specs=vmem)


CHUNK = tuple(
    (step, same, start, length)
    for step, start, length in ((0, 0, HALF), (1, 0, HALF), (3, 0, HALF), (2, 0, Q), (2, Q, Q))
    for same in (True, False)
)


def pairs(step, origin, has):
    return [
        (r * COLS + 2 * y + k, r * COLS + 2 * ((y + step) % YS) + k)
        for r in range(ROWS)
        for y in range(YS)
        for k in (0, 1)
        if has(r, (y + origin) % YS)
    ]


def other_core(value):
    return lax.ppermute(value, "col", [(c, c ^ 1) for c in range(COLS)])


def near_chips(chunk, has):
    behind = lax.ppermute(chunk, BOTH, pairs(1, 0, has))
    return lax.ppermute(chunk, BOTH, pairs(-1, 0, has)), behind


def far_chip(ahead, behind, has):
    return lax.ppermute(ahead[:Q], BOTH, pairs(-1, 1, has)), lax.ppermute(behind[Q:], BOTH, pairs(1, -1, has))


def both_cores(values):
    return [x for value in values for x in (value, other_core(value))]


def collect(place, arrays, blocks, buffer, first, sem):
    for (step, same, start, length), array in zip(CHUNK, arrays):
        core = place[CORE] if same else 1 - place[CORE]
        block = 2 * ((place[PLACE_Y] + step) & (YS - 1)) + core

        @pl.when(block < blocks)
        def _():
            pltpu.make_async_copy(array, buffer.at[block, pl.ds(first + start, length)], sem).start()


def assemble_kernel(place, *rest):
    arrays, (out, sem) = rest[: len(CHUNK)], rest[len(CHUNK) :]
    collect(place, arrays, COLS, out, 0, sem)
    pltpu.make_async_copy(out, out, sem).wait()


def assemble(place, arrays):
    in_hbm = [pl.BlockSpec(memory_space=pltpu.HBM)]
    scratch = [pltpu.SemaphoreType.DMA]
    shapes = [((COLS, HALF, Q), F32)]
    return call(assemble_kernel, "assemble", shapes, scratch, (place, *arrays), out_specs=in_hbm)[0]


def blocks_copies(top, bottom, base, buffer, sems):
    copies = [
        pltpu.make_async_copy(half.at[pl.ds(base, PARTS)], buffer.at[:, pl.ds(i * HALF, HALF)], sems.at[i])
        for i, half in enumerate((top, bottom))
    ]
    for copy in copies:
        copy.start()
    return copies


def eliminate(triangle, targets, store):
    for i in range(PARTS):
        value = product(halves(triangle[i, pl.ds(i * Q, Q), :]), halves(targets[i]))
        store(i, value)
        parts = halves(value)
        for k in range(i + 1, PARTS):
            targets[k] = targets[k] - product(halves(triangle[i, pl.ds(k * Q, Q), :]), parts)


def solve_kernel(place, rhs, top, *rest):
    bottoms, rest = rest[: len(CHUNK)], rest[len(CHUNK) :]
    one, two, three, others, triangle, rhs_buf, sem, top_sem, rhs_sem = rest

    @pl.when(place[ROW] == 0)
    def _():
        lower = triangle.at[:, pl.ds(HALF, HALF)]
        collect(place, bottoms, PARTS, triangle, HALF, sem)
        copies = [
            pltpu.make_async_copy(rhs, rhs_buf, rhs_sem),
            pltpu.make_async_copy(top.at[pl.ds(0, PARTS)], triangle.at[:, pl.ds(0, HALF)], top_sem),
        ]
        for copy in copies:
            copy.start()
        for copy in copies:
            copy.wait()
        pltpu.make_async_copy(lower, lower, sem).wait()

        def store(i, value):
            if i == 1:
                one[...] = value
            else:
                others[pl.ds(max(i - 1, 0) * Q, Q), :] = value
            if i >= 2:
                (two, three)[i - 2][...] = value

        eliminate(triangle, [rhs_buf[pl.ds(i * Q, Q), :] for i in range(PARTS)], store)


def solve(place, rhs, top, bottoms):
    scratch = [
        pltpu.VMEM((PARTS, NB, Q), F32),
        pltpu.VMEM((NB, Q), F32),
        pltpu.SemaphoreType.DMA,
        pltpu.SemaphoreType.DMA,
        pltpu.SemaphoreType.DMA,
    ]
    shapes = [((Q, Q), F32)] * 3 + [((3 * Q, Q), F32)]
    return call(solve_kernel, "solve", shapes, scratch, (place, rhs, top, *bottoms))


def second_kernel(place, rhs, top, bottom, one, others, *rest):
    out, (triangle, left, rhs_buf, first_buf, sem, left_sem, rhs_sem, first_sem) = rest[:PARTS], rest[PARTS:]

    @pl.when(place[ROW] == 1)
    def _():
        copies = [pltpu.make_async_copy(rhs, rhs_buf, rhs_sem)]
        for i, (array, start, at, length) in enumerate(((others, 0, 0, Q), (one, 0, Q, Q), (others, Q, 2 * Q, 2 * Q))):
            source = array.at[pl.ds(start, length)]
            copies.append(pltpu.make_async_copy(source, first_buf.at[pl.ds(at, length)], first_sem.at[i]))
        for copy in copies:
            copy.start()
        copies += blocks_copies(top, bottom, 0, left, left_sem)
        later = blocks_copies(top, bottom, PARTS, triangle, sem)
        for copy in copies:
            copy.wait()
        solved = [halves(first_buf[pl.ds(j * Q, Q), :]) for j in range(PARTS)]
        targets = []
        for i in range(PARTS):
            rows = pl.ds(i * Q, Q)
            value = rhs_buf[rows, :]
            for j in range(PARTS):
                value = value - product(halves(left[j, rows, :]), solved[j])
            targets.append(value)
        for copy in later:
            copy.wait()

        def store(i, value):
            out[i][...] = value

        eliminate(triangle, targets, store)


def second(place, rhs, top, bottom, one, others):
    scratch = [
        pltpu.VMEM((PARTS, NB, Q), F32),
        pltpu.VMEM((PARTS, NB, Q), F32),
        pltpu.VMEM((NB, Q), F32),
        pltpu.VMEM((NB, Q), F32),
        pltpu.SemaphoreType.DMA((2,)),
        pltpu.SemaphoreType.DMA((2,)),
        pltpu.SemaphoreType.DMA,
        pltpu.SemaphoreType.DMA((3,)),
    ]
    return call(second_kernel, "second", [((Q, Q), F32)] * PARTS, scratch, (place, rhs, top, bottom, one, others))


PIECES = ((0, Q), (Q, Q), (2 * Q, Q // 2), (2 * Q + Q // 2, Q // 2), (3 * Q, Q))


def update_kernel(last, place, target, top, bottom, *rest):
    pieces, rest = rest[: len(PIECES)], rest[len(PIECES) + int(last) :]
    out, whole, blocks, target_buf, solved_buf, panel_high, panel_low, sem, target_sem, solved_sem, whole_sem = rest
    base = PARTS * int(last)
    for piece, (at, length) in zip(pieces, PIECES):
        start = pl.multiple_of((at + place[TURN] * Q) & (NB - 1), Q // 2)
        pltpu.make_async_copy(piece, solved_buf.at[pl.ds(start, length)], solved_sem).start()
    waits = blocks_copies(top, bottom, base, blocks, sem)
    copy = pltpu.make_async_copy(target, target_buf, target_sem)
    copy.start()
    pltpu.make_async_copy(solved_buf, solved_buf, solved_sem).wait()
    keep = pltpu.make_async_copy(solved_buf, whole.at[pl.ds(int(last) * NB, NB)], whole_sem)
    keep.start()
    solved = halves(solved_buf[...])
    for wait in waits:
        wait.wait()
    for j in range(PARTS):
        high, low = halves(blocks[j])
        panel_high[:, j * Q : (j + 1) * Q] = high
        panel_low[:, j * Q : (j + 1) * Q] = low
    copy.wait()
    for i in range(PARTS):
        rows = pl.ds(i * Q, Q)
        result = target_buf[rows, :] - product((panel_high[rows, :], panel_low[rows, :]), solved)
        out[rows, :] = jnp.where(place[ROW] >= 2, result, 0.0) if last else result
    keep.wait()


def update(last, place, target, top, bottom, pieces, *before):
    scratch = [
        pltpu.VMEM((PARTS, NB, Q), F32),
        pltpu.VMEM((NB, Q), F32),
        pltpu.VMEM((NB, Q), F32),
        pltpu.VMEM((NB, NB), BF16),
        pltpu.VMEM((NB, NB), BF16),
        pltpu.SemaphoreType.DMA((2,)),
        pltpu.SemaphoreType.DMA,
        pltpu.SemaphoreType.DMA,
        pltpu.SemaphoreType.DMA,
    ]
    operands = (place, target, top, bottom, *pieces, *before)
    return call(
        functools.partial(update_kernel, last),
        "update%d" % int(last),
        [((NB, Q), F32), ((2 * NB, Q), F32)],
        scratch,
        operands,
        out_specs=[pl.BlockSpec(memory_space=pltpu.VMEM), pl.BlockSpec(memory_space=pl.ANY)],
        input_output_aliases={len(operands) - 1: 1} if before else {},
    )


def along_z(moves):
    return [(a * XS + x, b * XS + x) for a, b in moves for x in range(XS)]


TO_NEXT = [(r, r // XS * XS + (r + 1) % XS) for r in range(ROWS)]
TO_LAST = [(b, a) for a, b in TO_NEXT]


def scatter(pieces, root):
    got = [lax.ppermute(pieces[i], "row", [(root, (root + i) % XS)]) for i in (2, 1, 3)]
    return got[1], got[0], got[2]


def far_z(mine, z):
    near = lax.ppermute(mine, "row", along_z([(0, 3)]))
    far = lax.ppermute(mine, "row", along_z([(0, 5)]))
    return jnp.where(z == 0, mine, near + far)


def near_z(mine, z):
    up = lax.ppermute(mine, "row", along_z([(0, 1), (3, 4), (5, 6)]))
    down = lax.ppermute(mine, "row", along_z([(0, 7), (3, 2)]))
    return jnp.where((z == 0) | (z == 3) | (z == 5), mine, up + down)


def over_x(mine):
    after = lax.ppermute(mine, "row", TO_LAST)
    before = lax.ppermute(mine, "row", TO_NEXT)
    over_top = lax.ppermute(after[: Q // 2], "row", TO_LAST)
    over_rest = lax.ppermute(before[Q // 2 :], "row", TO_NEXT)
    return mine, after, over_top, over_rest, before


def body(panel, rhs):
    row = lax.axis_index("row")
    col = lax.axis_index("col")
    z = row // XS

    def place(root):
        return jnp.stack([row, col // 2, col % 2, (row - root) % XS])

    def after(value, *others):
        return lax.optimization_barrier((value, *others))[0]

    top, bottom = payload(place(0), panel)
    near = near_chips(top, lambda r, y: r > 0 or y == 0)
    top = assemble(place(0), both_cores((top, *near, *far_chip(*near, lambda r, y: r > 0 or y == 0))))
    near = near_chips(bottom, lambda r, y: r > 0 or y <= 1)
    bottoms = both_cores((bottom, *near, *far_chip(*near, lambda r, y: r > 0 or y <= 1)))
    one, two, three, others = solve(place(0), rhs, top, bottoms)
    others_ahead = lax.ppermute(others, "row", [(0, 1)])
    one_ahead, two_ahead, three_ahead = scatter((None, one, two, three), 0)
    bottom = assemble(place(0), bottoms)
    mine_one = jnp.where(row == 0, others[:Q], one_ahead + two_ahead + three_ahead)
    mine_one = far_z(mine_one, z)

    pieces = second(place(0), rhs, top, bottom, one_ahead, others_ahead)
    got = scatter(pieces, 1)
    mine_one = near_z(after(mine_one, *pieces), z)
    mine_two = jnp.where(row == 1, pieces[0], got[0] + got[1] + got[2])
    pieces_one = over_x(after(mine_one, mine_two))
    mine_two = far_z(mine_two, z)
    updated, whole = update(False, place(0), rhs, top, bottom, pieces_one)
    mine_two, updated, whole = lax.optimization_barrier((mine_two, updated, whole))
    pieces_two = over_x(near_z(mine_two, z))
    return tuple(update(True, place(1), updated, top, bottom, pieces_two, whole))


def solution(mesh):
    placed = (P("row", "col"), P("row", "col"))
    return jax.shard_map(
        body,
        mesh=mesh,
        in_specs=placed,
        out_specs=(P("row", "col"), P(None, "col")),
        check_vma=False,
    )
```

time: 529 us -> 169 us (0.32)
  waiting for transfers between devices: 252 us -> 70.2 us
  other arithmetic: 170 us -> 4.45 us
  starting transfers between devices: 0.3 us -> 64.1 us
  matrix products: 43.7 us -> 0 us
  local copies, waits for them, and re-layouts: 46 us -> 6.29 us
  Pallas kernels: 0 us -> 20.9 us
  between operations: 14.1 us -> 1.3 us
    psum x2 -> x0, waiting for transfers between devices: 194 us -> none  [spread(): return lax.psum(jnp.where(mine, shard, jnp.zeros_like(shard)), axis)]
    another operation x4 -> x2, other arithmetic: 165 us -> 0.15 us  [place(): return jnp.stack([row, col // 2, col % 2, (row - root) % XS])]
    ppermute x0 -> x41, waiting for transfers between devices: none -> 70.2 us  [the longest x6 31 us: scatter(): lax.ppermute(pieces[i], 'row', [(root, (root + i) % XS)])]
    ppermute x0 -> x41, starting transfers between devices: none -> 64.1 us  [the longest x2 8.47 us: far_chip(): lax.ppermute(ahead[:Q], BOTH, pairs(-1, 1, has))]
    all_gather x1 -> x0, waiting for transfers between devices: 57.1 us -> none  [body(): gathered = lax.all_gather(panel, 'col', axis=1, tiled=True)]
    another operation x51 -> x0, local copies, waits for them, and re-layouts: 46 us -> none  [tri_solve(): return jax.scipy.linalg.solve_triangular(matrix, targets, lower=True)]
    another operation x30 -> x0, matrix products: 24.3 us -> none  [tri_solve(): return jax.scipy.linalg.solve_triangular(matrix, targets, lower=True)]
    pallas_call x0 -> x7, Pallas kernels: none -> 20.9 us  [call(): pl.pallas_call(kernel, out_shape=[(pltpu.HBM if len(shape) == 3 else jax....]
  transfers between devices with their start and end apart: 3 -> 41, of which waited for: 3 -> 19; matrix products, arithmetic and copies ran while one was open for 19% -> 3% of each run, Pallas kernels for 0% -> 3%
where the time goes in v2:
time: 169 us; the launch traced here: 167 us
  waiting for transfers between devices  70.2 us (42%)
  starting transfers between devices  64.1 us (38%)
  Pallas kernels  20.9 us (12%)
  local copies, waits for them, and re-layouts  6.29 us (4%)
  other arithmetic  4.45 us (3%)
    ppermute x6, waiting for transfers between devices, scatter(): lax.ppermute(pieces[i], 'row', [(root, (root + i) % XS)])  31 us
    pallas_call x7, Pallas kernels, call(): pl.pallas_call(kernel, out_shape=[(pltpu.HBM if len(shape) == 3 else jax....  20.9 us
    ppermute x2, starting transfers between devices, far_chip(): lax.ppermute(ahead[:Q], BOTH, pairs(-1, 1, has))  8.47 us
    ppermute x2, starting transfers between devices, near_chips(): return (lax.ppermute(chunk, BOTH, pairs(-1, 0, has)), behind)  8.35 us
    ppermute x2, waiting for transfers between devices, near_chips(): behind = lax.ppermute(chunk, BOTH, pairs(1, 0, has))  7.78 us
    ppermute x2, waiting for transfers between devices, over_x(): before = lax.ppermute(mine, 'row', TO_NEXT)  7.52 us
    ppermute x6, starting transfers between devices, scatter(): lax.ppermute(pieces[i], 'row', [(root, (root + i) % XS)])  6.63 us
    ppermute x2, waiting for transfers between devices, over_x(): over_top = lax.ppermute(after[:Q // 2], 'row', TO_LAST)  6.3 us
  transfers between devices with their start and end apart: 41, of which 19 were waited for; matrix products, arithmetic and copies ran while one was open for 3% of the time, Pallas kernels for 3%

profile of v2, /device:TPU:6, one launch (start us, length us, event | category | flops | bytes accessed | tf_op | source)
XLA Modules:
  0.0 167.2 jit_solution(2998680580764830064)
XLA Ops:
  0.7 1.2 copy-done.11
  2.0 0.6 payload.1
  2.6 3.5 %collective-permute-start.3 = (f32[512,256]{1,0:T(8,128)S(1)}, f32[512,256]{1,0:T(8,128)S(1)}, u32[]{:S(2)}, u32[]{:S(2)}) collective-permute-start(f32[512,256]{1,0:T(8,128)S(1)} %get-tuple-element.19.rest_0_), channel_id=1, source_target_pairs={{0,2},{1,3},{8,10},{9,11},{10,12},{11,13},{12,14},{13,15},{14,8},{... | collective-permute-start | bytes 1572872 | tf_op jit(solution)/shard_map/ppermute | solution.py:108
  6.1 3.6 %collective-permute-start.1 = (f32[512,256]{1,0:T(8,128)S(1)}, f32[512,256]{1,0:T(8,128)S(1)}, u32[]{:S(2)}, u32[]{:S(2)}) collective-permute-start(f32[512,256]{1,0:T(8,128)S(1)} %get-tuple-element.19.rest_0_), channel_id=1, source_target_pairs={{0,6},{1,7},{8,14},{9,15},{10,8},{11,9},{12,10},{13,11},{14,12},{1... | collective-permute-start | bytes 1572872 | tf_op jit(solution)/shard_map/ppermute | solution.py:109
  9.6 2.3 %collective-permute-start.12 = (f32[512,256]{1,0:T(8,128)S(1)}, f32[512,256]{1,0:T(8,128)S(1)}, u32[]{:S(2)}, u32[]{:S(2)}) collective-permute-start(f32[512,256]{1,0:T(8,128)S(1)} %get-tuple-element.20.rest_0_), channel_id=1, source_target_pairs={{0,2},{1,3},{2,4},{3,5},{8,10},{9,11},{10,12},{11,13},{12,14},{13,... | collective-permute-start | bytes 1572872 | tf_op jit(solution)/shard_map/ppermute | solution.py:108
  11.9 4.8 %collective-permute-start.10 = (f32[512,256]{1,0:T(8,128)S(1)}, f32[512,256]{1,0:T(8,128)S(1)}, u32[]{:S(2)}, u32[]{:S(2)}) collective-permute-start(f32[512,256]{1,0:T(8,128)S(1)} %get-tuple-element.20.rest_0_), channel_id=1, source_target_pairs={{0,6},{1,7},{2,0},{3,1},{8,14},{9,15},{10,8},{11,9},{12,10},{13,11... | collective-permute-start | bytes 1572872 | tf_op jit(solution)/shard_map/ppermute | solution.py:109
  16.8 3.7 %collective-permute-done.3.rest_4_ = f32[512,256]{1,0:T(8,128)S(1)} collective-permute-done((f32[512,256]{1,0:T(8,128)S(1)}, f32[512,256]{1,0:T(8,128)S(1)}, u32[]{:S(2)}, u32[]{:S(2)}) %collective-permute-start.3) | collective-permute-done | bytes 524320 | tf_op jit(solution)/shard_map/ppermute | solution.py:108
  20.5 2.3 %collective-permute-start.7 = (f32[256,256]{1,0:T(8,128)S(1)}, f32[256,256]{1,0:T(8,128)S(1)}, u32[]{:S(2)}, u32[]{:S(2)}) collective-permute-start(f32[256,256]{1,0:T(8,128)S(1)} %slice.37), channel_id=1, source_target_pairs={{2,4},{3,5},{8,10},{9,11},{10,12},{11,13},{12,14},{13,15},{14,8},{... | collective-permute-start | bytes 786440 | tf_op jit(solution)/shard_map/ppermute | solution.py:113
  22.8 4.8 %collective-permute-start.5 = (f32[256,256]{1,0:T(8,128)S(1)}, f32[256,256]{1,0:T(8,128)S(1)}, u32[]{:S(2)}, u32[]{:S(2)}) collective-permute-start(f32[256,256]{1,0:T(8,128)S(1)} %slice.36), channel_id=1, source_target_pairs={{6,4},{7,5},{8,14},{9,15},{10,8},{11,9},{12,10},{13,11},{14,12},{1... | collective-permute-start | bytes 786440 | tf_op jit(solution)/shard_map/ppermute | solution.py:113
  27.6 4.1 %collective-permute-done.12.rest_4_ = f32[512,256]{1,0:T(8,128)S(1)} collective-permute-done((f32[512,256]{1,0:T(8,128)S(1)}, f32[512,256]{1,0:T(8,128)S(1)}, u32[]{:S(2)}, u32[]{:S(2)}) %collective-permute-start.12) | collective-permute-done | bytes 524320 | tf_op jit(solution)/shard_map/ppermute | solution.py:108
  31.7 2.3 %collective-permute-done.10.rest_2_ = f32[512,256]{1,0:T(8,128)S(1)} collective-permute-done((f32[512,256]{1,0:T(8,128)S(1)}, f32[512,256]{1,0:T(8,128)S(1)}, u32[]{:S(2)}, u32[]{:S(2)}) %collective-permute-start.10) | collective-permute-done | bytes 524320 | tf_op jit(solution)/shard_map/ppermute | solution.py:109
  34.0 3.5 %collective-permute-start.16 = (f32[256,256]{1,0:T(8,128)S(1)}, f32[256,256]{1,0:T(8,128)S(1)}, u32[]{:S(2)}, u32[]{:S(2)}) collective-permute-start(f32[256,256]{1,0:T(8,128)S(1)} %slice.39), channel_id=1, source_target_pairs={{2,4},{3,5},{4,6},{5,7},{8,10},{9,11},{10,12},{11,13},{12,14},{13,... | collective-permute-start | bytes 786440 | tf_op jit(solution)/shard_map/ppermute | solution.py:113
  37.6 3.7 %collective-permute-start.14 = (f32[256,256]{1,0:T(8,128)S(1)}, f32[256,256]{1,0:T(8,128)S(1)}, u32[]{:S(2)}, u32[]{:S(2)}) collective-permute-start(f32[256,256]{1,0:T(8,128)S(1)} %slice.38), channel_id=1, source_target_pairs={{0,6},{1,7},{6,4},{7,5},{8,14},{9,15},{10,8},{11,9},{12,10},{13,11... | collective-permute-start | bytes 786440 | tf_op jit(solution)/shard_map/ppermute | solution.py:113
  41.4 0.5 collective-permute-start.2
  41.9 1.7 %collective-permute-done.16.rest_8_ = f32[256,256]{1,0:T(8,128)S(1)} collective-permute-done((f32[256,256]{1,0:T(8,128)S(1)}, f32[256,256]{1,0:T(8,128)S(1)}, u32[]{:S(2)}, u32[]{:S(2)}) %collective-permute-start.16) | collective-permute-done | bytes 262176 | tf_op jit(solution)/shard_map/ppermute | solution.py:113
  43.6 2.4 %collective-permute-done.14.rest_6_ = f32[256,256]{1,0:T(8,128)S(1)} collective-permute-done((f32[256,256]{1,0:T(8,128)S(1)}, f32[256,256]{1,0:T(8,128)S(1)}, u32[]{:S(2)}, u32[]{:S(2)}) %collective-permute-start.14) | collective-permute-done | bytes 262176 | tf_op jit(solution)/shard_map/ppermute | solution.py:113
  46.0 0.5 collective-permute-start.13
  46.6 0.4 collective-permute-start.17
  47.1 2.5 %assemble.2.top = f32[8,512,256]{2,1,0:T(8,128)} custom-call(s32[4]{0:T(128)S(1)} %get-tuple-element.36.place, f32[512,256]{1,0:T(8,128)S(1)} %get-tuple-element.19.rest_0_, f32[512,256]{1,0:T(8,128)S(1)} %collective-permute-done.rest_1_, f32[512,256]{1,0:T(8,128)S(1)} %collective-permute-done.1.rest_2_, f32[512,256]{1,0:T(8,128)S(1)} %collective-permute-done.2.rest_3_, ...), custom_call_target="tpu_custom_call" | custom-call | flops 536870912 | bytes 8388608 | tf_op jit(solution)/shard_map/assemble/pallas_call | solution.py:36
  50.2 1.7 %solve.1 = (f32[256,256]{1,0:T(8,128)}, f32[256,256]{1,0:T(8,128)}, f32[256,256]{1,0:T(8,128)}, f32[768,256]{1,0:T(8,128)}) custom-call(s32[4]{0:T(128)S(1)} %get-tuple-element.36.place, f32[1024,256]{1,0:T(8,128)S(1)} %copy-done, f32[8,512,256]{2,1,0:T(8,128)} %assemble.2.top, f32[512,256]{1,0:T(8,128)S(1)} %get-tuple-element.20.rest_0_, ...), custom_call_target="tpu_custom_call" | custom-call | flops 536870912 | bytes 8388608 | tf_op jit(solution)/shard_map/solve/pallas_call | solution.py:36
  51.9 1.4 collective-permute-start.18
  53.3 1.4 collective-permute-start.25
  54.7 1.3 collective-permute-start.26
  56.0 1.5 collective-permute-start.19
  57.5 14.2 %collective-permute-done.26 = f32[256,256]{1,0:T(8,128)} collective-permute-done((f32[256,256]{1,0:T(8,128)}, f32[256,256]{1,0:T(8,128)}, u32[]{:S(2)}, u32[]{:S(2)}) %collective-permute-start.26) | collective-permute-done | bytes 262176 | tf_op jit(solution)/shard_map/ppermute | solution.py:313
  71.7 2.0 %add_select_fusion.3 = f32[256,256]{1,0:T(8,128)} fusion(f32[256,256]{1,0:T(8,128)} %collective-permute-done.26, f32[256,256]{1,0:T(8,128)} %collective-permute-done.18.one, f32[256,256]{1,0:T(8,128)} %collective-permute-done.25, f32[768,256]{1,0:T(8,128)} %get-tuple-element.22, pred[]{:T(512)S(6)} %eq.39), kind=kLoop, calls=%fused_computation.3 | loop fusion | flops 196608 | bytes 1310721 | tf_op jit(solution)/shard_map/jit(_where)/select_n | solution.py:357
  73.6 2.0 %collective-permute-start.28 = (f32[256,256]{1,0:T(8,128)}, f32[256,256]{1,0:T(8,128)}, u32[]{:S(2)}, u32[]{:S(2)}) collective-permute-start(f32[256,256]{1,0:T(8,128)} %add_select_fusion.3), channel_id=1, source_target_pairs={{0,160},{8,168},{16,176},{24,184},{1,161},{9,169},{17,177},{25,185... | collective-permute-start | bytes 786440 | tf_op jit(solution)/shard_map/ppermute | solution.py:319
  75.6 2.2 %collective-permute-start.27 = (f32[256,256]{1,0:T(8,128)}, f32[256,256]{1,0:T(8,128)}, u32[]{:S(2)}, u32[]{:S(2)}) collective-permute-start(f32[256,256]{1,0:T(8,128)} %add_select_fusion.3), channel_id=1, source_target_pairs={{0,96},{8,104},{16,112},{24,120},{1,97},{9,105},{17,113},{25,121},... | collective-permute-start | bytes 786440 | tf_op jit(solution)/shard_map/ppermute | solution.py:318
  77.8 1.0 copy-done.2
  78.8 1.0 copy-done.4
  79.9 0.9 copy-done.6
  80.8 0.9 copy-done.8
  81.8 0.9 copy-done.10
  82.7 2.5 %assemble.3.bottom = f32[8,512,256]{2,1,0:T(8,128)} custom-call(s32[4]{0:T(128)S(1)} %get-tuple-element.36.place, f32[512,256]{1,0:T(8,128)S(1)} %get-tuple-element.20.rest_0_, f32[512,256]{1,0:T(8,128)S(1)} %collective-permute-done.9.rest_1_, f32[512,256]{1,0:T(8,128)S(1)} %collective-permute-done.10.rest_2_, f32[512,256]{1,0:T(8,128)S(1)} %copy-done.4, ...), custom_call_target="tpu_custom_call" | custom-call | flops 536870912 | bytes 8388608 | tf_op jit(solution)/shard_map/assemble/pallas_call | solution.py:36
  85.3 1.2 add_select_fusion.2
  86.5 0.6 second.1
  87.1 1.3 collective-permute-start.30
  88.4 2.0 %collective-permute-start.29 = (f32[256,256]{1,0:T(8,128)S(1)}, f32[256,256]{1,0:T(8,128)}, u32[]{:S(2)}, u32[]{:S(2)}) collective-permute-start(f32[256,256]{1,0:T(8,128)S(1)} %add_select_fusion.2), channel_id=1, source_target_pairs={{0,32},{8,40},{16,48},{24,56},{96,128},{104,136},{112,144},{120,15... | collective-permute-start | bytes 786440 | tf_op jit(solution)/shard_map/ppermute | solution.py:324
  90.4 0.7 collective-permute-start.20
  91.1 1.3 collective-permute-start.21
  92.4 0.7 collective-permute-start.22
  93.1 0.6 collective-permute-done.30
  93.7 1.3 collective-permute-done.29
  95.0 1.0 add_select_fusion.1.rest_0_
  96.0 16.8 %collective-permute-done.21 = f32[256,256]{1,0:T(8,128)S(1)} collective-permute-done((f32[256,256]{1,0:T(8,128)S(1)}, f32[256,256]{1,0:T(8,128)S(1)}, u32[]{:S(2)}, u32[]{:S(2)}) %collective-permute-start.21) | collective-permute-done | bytes 262176 | tf_op jit(solution)/shard_map/ppermute | solution.py:313
  112.9 4.8 %collective-permute-start.33 = (f32[256,256]{1,0:T(8,128)S(1)}, f32[256,256]{1,0:T(8,128)S(1)}, u32[]{:S(2)}, u32[]{:S(2)}) collective-permute-start(f32[256,256]{1,0:T(8,128)S(1)} %add_select_fusion.1.rest_0_), channel_id=1, source_target_pairs={{0,8},{8,16},{16,24},{24,0},{32,40},{40,48},{48,56},{56,32},{64,72... | collective-permute-start | bytes 786440 | tf_op jit(solution)/shard_map/ppermute | solution.py:331
  117.7 1.3 collective-permute-start.24
  119.0 1.3 collective-permute-start.23
  120.3 1.8 %collective-permute-done.33.rest_4_ = f32[256,256]{1,0:T(8,128)S(1)} collective-permute-done((f32[256,256]{1,0:T(8,128)S(1)}, f32[256,256]{1,0:T(8,128)S(1)}, u32[]{:S(2)}, u32[]{:S(2)}) %collective-permute-start.33) | collective-permute-done | bytes 262176 | tf_op jit(solution)/shard_map/ppermute | solution.py:331
  122.1 3.8 %collective-permute-start.34 = (f32[128,256]{1,0:T(8,128)S(1)}, f32[128,256]{1,0:T(8,128)S(1)}, u32[]{:S(2)}, u32[]{:S(2)}) collective-permute-start(f32[128,256]{1,0:T(8,128)S(1)} %slice.41), channel_id=1, source_target_pairs={{0,8},{8,16},{16,24},{24,0},{32,40},{40,48},{48,56},{56,32},{64,72... | collective-permute-start | bytes 393224 | tf_op jit(solution)/shard_map/ppermute | solution.py:333
  126.1 2.3 %collective-permute-done.34.rest_3_ = f32[128,256]{1,0:T(8,128)S(1)} collective-permute-done((f32[128,256]{1,0:T(8,128)S(1)}, f32[128,256]{1,0:T(8,128)S(1)}, u32[]{:S(2)}, u32[]{:S(2)}) %collective-permute-start.34) | collective-permute-done | bytes 131104 | tf_op jit(solution)/shard_map/ppermute | solution.py:333
  128.4 3.8 %collective-permute-done.32.rest_2_ = f32[128,256]{1,0:T(8,128)S(1)} collective-permute-done((f32[128,256]{1,0:T(8,128)S(1)}, f32[128,256]{1,0:T(8,128)S(1)}, u32[]{:S(2)}, u32[]{:S(2)}) %collective-permute-start.32) | collective-permute-done | bytes 131104 | tf_op jit(solution)/shard_map/ppermute | solution.py:332
  132.2 6.0 %update0.1 = (f32[1024,256]{1,0:T(8,128)S(1)}, f32[2048,256]{1,0:T(8,128)}) custom-call(s32[4]{0:T(128)S(1)} %get-tuple-element.36.place, f32[1024,256]{1,0:T(8,128)S(1)} %copy-done, f32[8,512,256]{2,1,0:T(8,128)} %assemble.2.top, f32[8,512,256]{2,1,0:T(8,128)} %assemble.3.bottom, f32[256,256]{1,0:T(8,128)S(1)} %add_select_fusion.1.rest_0_, ...), custom_call_target="tpu_custom_call" | custom-call | flops 536870912 | bytes 8388608 | tf_op jit(solution)/shard_map/update0/pallas_call | solution.py:36
  138.1 1.3 collective-permute-start.36
  139.4 1.3 collective-permute-start.35
  140.8 2.5 %collective-permute-done.36 = f32[256,256]{1,0:T(8,128)S(1)} collective-permute-done((f32[256,256]{1,0:T(8,128)S(1)}, f32[256,256]{1,0:T(8,128)S(1)}, u32[]{:S(2)}, u32[]{:S(2)}) %collective-permute-start.36) | collective-permute-done | bytes 262176 | tf_op jit(solution)/shard_map/ppermute | solution.py:325
  143.3 1.3 collective-permute-done.35
  144.8 2.0 %collective-permute-start.37 = (f32[256,256]{1,0:T(8,128)S(1)}, f32[256,256]{1,0:T(8,128)S(1)}, u32[]{:S(2)}, u32[]{:S(2)}) collective-permute-start(f32[256,256]{1,0:T(8,128)S(1)} %add_select_fusion.rest_0_), channel_id=1, source_target_pairs={{8,0},{16,8},{24,16},{0,24},{40,32},{48,40},{56,48},{32,56},{72,64... | collective-permute-start | bytes 786440 | tf_op jit(solution)/shard_map/ppermute | solution.py:330
  146.8 5.8 %collective-permute-done.39.rest_4_ = f32[256,256]{1,0:T(8,128)S(1)} collective-permute-done((f32[256,256]{1,0:T(8,128)S(1)}, f32[256,256]{1,0:T(8,128)S(1)}, u32[]{:S(2)}, u32[]{:S(2)}) %collective-permute-start.39) | collective-permute-done | bytes 262176 | tf_op jit(solution)/shard_map/ppermute | solution.py:331
  152.5 1.1 collective-permute-start.40
  153.6 1.3 collective-permute-start.38
  155.0 2.6 %collective-permute-done.40.rest_3_ = f32[128,256]{1,0:T(8,128)S(1)} collective-permute-done((f32[128,256]{1,0:T(8,128)S(1)}, f32[128,256]{1,0:T(8,128)S(1)}, u32[]{:S(2)}, u32[]{:S(2)}) %collective-permute-start.40) | collective-permute-done | bytes 131104 | tf_op jit(solution)/shard_map/ppermute | solution.py:333
  157.6 2.5 %collective-permute-done.38.rest_2_ = f32[128,256]{1,0:T(8,128)S(1)} collective-permute-done((f32[128,256]{1,0:T(8,128)S(1)}, f32[128,256]{1,0:T(8,128)S(1)}, u32[]{:S(2)}, u32[]{:S(2)}) %collective-permute-start.38) | collective-permute-done | bytes 131104 | tf_op jit(solution)/shard_map/ppermute | solution.py:332
  160.1 6.9 %update1.1 = (f32[1024,256]{1,0:T(8,128)}, f32[2048,256]{1,0:T(8,128)}) custom-call(s32[4]{0:T(128)S(1)} %pad_add_fusion.place, f32[1024,256]{1,0:T(8,128)S(1)} %get-tuple-element.33.target, f32[8,512,256]{2,1,0:T(8,128)} %assemble.2.top, f32[8,512,256]{2,1,0:T(8,128)} %assemble.3.bottom, ...), custom_call_target="tpu_custom_call", output_to_operand_aliasing={{1}: (9, {})} | custom-call | flops 536870912 | bytes 8388608 | tf_op jit(solution)/shard_map/update1/pallas_call | solution.py:36
  (65 shorter events, 1.6 us)
Async XLA Ops:
  0.7 1.2 copy-start.11
  2.6 17.9 %collective-permute-start.3 = (f32[512,256]{1,0:T(8,128)S(1)}, f32[512,256]{1,0:T(8,128)S(1)}, u32[]{:S(2)}, u32[]{:S(2)}) collective-permute-start(f32[512,256]{1,0:T(8,128)S(1)} %get-tuple-element.19.rest_0_), channel_id=1, source_target_pairs={{0,2},{1,3},{8,10},{9,11},{10,12},{11,13},{12,14},{13,15},{14,8},{... | collective-permute-start | bytes 1572872 | tf_op jit(solution)/shard_map/ppermute | solution.py:108
  6.1 16.7 %collective-permute-start.1 = (f32[512,256]{1,0:T(8,128)S(1)}, f32[512,256]{1,0:T(8,128)S(1)}, u32[]{:S(2)}, u32[]{:S(2)}) collective-permute-start(f32[512,256]{1,0:T(8,128)S(1)} %get-tuple-element.19.rest_0_), channel_id=1, source_target_pairs={{0,6},{1,7},{8,14},{9,15},{10,8},{11,9},{12,10},{13,11},{14,12},{1... | collective-permute-start | bytes 1572872 | tf_op jit(solution)/shard_map/ppermute | solution.py:109
  9.6 22.1 %collective-permute-start.12 = (f32[512,256]{1,0:T(8,128)S(1)}, f32[512,256]{1,0:T(8,128)S(1)}, u32[]{:S(2)}, u32[]{:S(2)}) collective-permute-start(f32[512,256]{1,0:T(8,128)S(1)} %get-tuple-element.20.rest_0_), channel_id=1, source_target_pairs={{0,2},{1,3},{2,4},{3,5},{8,10},{9,11},{10,12},{11,13},{12,14},{13,... | collective-permute-start | bytes 1572872 | tf_op jit(solution)/shard_map/ppermute | solution.py:108
  11.9 22.1 %collective-permute-start.10 = (f32[512,256]{1,0:T(8,128)S(1)}, f32[512,256]{1,0:T(8,128)S(1)}, u32[]{:S(2)}, u32[]{:S(2)}) collective-permute-start(f32[512,256]{1,0:T(8,128)S(1)} %get-tuple-element.20.rest_0_), channel_id=1, source_target_pairs={{0,6},{1,7},{2,0},{3,1},{8,14},{9,15},{10,8},{11,9},{12,10},{13,11... | collective-permute-start | bytes 1572872 | tf_op jit(solution)/shard_map/ppermute | solution.py:109
  16.7 20.9 %collective-permute-start = (f32[512,256]{1,0:T(8,128)S(1)}, f32[512,256]{1,0:T(8,128)S(1)}, u32[]{:S(2)}, u32[]{:S(2)}) collective-permute-start(f32[512,256]{1,0:T(8,128)S(1)} %get-tuple-element.19.rest_0_), channel_id=1, source_target_pairs={{0,1},{1,0},{2,3},{3,2},{4,5},{5,4},{6,7},{7,6},{8,9},{9,8},{10,11... | collective-permute-start | bytes 1572872 | tf_op jit(solution)/shard_map/ppermute | solution.py:104
  20.5 20.8 %collective-permute-start.7 = (f32[256,256]{1,0:T(8,128)S(1)}, f32[256,256]{1,0:T(8,128)S(1)}, u32[]{:S(2)}, u32[]{:S(2)}) collective-permute-start(f32[256,256]{1,0:T(8,128)S(1)} %slice.37), channel_id=1, source_target_pairs={{2,4},{3,5},{8,10},{9,11},{10,12},{11,13},{12,14},{13,15},{14,8},{... | collective-permute-start | bytes 786440 | tf_op jit(solution)/shard_map/ppermute | solution.py:113
  22.8 18.6 %collective-permute-start.5 = (f32[256,256]{1,0:T(8,128)S(1)}, f32[256,256]{1,0:T(8,128)S(1)}, u32[]{:S(2)}, u32[]{:S(2)}) collective-permute-start(f32[256,256]{1,0:T(8,128)S(1)} %slice.36), channel_id=1, source_target_pairs={{6,4},{7,5},{8,14},{9,15},{10,8},{11,9},{12,10},{13,11},{14,12},{1... | collective-permute-start | bytes 786440 | tf_op jit(solution)/shard_map/ppermute | solution.py:113
  31.7 14.8 %collective-permute-start.4 = (f32[512,256]{1,0:T(8,128)S(1)}, f32[512,256]{1,0:T(8,128)S(1)}, u32[]{:S(2)}, u32[]{:S(2)}) collective-permute-start(f32[512,256]{1,0:T(8,128)S(1)} %collective-permute-done.3.rest_4_), channel_id=1, source_target_pairs={{0,1},{1,0},{2,3},{3,2},{4,5},{5,4},{6,7},{7,6},{8,9},{9,8},{10,11... | collective-permute-start | bytes 1572872 | tf_op jit(solution)/shard_map/ppermute | solution.py:104
  34.0 9.5 %collective-permute-start.16 = (f32[256,256]{1,0:T(8,128)S(1)}, f32[256,256]{1,0:T(8,128)S(1)}, u32[]{:S(2)}, u32[]{:S(2)}) collective-permute-start(f32[256,256]{1,0:T(8,128)S(1)} %slice.39), channel_id=1, source_target_pairs={{2,4},{3,5},{4,6},{5,7},{8,10},{9,11},{10,12},{11,13},{12,14},{13,... | collective-permute-start | bytes 786440 | tf_op jit(solution)/shard_map/ppermute | solution.py:113
  37.6 12.6 %copy-start = (f32[1024,256]{1,0:T(8,128)S(1)}, f32[1024,256]{1,0:T(8,128)}, u32[]{:S(2)}) copy-start(f32[1024,256]{1,0:T(8,128)} %target.1) | copy-start | bytes 3145732
  37.6 8.4 %collective-permute-start.14 = (f32[256,256]{1,0:T(8,128)S(1)}, f32[256,256]{1,0:T(8,128)S(1)}, u32[]{:S(2)}, u32[]{:S(2)}) collective-permute-start(f32[256,256]{1,0:T(8,128)S(1)} %slice.38), channel_id=1, source_target_pairs={{0,6},{1,7},{6,4},{7,5},{8,14},{9,15},{10,8},{11,9},{12,10},{13,11... | collective-permute-start | bytes 786440 | tf_op jit(solution)/shard_map/ppermute | solution.py:113
  41.3 4.7 %collective-permute-start.8 = (f32[256,256]{1,0:T(8,128)S(1)}, f32[256,256]{1,0:T(8,128)S(1)}, u32[]{:S(2)}, u32[]{:S(2)}) collective-permute-start(f32[256,256]{1,0:T(8,128)S(1)} %collective-permute-done.7.rest_8_), channel_id=1, source_target_pairs={{0,1},{1,0},{2,3},{3,2},{4,5},{5,4},{6,7},{7,6},{8,9},{9,8},{10,11... | collective-permute-start | bytes 786440 | tf_op jit(solution)/shard_map/ppermute | solution.py:104
  41.4 5.6 %collective-permute-start.2 = (f32[512,256]{1,0:T(8,128)S(1)}, f32[512,256]{1,0:T(8,128)S(1)}, u32[]{:S(2)}, u32[]{:S(2)}) collective-permute-start(f32[512,256]{1,0:T(8,128)S(1)} %collective-permute-done.1.rest_2_), channel_id=1, source_target_pairs={{0,1},{1,0},{2,3},{3,2},{4,5},{5,4},{6,7},{7,6},{8,9},{9,8},{10,11... | collective-permute-start | bytes 1572872 | tf_op jit(solution)/shard_map/ppermute | solution.py:104
  43.6 3.0 %collective-permute-start.6 = (f32[256,256]{1,0:T(8,128)S(1)}, f32[256,256]{1,0:T(8,128)S(1)}, u32[]{:S(2)}, u32[]{:S(2)}) collective-permute-start(f32[256,256]{1,0:T(8,128)S(1)} %collective-permute-done.5.rest_6_), channel_id=1, source_target_pairs={{0,1},{1,0},{2,3},{3,2},{4,5},{5,4},{6,7},{7,6},{8,9},{9,8},{10,11... | collective-permute-start | bytes 786440 | tf_op jit(solution)/shard_map/ppermute | solution.py:104
  46.0 4.2 %copy-start.5 = (f32[256,256]{1,0:T(8,128)}, f32[256,256]{1,0:T(8,128)S(1)}, u32[]{:S(2)}) copy-start(f32[256,256]{1,0:T(8,128)S(1)} %collective-permute-done.14.rest_6_) | copy-start | bytes 786436
  46.0 3.7 %collective-permute-start.9 = (f32[512,256]{1,0:T(8,128)S(1)}, f32[512,256]{1,0:T(8,128)S(1)}, u32[]{:S(2)}, u32[]{:S(2)}) collective-permute-start(f32[512,256]{1,0:T(8,128)S(1)} %get-tuple-element.20.rest_0_), channel_id=1, source_target_pairs={{0,1},{1,0},{2,3},{3,2},{4,5},{5,4},{6,7},{7,6},{8,9},{9,8},{10,11... | collective-permute-start | bytes 1572872 | tf_op jit(solution)/shard_map/ppermute | solution.py:104
  46.0 3.8 %collective-permute-start.13 = (f32[512,256]{1,0:T(8,128)S(1)}, f32[512,256]{1,0:T(8,128)S(1)}, u32[]{:S(2)}, u32[]{:S(2)}) collective-permute-start(f32[512,256]{1,0:T(8,128)S(1)} %collective-permute-done.12.rest_4_), channel_id=1, source_target_pairs={{0,1},{1,0},{2,3},{3,2},{4,5},{5,4},{6,7},{7,6},{8,9},{9,8},{10,11... | collective-permute-start | bytes 1572872 | tf_op jit(solution)/shard_map/ppermute | solution.py:104
  46.5 3.6 %collective-permute-start.11 = (f32[512,256]{1,0:T(8,128)S(1)}, f32[512,256]{1,0:T(8,128)S(1)}, u32[]{:S(2)}, u32[]{:S(2)}) collective-permute-start(f32[512,256]{1,0:T(8,128)S(1)} %collective-permute-done.10.rest_2_), channel_id=1, source_target_pairs={{0,1},{1,0},{2,3},{3,2},{4,5},{5,4},{6,7},{7,6},{8,9},{9,8},{10,11... | collective-permute-start | bytes 1572872 | tf_op jit(solution)/shard_map/ppermute | solution.py:104
  46.6 3.2 %collective-permute-start.17 = (f32[256,256]{1,0:T(8,128)S(1)}, f32[256,256]{1,0:T(8,128)S(1)}, u32[]{:S(2)}, u32[]{:S(2)}) collective-permute-start(f32[256,256]{1,0:T(8,128)S(1)} %collective-permute-done.16.rest_8_), channel_id=1, source_target_pairs={{0,1},{1,0},{2,3},{3,2},{4,5},{5,4},{6,7},{7,6},{8,9},{9,8},{10,11... | collective-permute-start | bytes 786440 | tf_op jit(solution)/shard_map/ppermute | solution.py:104
  47.0 3.1 %collective-permute-start.15 = (f32[256,256]{1,0:T(8,128)S(1)}, f32[256,256]{1,0:T(8,128)S(1)}, u32[]{:S(2)}, u32[]{:S(2)}) collective-permute-start(f32[256,256]{1,0:T(8,128)S(1)} %collective-permute-done.14.rest_6_), channel_id=1, source_target_pairs={{0,1},{1,0},{2,3},{3,2},{4,5},{5,4},{6,7},{7,6},{8,9},{9,8},{10,11... | collective-permute-start | bytes 786440 | tf_op jit(solution)/shard_map/ppermute | solution.py:104
  49.8 2.1 %copy-start.7 = (f32[256,256]{1,0:T(8,128)}, f32[256,256]{1,0:T(8,128)S(1)}, u32[]{:S(2)}) copy-start(f32[256,256]{1,0:T(8,128)S(1)} %collective-permute-done.17.rest_9_) | copy-start | bytes 786436
  49.8 2.1 %copy-start.1 = (f32[512,256]{1,0:T(8,128)}, f32[512,256]{1,0:T(8,128)S(1)}, u32[]{:S(2)}) copy-start(f32[512,256]{1,0:T(8,128)S(1)} %collective-permute-done.13.rest_5_) | copy-start | bytes 1572868
  50.1 1.8 %copy-start.9 = (f32[256,256]{1,0:T(8,128)}, f32[256,256]{1,0:T(8,128)S(1)}, u32[]{:S(2)}) copy-start(f32[256,256]{1,0:T(8,128)S(1)} %collective-permute-done.15.rest_7_) | copy-start | bytes 786436
  50.2 1.8 %copy-start.3 = (f32[512,256]{1,0:T(8,128)}, f32[512,256]{1,0:T(8,128)S(1)}, u32[]{:S(2)}) copy-start(f32[512,256]{1,0:T(8,128)S(1)} %collective-permute-done.11.rest_3_) | copy-start | bytes 1572868
  51.9 5.6 %collective-permute-start.18 = (f32[256,256]{1,0:T(8,128)}, f32[256,256]{1,0:T(8,128)}, u32[]{:S(2)}, u32[]{:S(2)}) collective-permute-start(f32[256,256]{1,0:T(8,128)} %get-tuple-element.21), channel_id=1, source_target_pairs={{0,8},{1,9},{2,10},{3,11},{4,12},{5,13},{6,14},{7,15}} | collective-permute-start | bytes 786440 | tf_op jit(solution)/shard_map/ppermute | solution.py:313
  53.3 4.2 %collective-permute-start.25 = (f32[256,256]{1,0:T(8,128)}, f32[256,256]{1,0:T(8,128)}, u32[]{:S(2)}, u32[]{:S(2)}) collective-permute-start(f32[256,256]{1,0:T(8,128)} %get-tuple-element.27), channel_id=1, source_target_pairs={{0,16},{1,17},{2,18},{3,19},{4,20},{5,21},{6,22},{7,23}} | collective-permute-start | bytes 786440 | tf_op jit(solution)/shard_map/ppermute | solution.py:313
  54.7 17.0 %collective-permute-start.26 = (f32[256,256]{1,0:T(8,128)}, f32[256,256]{1,0:T(8,128)}, u32[]{:S(2)}, u32[]{:S(2)}) collective-permute-start(f32[256,256]{1,0:T(8,128)} %get-tuple-element.28), channel_id=1, source_target_pairs={{0,24},{1,25},{2,26},{3,27},{4,28},{5,29},{6,30},{7,31}} | collective-permute-start | bytes 786440 | tf_op jit(solution)/shard_map/ppermute | solution.py:313
  56.0 30.5 %collective-permute-start.19 = (f32[768,256]{1,0:T(8,128)}, f32[768,256]{1,0:T(8,128)}, u32[]{:S(2)}, u32[]{:S(2)}) collective-permute-start(f32[768,256]{1,0:T(8,128)} %get-tuple-element.22), channel_id=1, source_target_pairs={{0,8},{1,9},{2,10},{3,11},{4,12},{5,13},{6,14},{7,15}} | collective-permute-start | bytes 2359304 | tf_op jit(solution)/shard_map/ppermute | solution.py:354
  73.6 11.6 %collective-permute-start.28 = (f32[256,256]{1,0:T(8,128)}, f32[256,256]{1,0:T(8,128)}, u32[]{:S(2)}, u32[]{:S(2)}) collective-permute-start(f32[256,256]{1,0:T(8,128)} %add_select_fusion.3), channel_id=1, source_target_pairs={{0,160},{8,168},{16,176},{24,184},{1,161},{9,169},{17,177},{25,185... | collective-permute-start | bytes 786440 | tf_op jit(solution)/shard_map/ppermute | solution.py:319
  75.6 9.6 %collective-permute-start.27 = (f32[256,256]{1,0:T(8,128)}, f32[256,256]{1,0:T(8,128)}, u32[]{:S(2)}, u32[]{:S(2)}) collective-permute-start(f32[256,256]{1,0:T(8,128)} %add_select_fusion.3), channel_id=1, source_target_pairs={{0,96},{8,104},{16,112},{24,120},{1,97},{9,105},{17,113},{25,121},... | collective-permute-start | bytes 786440 | tf_op jit(solution)/shard_map/ppermute | solution.py:318
  77.8 1.0 copy-start.2
  78.8 1.0 copy-start.4
  79.9 0.9 copy-start.6
  80.8 0.9 copy-start.8
  81.8 0.9 copy-start.10
  87.1 6.6 %collective-permute-start.30 = (f32[256,256]{1,0:T(8,128)S(1)}, f32[256,256]{1,0:T(8,128)S(1)}, u32[]{:S(2)}, u32[]{:S(2)}) collective-permute-start(f32[256,256]{1,0:T(8,128)S(1)} %add_select_fusion.2), channel_id=1, source_target_pairs={{0,224},{8,232},{16,240},{24,248},{96,64},{104,72},{112,80},{120,8... | collective-permute-start | bytes 786440 | tf_op jit(solution)/shard_map/ppermute | solution.py:325
  88.4 6.6 %collective-permute-start.29 = (f32[256,256]{1,0:T(8,128)S(1)}, f32[256,256]{1,0:T(8,128)}, u32[]{:S(2)}, u32[]{:S(2)}) collective-permute-start(f32[256,256]{1,0:T(8,128)S(1)} %add_select_fusion.2), channel_id=1, source_target_pairs={{0,32},{8,40},{16,48},{24,56},{96,128},{104,136},{112,144},{120,15... | collective-permute-start | bytes 786440 | tf_op jit(solution)/shard_map/ppermute | solution.py:324
  90.4 5.6 %collective-permute-start.20 = (f32[256,256]{1,0:T(8,128)S(1)}, f32[256,256]{1,0:T(8,128)S(1)}, u32[]{:S(2)}, u32[]{:S(2)}) collective-permute-start(f32[256,256]{1,0:T(8,128)S(1)} %get-tuple-element.24), channel_id=1, source_target_pairs={{8,16},{9,17},{10,18},{11,19},{12,20},{13,21},{14,22},{15,23}} | collective-permute-start | bytes 786440 | tf_op jit(solution)/shard_map/ppermute | solution.py:313
  91.1 21.8 %collective-permute-start.21 = (f32[256,256]{1,0:T(8,128)S(1)}, f32[256,256]{1,0:T(8,128)S(1)}, u32[]{:S(2)}, u32[]{:S(2)}) collective-permute-start(f32[256,256]{1,0:T(8,128)S(1)} %get-tuple-element.25), channel_id=1, source_target_pairs={{8,24},{9,25},{10,26},{11,27},{12,28},{13,29},{14,30},{15,31}} | collective-permute-start | bytes 786440 | tf_op jit(solution)/shard_map/ppermute | solution.py:313
  92.4 20.5 %collective-permute-start.22 = (f32[256,256]{1,0:T(8,128)S(1)}, f32[256,256]{1,0:T(8,128)S(1)}, u32[]{:S(2)}, u32[]{:S(2)}) collective-permute-start(f32[256,256]{1,0:T(8,128)S(1)} %get-tuple-element.26), channel_id=1, source_target_pairs={{8,0},{9,1},{10,2},{11,3},{12,4},{13,5},{14,6},{15,7}} | collective-permute-start | bytes 786440 | tf_op jit(solution)/shard_map/ppermute | solution.py:313
  112.9 9.2 %collective-permute-start.33 = (f32[256,256]{1,0:T(8,128)S(1)}, f32[256,256]{1,0:T(8,128)S(1)}, u32[]{:S(2)}, u32[]{:S(2)}) collective-permute-start(f32[256,256]{1,0:T(8,128)S(1)} %add_select_fusion.1.rest_0_), channel_id=1, source_target_pairs={{0,8},{8,16},{16,24},{24,0},{32,40},{40,48},{48,56},{56,32},{64,72... | collective-permute-start | bytes 786440 | tf_op jit(solution)/shard_map/ppermute | solution.py:331
  117.7 8.2 %collective-permute-start.31 = (f32[256,256]{1,0:T(8,128)S(1)}, f32[256,256]{1,0:T(8,128)S(1)}, u32[]{:S(2)}, u32[]{:S(2)}) collective-permute-start(f32[256,256]{1,0:T(8,128)S(1)} %add_select_fusion.1.rest_0_), channel_id=1, source_target_pairs={{8,0},{16,8},{24,16},{0,24},{40,32},{48,40},{56,48},{32,56},{72,64... | collective-permute-start | bytes 786440 | tf_op jit(solution)/shard_map/ppermute | solution.py:330
  117.7 8.3 %collective-permute-start.24 = (f32[256,256]{1,0:T(8,128)S(1)}, f32[256,256]{1,0:T(8,128)S(1)}, u32[]{:S(2)}, u32[]{:S(2)}) collective-permute-start(f32[256,256]{1,0:T(8,128)S(1)} %add_select_fusion.5), channel_id=1, source_target_pairs={{0,160},{8,168},{16,176},{24,184},{1,161},{9,169},{17,177},{25,185... | collective-permute-start | bytes 786440 | tf_op jit(solution)/shard_map/ppermute | solution.py:319
  119.0 7.0 %collective-permute-start.23 = (f32[256,256]{1,0:T(8,128)S(1)}, f32[256,256]{1,0:T(8,128)S(1)}, u32[]{:S(2)}, u32[]{:S(2)}) collective-permute-start(f32[256,256]{1,0:T(8,128)S(1)} %add_select_fusion.5), channel_id=1, source_target_pairs={{0,96},{8,104},{16,112},{24,120},{1,97},{9,105},{17,113},{25,121},... | collective-permute-start | bytes 786440 | tf_op jit(solution)/shard_map/ppermute | solution.py:318
  122.1 6.3 %collective-permute-start.34 = (f32[128,256]{1,0:T(8,128)S(1)}, f32[128,256]{1,0:T(8,128)S(1)}, u32[]{:S(2)}, u32[]{:S(2)}) collective-permute-start(f32[128,256]{1,0:T(8,128)S(1)} %slice.41), channel_id=1, source_target_pairs={{0,8},{8,16},{16,24},{24,0},{32,40},{40,48},{48,56},{56,32},{64,72... | collective-permute-start | bytes 393224 | tf_op jit(solution)/shard_map/ppermute | solution.py:333
  125.9 6.3 %collective-permute-start.32 = (f32[128,256]{1,0:T(8,128)S(1)}, f32[128,256]{1,0:T(8,128)S(1)}, u32[]{:S(2)}, u32[]{:S(2)}) collective-permute-start(f32[128,256]{1,0:T(8,128)S(1)} %slice.40), channel_id=1, source_target_pairs={{8,0},{16,8},{24,16},{0,24},{40,32},{48,40},{56,48},{32,56},{72,64... | collective-permute-start | bytes 393224 | tf_op jit(solution)/shard_map/ppermute | solution.py:332
  138.1 5.2 %collective-permute-start.36 = (f32[256,256]{1,0:T(8,128)S(1)}, f32[256,256]{1,0:T(8,128)S(1)}, u32[]{:S(2)}, u32[]{:S(2)}) collective-permute-start(f32[256,256]{1,0:T(8,128)S(1)} %add_select_fusion.4), channel_id=1, source_target_pairs={{0,224},{8,232},{16,240},{24,248},{96,64},{104,72},{112,80},{120,8... | collective-permute-start | bytes 786440 | tf_op jit(solution)/shard_map/ppermute | solution.py:325
  139.4 5.2 %collective-permute-start.35 = (f32[256,256]{1,0:T(8,128)S(1)}, f32[256,256]{1,0:T(8,128)S(1)}, u32[]{:S(2)}, u32[]{:S(2)}) collective-permute-start(f32[256,256]{1,0:T(8,128)S(1)} %add_select_fusion.4), channel_id=1, source_target_pairs={{0,32},{8,40},{16,48},{24,56},{96,128},{104,136},{112,144},{120,15... | collective-permute-start | bytes 786440 | tf_op jit(solution)/shard_map/ppermute | solution.py:324
  144.7 7.9 %collective-permute-start.39 = (f32[256,256]{1,0:T(8,128)S(1)}, f32[256,256]{1,0:T(8,128)S(1)}, u32[]{:S(2)}, u32[]{:S(2)}) collective-permute-start(f32[256,256]{1,0:T(8,128)S(1)} %add_select_fusion.rest_0_), channel_id=1, source_target_pairs={{0,8},{8,16},{16,24},{24,0},{32,40},{40,48},{48,56},{56,32},{64,72... | collective-permute-start | bytes 786440 | tf_op jit(solution)/shard_map/ppermute | solution.py:331
  144.8 8.9 %collective-permute-start.37 = (f32[256,256]{1,0:T(8,128)S(1)}, f32[256,256]{1,0:T(8,128)S(1)}, u32[]{:S(2)}, u32[]{:S(2)}) collective-permute-start(f32[256,256]{1,0:T(8,128)S(1)} %add_select_fusion.rest_0_), channel_id=1, source_target_pairs={{8,0},{16,8},{24,16},{0,24},{40,32},{48,40},{56,48},{32,56},{72,64... | collective-permute-start | bytes 786440 | tf_op jit(solution)/shard_map/ppermute | solution.py:330
  152.5 5.0 %collective-permute-start.40 = (f32[128,256]{1,0:T(8,128)S(1)}, f32[128,256]{1,0:T(8,128)S(1)}, u32[]{:S(2)}, u32[]{:S(2)}) collective-permute-start(f32[128,256]{1,0:T(8,128)S(1)} %slice.43), channel_id=1, source_target_pairs={{0,8},{8,16},{16,24},{24,0},{32,40},{40,48},{48,56},{56,32},{64,72... | collective-permute-start | bytes 393224 | tf_op jit(solution)/shard_map/ppermute | solution.py:333
  153.6 6.5 %collective-permute-start.38 = (f32[128,256]{1,0:T(8,128)S(1)}, f32[128,256]{1,0:T(8,128)S(1)}, u32[]{:S(2)}, u32[]{:S(2)}) collective-permute-start(f32[128,256]{1,0:T(8,128)S(1)} %slice.42), channel_id=1, source_target_pairs={{8,0},{16,8},{24,16},{0,24},{40,32},{48,40},{56,48},{32,56},{72,64... | collective-permute-start | bytes 393224 | tf_op jit(solution)/shard_map/ppermute | solution.py:332

commit v3 on v2

v3 whole, which is shorter than its diff:
```python
import functools

import jax
import jax.numpy as jnp
from jax import lax
from jax.experimental import pallas as pl
from jax.experimental.pallas import tpu as pltpu
from jax.sharding import PartitionSpec as P

NB = 1024
HALF = NB // 2
Q = 256
PARTS = 4
XS = 4
YS = 4
ZS = 8
ROWS = XS * ZS
COLS = 2 * YS
F32 = jnp.float32
BF16 = jnp.bfloat16
BOTH = ("row", "col")
UPDATE_COST = 60


def halves(value):
    high = value.astype(BF16)
    return high, (value - high.astype(F32)).astype(BF16)


def product(left, right):
    dot = functools.partial(jnp.dot, preferred_element_type=F32)
    return dot(left[0], right[0]) + (dot(left[0], right[1]) + dot(left[1], right[0]))


def call(kernel, name, shapes, scratch, operands, in_specs=None, out_specs=None, vmem=24, flops=2 * NB * NB * Q, **options):
    operands = [pltpu.with_memory_space_constraint(x, pltpu.HBM) if x.ndim == 3 else x for x in operands]
    return pl.pallas_call(
        kernel,
        out_shape=[(pltpu.HBM if len(shape) == 3 else jax.ShapeDtypeStruct)(shape, dtype) for shape, dtype in shapes],
        in_specs=[pl.BlockSpec(memory_space=pltpu.SMEM)]
        + (in_specs or [pl.BlockSpec(memory_space=pl.ANY)] * (len(operands) - 1)),
        out_specs=out_specs or [pl.BlockSpec(memory_space=pltpu.VMEM)] * len(shapes),
        scratch_shapes=scratch,
        compiler_params=pltpu.CompilerParams(vmem_limit_bytes=vmem << 20),
        cost_estimate=pl.CostEstimate(flops=flops, bytes_accessed=8 << 20, transcendentals=0),
        name=name,
        **options,
    )(*operands)


ROW, PLACE_Y, CORE, TURN = range(4)


def payload_kernel(place, panel_ref, top_ref, bottom_ref):
    top_ref[...] = panel_ref[pl.ds(0, HALF), :]
    bottom_ref[...] = panel_ref[pl.ds(HALF, HALF), :]
    col = 2 * place[PLACE_Y] + place[CORE]
    number = col & (PARTS - 1)

    @pl.when(((place[ROW] == 0) & (col < PARTS)) | ((place[ROW] == 1) & (col >= PARTS)))
    def _():
        rows = lax.broadcasted_iota(jnp.int32, (Q, Q), 0)
        cols = lax.broadcasted_iota(jnp.int32, (Q, Q), 1)
        block = panel_ref[pl.ds(pl.multiple_of(number * Q, Q), Q), :]
        inverse = jnp.where(rows == cols, 1.0 / jnp.where(rows == cols, block, 1.0), 0.0)
        level = 0
        while (1 << level) < Q:
            pair = (rows >> (level + 1)) == (cols >> (level + 1))
            below = pair & (((rows >> level) & 1) == 1) & (((cols >> level) & 1) == 0)
            parts = halves(inverse)
            inner = product(halves(jnp.where(below, block, 0.0)), parts)
            inverse = inverse - product(parts, halves(inner))
            level += 1
        for i in range(PARTS):

            @pl.when(number == i)
            def _():
                half = (top_ref, bottom_ref)[i // 2]
                half[pl.ds((i % 2) * Q, Q), :] = inverse


def payload(place, panel):
    vmem = [pl.BlockSpec(memory_space=pltpu.VMEM)]
    return call(payload_kernel, "payload", [((HALF, Q), F32)] * 2, [], (place, panel), in_specs=vmem)


CHUNK = tuple((step, same) for step in (0, 1, 3, 2) for same in (True, False))


def pairs(step, origin, has):
    return [
        (r * COLS + 2 * y + k, r * COLS + 2 * ((y + step) % YS) + k)
        for r in range(ROWS)
        for y in range(YS)
        for k in (0, 1)
        if has(r, (y + origin) % YS)
    ]


def other_core(value):
    return lax.ppermute(value, "col", [(c, c ^ 1) for c in range(COLS)])


def near_chips(chunk, has):
    behind = lax.ppermute(chunk, BOTH, pairs(1, 0, has))
    return lax.ppermute(chunk, BOTH, pairs(-1, 0, has)), behind


def far_chip(ahead, behind, has):
    if behind is None:
        return lax.ppermute(ahead, BOTH, pairs(-1, 1, has))
    return lax.ppermute(behind, BOTH, pairs(1, -1, has))


def both_cores(values):
    return [x for value in values for x in (value, other_core(value))]


def assemble_kernel(place, *rest):
    arrays, (out, sem) = rest[: len(CHUNK)], rest[len(CHUNK) :]
    blocks = jnp.where(place[ROW] == 0, PARTS, COLS)
    for wait in (False, True):
        for (step, same), array in zip(CHUNK, arrays):
            core = place[CORE] if same else 1 - place[CORE]
            block = 2 * ((place[PLACE_Y] + step) & (YS - 1)) + core

            @pl.when(block < blocks)
            def _():
                copy = pltpu.make_async_copy(array, out.at[block], sem.at[block])
                copy.wait() if wait else copy.start()


def assemble(place, arrays):
    in_hbm = [pl.BlockSpec(memory_space=pltpu.HBM)]
    scratch = [pltpu.SemaphoreType.DMA((COLS,))]
    shapes = [((COLS, HALF, Q), F32)]
    return call(assemble_kernel, "assemble", shapes, scratch, (place, *arrays), out_specs=in_hbm)[0]


def blocks_copies(top, bottom, base, buffer, sems):
    copies = [
        pltpu.make_async_copy(half.at[pl.ds(base, PARTS)], buffer.at[:, pl.ds(i * HALF, HALF)], sems.at[i])
        for i, half in enumerate((top, bottom))
    ]
    for copy in copies:
        copy.start()
    return copies


def eliminate(triangle, targets, store):
    for i in range(PARTS):
        value = product(halves(triangle[i, pl.ds(i * Q, Q), :]), halves(targets[i]))
        store(i, value)
        parts = halves(value)
        for k in range(i + 1, PARTS):
            targets[k] = targets[k] - product(halves(triangle[i, pl.ds(k * Q, Q), :]), parts)


def solve_kernel(place, rhs, top, bottom, whole, two, three, triangle, rhs_buf, sem, rhs_sem):
    @pl.when(place[ROW] == 0)
    def _():
        copy = pltpu.make_async_copy(rhs, rhs_buf, rhs_sem)
        copy.start()
        for wait in blocks_copies(top, bottom, 0, triangle, sem):
            wait.wait()
        copy.wait()

        def store(i, value):
            whole[pl.ds(i * Q, Q), :] = value
            if i >= 2:
                (two, three)[i - 2][...] = value

        eliminate(triangle, [rhs_buf[pl.ds(i * Q, Q), :] for i in range(PARTS)], store)


def solve(place, rhs, top, bottom):
    scratch = [
        pltpu.VMEM((PARTS, NB, Q), F32),
        pltpu.VMEM((NB, Q), F32),
        pltpu.SemaphoreType.DMA((2,)),
        pltpu.SemaphoreType.DMA,
    ]
    shapes = [((NB, Q), F32), ((Q, Q), F32), ((Q, Q), F32)]
    return call(solve_kernel, "solve", shapes, scratch, (place, rhs, top, bottom))


def prepare_kernel(place, rhs, top, bottom, w_high, w_low, y_out, triangle, targets, sem, left_sem, rhs_sem):
    @pl.when(place[ROW] == 1)
    def _():
        copies = [pltpu.make_async_copy(rhs, targets.at[:, pl.ds(NB, Q)], rhs_sem)]
        for j in range(PARTS):
            for i, half in enumerate((top, bottom)):
                target = targets.at[pl.ds(i * HALF, HALF), pl.ds(j * Q, Q)]
                copies.append(pltpu.make_async_copy(half.at[j], target, left_sem.at[2 * j + i]))
        for copy in copies:
            copy.start()
        for copy in (*blocks_copies(top, bottom, PARTS, triangle, sem), *copies):
            copy.wait()
        for i in range(PARTS):
            rows = pl.ds(i * Q, Q)
            value = product(halves(triangle[i, rows, :]), halves(targets[rows, :]))
            parts = halves(value)
            w_high[rows, :], w_low[rows, :] = parts[0][:, :NB], parts[1][:, :NB]
            y_out[rows, :] = value[:, NB:]
            for k in range(i + 1, PARTS):
                below = pl.ds(k * Q, Q)
                targets[below, :] -= product(halves(triangle[i, below, :]), parts)


def prepare(place, rhs, top, bottom):
    scratch = [
        pltpu.VMEM((PARTS, NB, Q), F32),
        pltpu.VMEM((NB, NB + Q), F32),
        pltpu.SemaphoreType.DMA((2,)),
        pltpu.SemaphoreType.DMA((2 * PARTS,)),
        pltpu.SemaphoreType.DMA,
    ]
    shapes = [((NB, NB), BF16)] * 2 + [((NB, Q), F32)]
    return call(prepare_kernel, "prepare", shapes, scratch, (place, rhs, top, bottom), vmem=32)


def combine_kernel(place, w_high, w_low, y_ref, first, *out):
    @pl.when(place[ROW] == 1)
    def _():
        solved = halves(first[...])
        for i in range(PARTS):
            rows = pl.ds(i * Q, Q)
            out[i][...] = y_ref[rows, :] - product((w_high[rows, :], w_low[rows, :]), solved)


def combine(place, w_high, w_low, y_value, first):
    vmem = [pl.BlockSpec(memory_space=pltpu.VMEM)] * 4
    operands = (place, w_high, w_low, y_value, first)
    return call(combine_kernel, "combine", [((Q, Q), F32)] * PARTS, [], operands, in_specs=vmem)


PIECES = ((0, Q), (Q, Q), (2 * Q, Q // 2), (2 * Q + Q // 2, Q // 2), (3 * Q, Q))


def update_kernel(base, slots, last, place, target, top, bottom, *rest):
    used = [n for n, (at, _) in enumerate(PIECES) if at // Q in slots]
    pieces, rest = rest[: len(used)], rest[len(used) + int(base + len(slots) > PARTS) :]
    out, whole, blocks, target_buf, solved_buf, sem, target_sem, solved_sem, whole_sem = rest
    copies, kept = [], []
    for i, (n, piece) in enumerate(zip(used, pieces)):
        at, length = PIECES[n]
        here = pl.ds(slots.index(at // Q) * Q + at % Q, length)
        copies.append(pltpu.make_async_copy(piece, solved_buf.at[here], solved_sem.at[i]))
        start = pl.multiple_of(((at + place[TURN] * Q) & (NB - 1)) + base * Q, Q // 2)
        kept.append(pltpu.make_async_copy(solved_buf.at[here], whole.at[pl.ds(start, length)], whole_sem.at[i]))
    copies.append(pltpu.make_async_copy(target, target_buf, target_sem))
    for i, slot in enumerate(slots):
        block = base + ((slot + place[TURN]) & (PARTS - 1))
        for k, half in enumerate((top, bottom)):
            copies.append(
                pltpu.make_async_copy(half.at[block], blocks.at[i, pl.ds(k * HALF, HALF)], sem.at[2 * i + k])
            )
    for copy in copies:
        copy.start()
    for copy in copies[: len(used)]:
        copy.wait()
    for copy in kept:
        copy.start()
    solved = [halves(solved_buf[pl.ds(i * Q, Q), :]) for i in range(len(slots))]
    for copy in copies[len(used) :]:
        copy.wait()
    for r in range(PARTS):
        rows = pl.ds(r * Q, Q)
        result = target_buf[rows, :]
        for i in range(len(slots)):
            result = result - product(halves(blocks[i, rows, :]), solved[i])
        out[rows, :] = jnp.where(place[ROW] >= 2, result, 0.0) if last else result
    for copy in kept:
        copy.wait()


def update(name, base, slots, last, place, target, top, bottom, pieces, *before):
    scratch = [
        pltpu.VMEM((len(slots), NB, Q), F32),
        pltpu.VMEM((NB, Q), F32),
        pltpu.VMEM((len(slots) * Q, Q), F32),
        pltpu.SemaphoreType.DMA((2 * len(slots),)),
        pltpu.SemaphoreType.DMA,
        pltpu.SemaphoreType.DMA((len(pieces),)),
        pltpu.SemaphoreType.DMA((len(pieces),)),
    ]
    operands = (place, target, top, bottom, *pieces, *before)
    return call(
        functools.partial(update_kernel, base, slots, last),
        name,
        [((NB, Q), F32), ((2 * NB, Q), F32)],
        scratch,
        operands,
        out_specs=[pl.BlockSpec(memory_space=pltpu.VMEM), pl.BlockSpec(memory_space=pl.ANY)],
        input_output_aliases={len(operands) - 1: 1} if before else {},
        flops=(6 if before else UPDATE_COST) * NB * NB * Q,
    )


def along_z(moves):
    return [(a * XS + x, b * XS + x) for a, b in moves for x in range(XS)]


TO_NEXT = [(r, r // XS * XS + (r + 1) % XS) for r in range(ROWS)]
TO_LAST = [(b, a) for a, b in TO_NEXT]


def after(value, *others):
    return lax.optimization_barrier((value, *others))[0]


def scatter_first(two, three):
    relay = lax.ppermute(two, "row", [(0, 3)])
    return lax.ppermute(relay, "row", [(3, 2)]), lax.ppermute(three, "row", [(0, 3)])


def scatter_second(pieces):
    return [lax.ppermute(pieces[i], "row", [(1, (1 + i) % XS)]) for i in (1, 2, 3)]


def far_z(mine, z):
    near = lax.ppermute(mine, "row", along_z([(0, 3)]))
    far = lax.ppermute(mine, "row", along_z([(0, 5)]))
    return jnp.where(z == 0, mine, near + far)


def near_z(mine, z):
    up = lax.ppermute(mine, "row", along_z([(0, 1), (3, 4), (5, 6)]))
    down = lax.ppermute(mine, "row", along_z([(0, 7), (3, 2)]))
    return jnp.where((z == 0) | (z == 3) | (z == 5), mine, up + down)


def over_x(mine):
    return lax.ppermute(mine, "row", TO_LAST), lax.ppermute(mine, "row", TO_NEXT)


def across_x(after, before):
    return lax.ppermute(after[: Q // 2], "row", TO_LAST), lax.ppermute(before[Q // 2 :], "row", TO_NEXT)


def body(panel, rhs):
    row = lax.axis_index("row")
    col = lax.axis_index("col")
    z = row // XS

    def place(root):
        return jnp.stack([row, col // 2, col % 2, (row - root) % XS])

    def after(value, *others):
        return lax.optimization_barrier((value, *others))[0]

    top, bottom = payload(place(0), panel)
    top_near = near_chips(top, lambda r, y: r > 0 or y == 0)
    bottom_near = near_chips(bottom, lambda r, y: r > 0 or y <= 1)
    top_far = far_chip(top_near[0], None, lambda r, y: r > 0 or y == 0)
    bottom_far = far_chip(None, bottom_near[1], lambda r, y: r > 0 or y <= 1)
    top = assemble(place(0), both_cores((top, *top_near, top_far)))
    bottom = assemble(place(0), both_cores((bottom, *bottom_near, bottom_far)))

    first, two, three = solve(place(0), rhs, top, bottom)
    ahead = lax.ppermute(first, "row", [(0, 1)])
    two_ahead, three_ahead = scatter_first(two, three)
    w_high, w_low, y_value = prepare(place(0), rhs, top, bottom)
    mine_one = jnp.where(row == 1, ahead[Q : 2 * Q], two_ahead + three_ahead)
    mine_one = far_z(after(jnp.where(row == 0, first[:Q], mine_one), w_high), z)

    pieces = combine(place(0), w_high, w_low, y_value, ahead)
    got = scatter_second(pieces)
    mine_one = near_z(after(mine_one, *pieces), z)
    mine_two = jnp.where(row == 1, pieces[0], got[0] + got[1] + got[2])
    beside_one = over_x(after(mine_one, got[0]))
    across_one = across_x(*beside_one)
    mine_two = far_z(mine_two, z)
    pieces_one = [after(x, mine_two) for x in (mine_one, beside_one[0], *across_one, beside_one[1])]
    updated, whole = update("update", 0, (0, 1, 2, 3), False, place(0), rhs, top, bottom, pieces_one)
    mine_two = near_z(mine_two, z)
    beside_two = [after(piece, updated) for piece in over_x(mine_two)]
    across_two = across_x(*beside_two)
    pieces_two = (mine_two, *beside_two)
    updated, whole = update("most", PARTS, (0, 1, 3), False, place(1), updated, top, bottom, pieces_two, whole)
    return tuple(update("last", PARTS, (2,), True, place(1), updated, top, bottom, across_two, whole))


def solution(mesh):
    placed = (P("row", "col"), P("row", "col"))
    return jax.shard_map(
        body,
        mesh=mesh,
        in_specs=placed,
        out_specs=(P("row", "col"), P(None, "col")),
        check_vma=False,
    )
```

time: 169 us -> 153 us (0.905)
  starting transfers between devices: 64.1 us -> 57.4 us
  local copies, waits for them, and re-layouts: 6.29 us -> 1.27 us
  waiting for transfers between devices: 70.2 us -> 66 us
    ppermute x2, waiting for transfers between devices: 2.32 us -> 15.2 us  [near_chips(): return (lax.ppermute(chunk, BOTH, pairs(-1, 0, has)), behind)]
    ppermute x19 -> x17, waiting for transfers between devices: 53.8 us -> 42.4 us  [the longest x1 14.3 us: scatter_first(): relay = lax.ppermute(two, 'row', [(0, 3)])]
    unnamed x24 -> x4, local copies, waits for them, and re-layouts: 6.18 us -> 1.23 us
    ppermute x19 -> x17, starting transfers between devices: 35.5 us -> 32.2 us  [the longest x2 8.66 us: over_x(): lax.ppermute(mine, 'row', TO_NEXT)]
    ppermute x2, waiting for transfers between devices: 3.17 us -> 0.01 us  [near_z(): down = lax.ppermute(mine, 'row', along_z([(0, 7), (3, 2)]))]
    ppermute x2, waiting for transfers between devices: 2.63 us -> 0.01 us  [near_z(): up = lax.ppermute(mine, 'row', along_z([(0, 1), (3, 4), (5, 6)]))]
    pallas_call x7 -> x9, Pallas kernels: 20.9 us -> 21.4 us  [call(): pl.pallas_call(kernel, out_shape=[(pltpu.HBM if len(shape) == 3 else jax....]
  transfers between devices with their start and end apart: 41 -> 37, of which waited for: 19 -> 10; matrix products, arithmetic and copies ran while one was open for 3% -> 2% of each run, Pallas kernels for 3% -> 9%
where the time goes in v3:
time: 153 us; the launch traced here: 152 us
  waiting for transfers between devices  66 us (43%)
  starting transfers between devices  57.4 us (38%)
  Pallas kernels  21.4 us (14%)
  other arithmetic  4.46 us (3%)
    pallas_call x9, Pallas kernels, call(): pl.pallas_call(kernel, out_shape=[(pltpu.HBM if len(shape) == 3 else jax....  21.4 us
    ppermute x2, waiting for transfers between devices, near_chips(): return (lax.ppermute(chunk, BOTH, pairs(-1, 0, has)), behind)  15.2 us
    ppermute x1, waiting for transfers between devices, scatter_first(): relay = lax.ppermute(two, 'row', [(0, 3)])  14.3 us
    ppermute x3, waiting for transfers between devices, scatter_second(): lax.ppermute(pieces[i], 'row', [(1, (1 + i) % XS)])  13.3 us
    ppermute x2, starting transfers between devices, over_x(): lax.ppermute(mine, 'row', TO_NEXT)  8.66 us
    ppermute x2, waiting for transfers between devices, near_chips(): behind = lax.ppermute(chunk, BOTH, pairs(1, 0, has))  8.43 us
    ppermute x2, starting transfers between devices, across_x(): lax.ppermute(before[Q // 2:], 'row', TO_NEXT)  6.99 us
    ppermute x2, starting transfers between devices, near_chips(): return (lax.ppermute(chunk, BOTH, pairs(-1, 0, has)), behind)  6.84 us
  transfers between devices with their start and end apart: 37, of which 10 were waited for; matrix products, arithmetic and copies ran while one was open for 2% of the time, Pallas kernels for 9%

profile of v3, /device:TPU:6, one launch (start us, length us, event | category | flops | bytes accessed | tf_op | source)
XLA Modules:
  0.0 151.9 jit_solution(11764634140925263293)
XLA Ops:
  0.7 0.1 pad_add_fusion.2
  0.7 1.2 copy-done.1
  2.0 0.6 payload.1
  2.6 4.9 %collective-permute-start.1 = (f32[512,256]{1,0:T(8,128)S(1)}, f32[512,256]{1,0:T(8,128)S(1)}, u32[]{:S(2)}, u32[]{:S(2)}) collective-permute-start(f32[512,256]{1,0:T(8,128)S(1)} %get-tuple-element.28.rest_0_), channel_id=1, source_target_pairs={{0,6},{1,7},{8,14},{9,15},{10,8},{11,9},{12,10},{13,11},{14,12},{1... | collective-permute-start | bytes 1572872 | tf_op jit(solution)/shard_map/ppermute | solution.py:106
  7.5 1.9 %collective-permute-start.3 = (f32[512,256]{1,0:T(8,128)S(1)}, f32[512,256]{1,0:T(8,128)S(1)}, u32[]{:S(2)}, u32[]{:S(2)}) collective-permute-start(f32[512,256]{1,0:T(8,128)S(1)} %get-tuple-element.28.rest_0_), channel_id=1, source_target_pairs={{0,2},{1,3},{8,10},{9,11},{10,12},{11,13},{12,14},{13,15},{14,8},{... | collective-permute-start | bytes 1572872 | tf_op jit(solution)/shard_map/ppermute | solution.py:105
  9.4 0.1 collective-permute-start
  9.5 2.5 %collective-permute-start.10 = (f32[512,256]{1,0:T(8,128)S(1)}, f32[512,256]{1,0:T(8,128)S(1)}, u32[]{:S(2)}, u32[]{:S(2)}) collective-permute-start(f32[512,256]{1,0:T(8,128)S(1)} %get-tuple-element.29.rest_0_), channel_id=1, source_target_pairs={{0,2},{1,3},{2,4},{3,5},{8,10},{9,11},{10,12},{11,13},{12,14},{13,... | collective-permute-start | bytes 1572872 | tf_op jit(solution)/shard_map/ppermute | solution.py:105
  12.0 6.6 %collective-permute-done.1.rest_2_ = f32[512,256]{1,0:T(8,128)S(1)} collective-permute-done((f32[512,256]{1,0:T(8,128)S(1)}, f32[512,256]{1,0:T(8,128)S(1)}, u32[]{:S(2)}, u32[]{:S(2)}) %collective-permute-start.1) | collective-permute-done | bytes 524320 | tf_op jit(solution)/shard_map/ppermute | solution.py:106
  18.7 5.6 %collective-permute-start.5 = (f32[512,256]{1,0:T(8,128)S(1)}, f32[512,256]{1,0:T(8,128)S(1)}, u32[]{:S(2)}, u32[]{:S(2)}) collective-permute-start(f32[512,256]{1,0:T(8,128)S(1)} %collective-permute-done.1.rest_2_), channel_id=1, source_target_pairs={{6,4},{7,5},{8,14},{9,15},{10,8},{11,9},{12,10},{13,11},{14,12},{1... | collective-permute-start | bytes 1572872 | tf_op jit(solution)/shard_map/ppermute | solution.py:111
  24.3 1.9 %collective-permute-start.8 = (f32[512,256]{1,0:T(8,128)S(1)}, f32[512,256]{1,0:T(8,128)S(1)}, u32[]{:S(2)}, u32[]{:S(2)}) collective-permute-start(f32[512,256]{1,0:T(8,128)S(1)} %get-tuple-element.29.rest_0_), channel_id=1, source_target_pairs={{0,6},{1,7},{2,0},{3,1},{8,14},{9,15},{10,8},{11,9},{12,10},{13,11... | collective-permute-start | bytes 1572872 | tf_op jit(solution)/shard_map/ppermute | solution.py:106
  26.2 0.0 collective-permute-done.3.rest_4_
  26.2 0.1 collective-permute-start.4
  26.3 0.5 collective-permute-start.2
  26.8 8.4 %collective-permute-done.10.rest_4_ = f32[512,256]{1,0:T(8,128)S(1)} collective-permute-done((f32[512,256]{1,0:T(8,128)S(1)}, f32[512,256]{1,0:T(8,128)S(1)}, u32[]{:S(2)}, u32[]{:S(2)}) %collective-permute-start.10) | collective-permute-done | bytes 524320 | tf_op jit(solution)/shard_map/ppermute | solution.py:105
  35.2 1.9 %collective-permute-start.12 = (f32[512,256]{1,0:T(8,128)S(1)}, f32[512,256]{1,0:T(8,128)S(1)}, u32[]{:S(2)}, u32[]{:S(2)}) collective-permute-start(f32[512,256]{1,0:T(8,128)S(1)} %collective-permute-done.10.rest_4_), channel_id=1, source_target_pairs={{2,4},{3,5},{4,6},{5,7},{8,10},{9,11},{10,12},{11,13},{12,14},{13,... | collective-permute-start | bytes 1572872 | tf_op jit(solution)/shard_map/ppermute | solution.py:112
  37.2 0.1 collective-permute-start.6
  37.3 8.5 %collective-permute-done.8.rest_2_ = f32[512,256]{1,0:T(8,128)S(1)} collective-permute-done((f32[512,256]{1,0:T(8,128)S(1)}, f32[512,256]{1,0:T(8,128)S(1)}, u32[]{:S(2)}, u32[]{:S(2)}) %collective-permute-start.8) | collective-permute-done | bytes 524320 | tf_op jit(solution)/shard_map/ppermute | solution.py:106
  45.8 0.5 collective-permute-start.11
  46.3 0.1 collective-permute-start.9
  46.4 4.4 %collective-permute-done.12.rest_6_ = f32[512,256]{1,0:T(8,128)S(1)} collective-permute-done((f32[512,256]{1,0:T(8,128)S(1)}, f32[512,256]{1,0:T(8,128)S(1)}, u32[]{:S(2)}, u32[]{:S(2)}) %collective-permute-start.12) | collective-permute-done | bytes 524320 | tf_op jit(solution)/shard_map/ppermute | solution.py:112
  50.8 2.6 %assemble.2.top = f32[8,512,256]{2,1,0:T(8,128)} custom-call(s32[4]{0:T(128)S(1)} %get-tuple-element.54.place, f32[512,256]{1,0:T(8,128)S(1)} %get-tuple-element.28.rest_0_, f32[512,256]{1,0:T(8,128)S(1)} %collective-permute-done.rest_1_, f32[512,256]{1,0:T(8,128)S(1)} %collective-permute-done.1.rest_2_, f32[512,256]{1,0:T(8,128)S(1)} %collective-permute-done.2.rest_3_, ...), custom_call_target="tpu_custom_call" | custom-call | flops 536870912 | bytes 8388608 | tf_op jit(solution)/shard_map/assemble/pallas_call | solution.py:37
  53.4 0.0 copy-start
  53.5 2.6 %assemble.3.bottom = f32[8,512,256]{2,1,0:T(8,128)} custom-call(s32[4]{0:T(128)S(1)} %get-tuple-element.54.place, f32[512,256]{1,0:T(8,128)S(1)} %get-tuple-element.29.rest_0_, f32[512,256]{1,0:T(8,128)S(1)} %collective-permute-done.7.rest_1_, f32[512,256]{1,0:T(8,128)S(1)} %collective-permute-done.8.rest_2_, f32[512,256]{1,0:T(8,128)S(1)} %collective-permute-done.9.rest_3_, ...), custom_call_target="tpu_custom_call" | custom-call | flops 536870912 | bytes 8388608 | tf_op jit(solution)/shard_map/assemble/pallas_call | solution.py:37
  56.1 0.6 solve.1
  56.7 0.7 collective-permute-start.14
  57.4 1.3 collective-permute-start.15
  58.7 1.3 collective-permute-start.17
  60.0 14.3 %collective-permute-done.15 = f32[256,256]{1,0:T(8,128)} collective-permute-done((f32[256,256]{1,0:T(8,128)S(1)}, f32[256,256]{1,0:T(8,128)}, u32[]{:S(2)}, u32[]{:S(2)}) %collective-permute-start.15) | collective-permute-done | bytes 262176 | tf_op jit(solution)/shard_map/ppermute | solution.py:313
  74.3 2.0 %collective-permute-start.16 = (f32[256,256]{1,0:T(8,128)}, f32[256,256]{1,0:T(8,128)}, u32[]{:S(2)}, u32[]{:S(2)}) collective-permute-start(f32[256,256]{1,0:T(8,128)} %collective-permute-done.15), channel_id=1, source_target_pairs={{24,16},{25,17},{26,18},{27,19},{28,20},{29,21},{30,22},{31,23}} | collective-permute-start | bytes 786440 | tf_op jit(solution)/shard_map/ppermute | solution.py:314
  76.3 0.8 prepare.1
  77.2 2.4 %collective-permute-done.17 = f32[256,256]{1,0:T(8,128)} collective-permute-done((f32[256,256]{1,0:T(8,128)S(1)}, f32[256,256]{1,0:T(8,128)}, u32[]{:S(2)}, u32[]{:S(2)}) %collective-permute-start.17) | collective-permute-done | bytes 262176 | tf_op jit(solution)/shard_map/ppermute | solution.py:314
  79.5 1.7 %collective-permute-done.16 = f32[256,256]{1,0:T(8,128)} collective-permute-done((f32[256,256]{1,0:T(8,128)}, f32[256,256]{1,0:T(8,128)}, u32[]{:S(2)}, u32[]{:S(2)}) %collective-permute-start.16) | collective-permute-done | bytes 262176 | tf_op jit(solution)/shard_map/ppermute | solution.py:314
  81.2 1.1 fusion
  82.3 2.0 %collective-permute-start.19 = (f32[256,256]{1,0:T(8,128)S(1)}, f32[256,256]{1,0:T(8,128)}, u32[]{:S(2)}, u32[]{:S(2)}) collective-permute-start(f32[256,256]{1,0:T(8,128)S(1)} %fusion), channel_id=1, source_target_pairs={{0,160},{8,168},{16,176},{24,184},{1,161},{9,169},{17,177},{25,185... | collective-permute-start | bytes 786440 | tf_op jit(solution)/shard_map/ppermute | solution.py:323
  84.3 2.0 %collective-permute-start.18 = (f32[256,256]{1,0:T(8,128)S(1)}, f32[256,256]{1,0:T(8,128)}, u32[]{:S(2)}, u32[]{:S(2)}) collective-permute-start(f32[256,256]{1,0:T(8,128)S(1)} %fusion), channel_id=1, source_target_pairs={{0,96},{8,104},{16,112},{24,120},{1,97},{9,105},{17,113},{25,121},... | collective-permute-start | bytes 786440 | tf_op jit(solution)/shard_map/ppermute | solution.py:322
  86.3 0.5 combine.1
  86.9 0.7 collective-permute-start.22
  87.6 1.3 collective-permute-start.23
  88.9 1.4 collective-permute-start.24
  90.3 0.0 collective-permute-done.18
  90.3 1.1 add_select_fusion.4
  91.4 1.3 collective-permute-start.21
  92.7 2.0 %collective-permute-start.20 = (f32[256,256]{1,0:T(8,128)S(1)}, f32[256,256]{1,0:T(8,128)}, u32[]{:S(2)}, u32[]{:S(2)}) collective-permute-start(f32[256,256]{1,0:T(8,128)S(1)} %add_select_fusion.4), channel_id=1, source_target_pairs={{0,32},{8,40},{16,48},{24,56},{96,128},{104,136},{112,144},{120,15... | collective-permute-start | bytes 786440 | tf_op jit(solution)/shard_map/ppermute | solution.py:328
  94.7 13.3 %collective-permute-done.23 = f32[256,256]{1,0:T(8,128)S(1)} collective-permute-done((f32[256,256]{1,0:T(8,128)S(1)}, f32[256,256]{1,0:T(8,128)S(1)}, u32[]{:S(2)}, u32[]{:S(2)}) %collective-permute-start.23) | collective-permute-done | bytes 262176 | tf_op jit(solution)/shard_map/ppermute | solution.py:318
  108.0 1.0 add_select_fusion.2
  109.0 1.3 collective-permute-start.26
  110.3 1.3 collective-permute-start.25
  111.7 1.0 add_select_fusion.3.rest_0_
  112.7 5.4 %collective-permute-start.29 = (f32[256,256]{1,0:T(8,128)S(1)}, f32[256,256]{1,0:T(8,128)S(1)}, u32[]{:S(2)}, u32[]{:S(2)}) collective-permute-start(f32[256,256]{1,0:T(8,128)S(1)} %add_select_fusion.3.rest_0_), channel_id=1, source_target_pairs={{0,8},{8,16},{16,24},{24,0},{32,40},{40,48},{48,56},{56,32},{64,72... | collective-permute-start | bytes 786440 | tf_op jit(solution)/shard_map/ppermute | solution.py:334
  118.1 0.1 add_select_fusion.1
  118.1 1.3 collective-permute-start.32
  119.5 1.3 collective-permute-start.31
  120.8 0.1 pad_add_fusion.place
  120.9 2.1 %collective-permute-done.29.rest_4_ = f32[256,256]{1,0:T(8,128)S(1)} collective-permute-done((f32[256,256]{1,0:T(8,128)S(1)}, f32[256,256]{1,0:T(8,128)S(1)}, u32[]{:S(2)}, u32[]{:S(2)}) %collective-permute-start.29) | collective-permute-done | bytes 262176 | tf_op jit(solution)/shard_map/ppermute | solution.py:334
  122.9 3.8 %collective-permute-start.30 = (f32[128,256]{1,0:T(8,128)S(1)}, f32[128,256]{1,0:T(8,128)S(1)}, u32[]{:S(2)}, u32[]{:S(2)}) collective-permute-start(f32[128,256]{1,0:T(8,128)S(1)} %slice.26), channel_id=1, source_target_pairs={{0,8},{8,16},{16,24},{24,0},{32,40},{40,48},{48,56},{56,32},{64,72... | collective-permute-start | bytes 393224 | tf_op jit(solution)/shard_map/ppermute | solution.py:338
  126.7 0.3 collective-permute-start.28
  127.1 0.1 add_select_fusion.rest_0_
  127.1 3.3 %collective-permute-start.34 = (f32[256,256]{1,0:T(8,128)S(1)}, f32[256,256]{1,0:T(8,128)S(1)}, u32[]{:S(2)}, u32[]{:S(2)}) collective-permute-start(f32[256,256]{1,0:T(8,128)S(1)} %add_select_fusion.rest_0_), channel_id=1, source_target_pairs={{0,8},{8,16},{16,24},{24,0},{32,40},{40,48},{48,56},{56,32},{64,72... | collective-permute-start | bytes 786440 | tf_op jit(solution)/shard_map/ppermute | solution.py:334
  130.4 4.2 %collective-permute-done.28.rest_2_ = f32[128,256]{1,0:T(8,128)S(1)} collective-permute-done((f32[128,256]{1,0:T(8,128)S(1)}, f32[128,256]{1,0:T(8,128)S(1)}, u32[]{:S(2)}, u32[]{:S(2)}) %collective-permute-start.28) | collective-permute-done | bytes 131104 | tf_op jit(solution)/shard_map/ppermute | solution.py:338
  134.6 5.5 %update.1 = (f32[1024,256]{1,0:T(8,128)S(1)}, f32[2048,256]{1,0:T(8,128)}) custom-call(s32[4]{0:T(128)S(1)} %get-tuple-element.54.place, f32[1024,256]{1,0:T(8,128)S(1)} %copy-done, f32[8,512,256]{2,1,0:T(8,128)} %assemble.2.top, f32[8,512,256]{2,1,0:T(8,128)} %assemble.3.bottom, f32[256,256]{1,0:T(8,128)S(1)} %add_select_fusion.3.rest_0_, ...), custom_call_target="tpu_custom_call" | custom-call | flops 16106127360 | bytes 8388608 | tf_op jit(solution)/shard_map/update/pallas_call | solution.py:37
  140.2 0.1 collective-permute-start.35
  140.3 3.2 %collective-permute-start.36 = (f32[128,256]{1,0:T(8,128)S(1)}, f32[128,256]{1,0:T(8,128)S(1)}, u32[]{:S(2)}, u32[]{:S(2)}) collective-permute-start(f32[128,256]{1,0:T(8,128)S(1)} %slice.23), channel_id=1, source_target_pairs={{0,8},{8,16},{16,24},{24,0},{32,40},{40,48},{48,56},{56,32},{64,72... | collective-permute-start | bytes 393224 | tf_op jit(solution)/shard_map/ppermute | solution.py:338
  143.5 4.3 %most.1 = (f32[1024,256]{1,0:T(8,128)S(1)}, f32[2048,256]{1,0:T(8,128)}) custom-call(s32[4]{0:T(128)S(1)} %pad_add_fusion.place, f32[1024,256]{1,0:T(8,128)S(1)} %get-tuple-element.48.target, f32[8,512,256]{2,1,0:T(8,128)} %assemble.2.top, f32[8,512,256]{2,1,0:T(8,128)} %assemble.3.bottom, ...), custom_call_target="tpu_custom_call", output_to_operand_aliasing={{1}: (7, {})} | custom-call | flops 1610612736 | bytes 8388608 | tf_op jit(solution)/shard_map/most/pallas_call | solution.py:37
  147.8 3.9 %last.1 = (f32[1024,256]{1,0:T(8,128)}, f32[2048,256]{1,0:T(8,128)}) custom-call(s32[4]{0:T(128)S(1)} %pad_add_fusion.place, f32[1024,256]{1,0:T(8,128)S(1)} %get-tuple-element.52.target, f32[8,512,256]{2,1,0:T(8,128)} %assemble.2.top, f32[8,512,256]{2,1,0:T(8,128)} %assemble.3.bottom, ...), custom_call_target="tpu_custom_call", output_to_operand_aliasing={{1}: (6, {})} | custom-call | flops 1610612736 | bytes 8388608 | tf_op jit(solution)/shard_map/last/pallas_call | solution.py:37
  (35 shorter events, 0.1 us)
Async XLA Ops:
  0.7 1.2 copy-start.1
  2.6 16.1 %collective-permute-start.1 = (f32[512,256]{1,0:T(8,128)S(1)}, f32[512,256]{1,0:T(8,128)S(1)}, u32[]{:S(2)}, u32[]{:S(2)}) collective-permute-start(f32[512,256]{1,0:T(8,128)S(1)} %get-tuple-element.28.rest_0_), channel_id=1, source_target_pairs={{0,6},{1,7},{8,14},{9,15},{10,8},{11,9},{12,10},{13,11},{14,12},{1... | collective-permute-start | bytes 1572872 | tf_op jit(solution)/shard_map/ppermute | solution.py:106
  7.5 18.7 %collective-permute-start.3 = (f32[512,256]{1,0:T(8,128)S(1)}, f32[512,256]{1,0:T(8,128)S(1)}, u32[]{:S(2)}, u32[]{:S(2)}) collective-permute-start(f32[512,256]{1,0:T(8,128)S(1)} %get-tuple-element.28.rest_0_), channel_id=1, source_target_pairs={{0,2},{1,3},{8,10},{9,11},{10,12},{11,13},{12,14},{13,15},{14,8},{... | collective-permute-start | bytes 1572872 | tf_op jit(solution)/shard_map/ppermute | solution.py:105
  9.4 16.9 %collective-permute-start = (f32[512,256]{1,0:T(8,128)S(1)}, f32[512,256]{1,0:T(8,128)S(1)}, u32[]{:S(2)}, u32[]{:S(2)}) collective-permute-start(f32[512,256]{1,0:T(8,128)S(1)} %get-tuple-element.28.rest_0_), channel_id=1, source_target_pairs={{0,1},{1,0},{2,3},{3,2},{4,5},{5,4},{6,7},{7,6},{8,9},{9,8},{10,11... | collective-permute-start | bytes 1572872 | tf_op jit(solution)/shard_map/ppermute | solution.py:101
  9.5 25.7 %collective-permute-start.10 = (f32[512,256]{1,0:T(8,128)S(1)}, f32[512,256]{1,0:T(8,128)S(1)}, u32[]{:S(2)}, u32[]{:S(2)}) collective-permute-start(f32[512,256]{1,0:T(8,128)S(1)} %get-tuple-element.29.rest_0_), channel_id=1, source_target_pairs={{0,2},{1,3},{2,4},{3,5},{8,10},{9,11},{10,12},{11,13},{12,14},{13,... | collective-permute-start | bytes 1572872 | tf_op jit(solution)/shard_map/ppermute | solution.py:105
  18.7 18.5 %collective-permute-start.5 = (f32[512,256]{1,0:T(8,128)S(1)}, f32[512,256]{1,0:T(8,128)S(1)}, u32[]{:S(2)}, u32[]{:S(2)}) collective-permute-start(f32[512,256]{1,0:T(8,128)S(1)} %collective-permute-done.1.rest_2_), channel_id=1, source_target_pairs={{6,4},{7,5},{8,14},{9,15},{10,8},{11,9},{12,10},{13,11},{14,12},{1... | collective-permute-start | bytes 1572872 | tf_op jit(solution)/shard_map/ppermute | solution.py:111
  24.3 21.5 %collective-permute-start.8 = (f32[512,256]{1,0:T(8,128)S(1)}, f32[512,256]{1,0:T(8,128)S(1)}, u32[]{:S(2)}, u32[]{:S(2)}) collective-permute-start(f32[512,256]{1,0:T(8,128)S(1)} %get-tuple-element.29.rest_0_), channel_id=1, source_target_pairs={{0,6},{1,7},{2,0},{3,1},{8,14},{9,15},{10,8},{11,9},{12,10},{13,11... | collective-permute-start | bytes 1572872 | tf_op jit(solution)/shard_map/ppermute | solution.py:106
  26.2 19.6 %collective-permute-start.4 = (f32[512,256]{1,0:T(8,128)S(1)}, f32[512,256]{1,0:T(8,128)S(1)}, u32[]{:S(2)}, u32[]{:S(2)}) collective-permute-start(f32[512,256]{1,0:T(8,128)S(1)} %collective-permute-done.3.rest_4_), channel_id=1, source_target_pairs={{0,1},{1,0},{2,3},{3,2},{4,5},{5,4},{6,7},{7,6},{8,9},{9,8},{10,11... | collective-permute-start | bytes 1572872 | tf_op jit(solution)/shard_map/ppermute | solution.py:101
  26.3 20.0 %collective-permute-start.2 = (f32[512,256]{1,0:T(8,128)S(1)}, f32[512,256]{1,0:T(8,128)S(1)}, u32[]{:S(2)}, u32[]{:S(2)}) collective-permute-start(f32[512,256]{1,0:T(8,128)S(1)} %collective-permute-done.1.rest_2_), channel_id=1, source_target_pairs={{0,1},{1,0},{2,3},{3,2},{4,5},{5,4},{6,7},{7,6},{8,9},{9,8},{10,11... | collective-permute-start | bytes 1572872 | tf_op jit(solution)/shard_map/ppermute | solution.py:101
  35.2 15.6 %collective-permute-start.12 = (f32[512,256]{1,0:T(8,128)S(1)}, f32[512,256]{1,0:T(8,128)S(1)}, u32[]{:S(2)}, u32[]{:S(2)}) collective-permute-start(f32[512,256]{1,0:T(8,128)S(1)} %collective-permute-done.10.rest_4_), channel_id=1, source_target_pairs={{2,4},{3,5},{4,6},{5,7},{8,10},{9,11},{10,12},{11,13},{12,14},{13,... | collective-permute-start | bytes 1572872 | tf_op jit(solution)/shard_map/ppermute | solution.py:112
  37.2 13.6 %collective-permute-start.6 = (f32[512,256]{1,0:T(8,128)S(1)}, f32[512,256]{1,0:T(8,128)S(1)}, u32[]{:S(2)}, u32[]{:S(2)}) collective-permute-start(f32[512,256]{1,0:T(8,128)S(1)} %collective-permute-done.5.rest_6_), channel_id=1, source_target_pairs={{0,1},{1,0},{2,3},{3,2},{4,5},{5,4},{6,7},{7,6},{8,9},{9,8},{10,11... | collective-permute-start | bytes 1572872 | tf_op jit(solution)/shard_map/ppermute | solution.py:101
  45.8 7.6 %collective-permute-start.7 = (f32[512,256]{1,0:T(8,128)S(1)}, f32[512,256]{1,0:T(8,128)S(1)}, u32[]{:S(2)}, u32[]{:S(2)}) collective-permute-start(f32[512,256]{1,0:T(8,128)S(1)} %get-tuple-element.29.rest_0_), channel_id=1, source_target_pairs={{0,1},{1,0},{2,3},{3,2},{4,5},{5,4},{6,7},{7,6},{8,9},{9,8},{10,11... | collective-permute-start | bytes 1572872 | tf_op jit(solution)/shard_map/ppermute | solution.py:101
  45.8 7.6 %collective-permute-start.11 = (f32[512,256]{1,0:T(8,128)S(1)}, f32[512,256]{1,0:T(8,128)S(1)}, u32[]{:S(2)}, u32[]{:S(2)}) collective-permute-start(f32[512,256]{1,0:T(8,128)S(1)} %collective-permute-done.10.rest_4_), channel_id=1, source_target_pairs={{0,1},{1,0},{2,3},{3,2},{4,5},{5,4},{6,7},{7,6},{8,9},{9,8},{10,11... | collective-permute-start | bytes 1572872 | tf_op jit(solution)/shard_map/ppermute | solution.py:101
  46.3 7.1 %collective-permute-start.9 = (f32[512,256]{1,0:T(8,128)S(1)}, f32[512,256]{1,0:T(8,128)S(1)}, u32[]{:S(2)}, u32[]{:S(2)}) collective-permute-start(f32[512,256]{1,0:T(8,128)S(1)} %collective-permute-done.8.rest_2_), channel_id=1, source_target_pairs={{0,1},{1,0},{2,3},{3,2},{4,5},{5,4},{6,7},{7,6},{8,9},{9,8},{10,11... | collective-permute-start | bytes 1572872 | tf_op jit(solution)/shard_map/ppermute | solution.py:101
  50.8 2.6 %collective-permute-start.13 = (f32[512,256]{1,0:T(8,128)S(1)}, f32[512,256]{1,0:T(8,128)S(1)}, u32[]{:S(2)}, u32[]{:S(2)}) collective-permute-start(f32[512,256]{1,0:T(8,128)S(1)} %collective-permute-done.12.rest_6_), channel_id=1, source_target_pairs={{0,1},{1,0},{2,3},{3,2},{4,5},{5,4},{6,7},{7,6},{8,9},{9,8},{10,11... | collective-permute-start | bytes 1572872 | tf_op jit(solution)/shard_map/ppermute | solution.py:101
  53.4 2.7 %copy-start = (f32[1024,256]{1,0:T(8,128)S(1)}, f32[1024,256]{1,0:T(8,128)}, u32[]{:S(2)}) copy-start(f32[1024,256]{1,0:T(8,128)} %target.1) | copy-start | bytes 3145732
  56.7 24.6 %collective-permute-start.14 = (f32[1024,256]{1,0:T(8,128)S(1)}, f32[1024,256]{1,0:T(8,128)S(1)}, u32[]{:S(2)}, u32[]{:S(2)}) collective-permute-start(f32[1024,256]{1,0:T(8,128)S(1)} %get-tuple-element.30), channel_id=1, source_target_pairs={{0,8},{1,9},{2,10},{3,11},{4,12},{5,13},{6,14},{7,15}} | collective-permute-start | bytes 3145736 | tf_op jit(solution)/shard_map/ppermute | solution.py:361
  57.4 16.9 %collective-permute-start.15 = (f32[256,256]{1,0:T(8,128)S(1)}, f32[256,256]{1,0:T(8,128)}, u32[]{:S(2)}, u32[]{:S(2)}) collective-permute-start(f32[256,256]{1,0:T(8,128)S(1)} %get-tuple-element.31), channel_id=1, source_target_pairs={{0,24},{1,25},{2,26},{3,27},{4,28},{5,29},{6,30},{7,31}} | collective-permute-start | bytes 786440 | tf_op jit(solution)/shard_map/ppermute | solution.py:313
  58.7 20.8 %collective-permute-start.17 = (f32[256,256]{1,0:T(8,128)S(1)}, f32[256,256]{1,0:T(8,128)}, u32[]{:S(2)}, u32[]{:S(2)}) collective-permute-start(f32[256,256]{1,0:T(8,128)S(1)} %get-tuple-element.32), channel_id=1, source_target_pairs={{0,24},{1,25},{2,26},{3,27},{4,28},{5,29},{6,30},{7,31}} | collective-permute-start | bytes 786440 | tf_op jit(solution)/shard_map/ppermute | solution.py:314
  74.3 6.9 %collective-permute-start.16 = (f32[256,256]{1,0:T(8,128)}, f32[256,256]{1,0:T(8,128)}, u32[]{:S(2)}, u32[]{:S(2)}) collective-permute-start(f32[256,256]{1,0:T(8,128)} %collective-permute-done.15), channel_id=1, source_target_pairs={{24,16},{25,17},{26,18},{27,19},{28,20},{29,21},{30,22},{31,23}} | collective-permute-start | bytes 786440 | tf_op jit(solution)/shard_map/ppermute | solution.py:314
  82.3 7.9 %collective-permute-start.19 = (f32[256,256]{1,0:T(8,128)S(1)}, f32[256,256]{1,0:T(8,128)}, u32[]{:S(2)}, u32[]{:S(2)}) collective-permute-start(f32[256,256]{1,0:T(8,128)S(1)} %fusion), channel_id=1, source_target_pairs={{0,160},{8,168},{16,176},{24,184},{1,161},{9,169},{17,177},{25,185... | collective-permute-start | bytes 786440 | tf_op jit(solution)/shard_map/ppermute | solution.py:323
  84.3 5.9 %collective-permute-start.18 = (f32[256,256]{1,0:T(8,128)S(1)}, f32[256,256]{1,0:T(8,128)}, u32[]{:S(2)}, u32[]{:S(2)}) collective-permute-start(f32[256,256]{1,0:T(8,128)S(1)} %fusion), channel_id=1, source_target_pairs={{0,96},{8,104},{16,112},{24,120},{1,97},{9,105},{17,113},{25,121},... | collective-permute-start | bytes 786440 | tf_op jit(solution)/shard_map/ppermute | solution.py:322
  86.9 7.8 %collective-permute-start.22 = (f32[256,256]{1,0:T(8,128)S(1)}, f32[256,256]{1,0:T(8,128)S(1)}, u32[]{:S(2)}, u32[]{:S(2)}) collective-permute-start(f32[256,256]{1,0:T(8,128)S(1)} %get-tuple-element.38), channel_id=1, source_target_pairs={{8,16},{9,17},{10,18},{11,19},{12,20},{13,21},{14,22},{15,23}} | collective-permute-start | bytes 786440 | tf_op jit(solution)/shard_map/ppermute | solution.py:318
  87.6 20.4 %collective-permute-start.23 = (f32[256,256]{1,0:T(8,128)S(1)}, f32[256,256]{1,0:T(8,128)S(1)}, u32[]{:S(2)}, u32[]{:S(2)}) collective-permute-start(f32[256,256]{1,0:T(8,128)S(1)} %get-tuple-element.39), channel_id=1, source_target_pairs={{8,24},{9,25},{10,26},{11,27},{12,28},{13,29},{14,30},{15,31}} | collective-permute-start | bytes 786440 | tf_op jit(solution)/shard_map/ppermute | solution.py:318
  88.9 19.1 %collective-permute-start.24 = (f32[256,256]{1,0:T(8,128)S(1)}, f32[256,256]{1,0:T(8,128)}, u32[]{:S(2)}, u32[]{:S(2)}) collective-permute-start(f32[256,256]{1,0:T(8,128)S(1)} %get-tuple-element.40), channel_id=1, source_target_pairs={{8,0},{9,1},{10,2},{11,3},{12,4},{13,5},{14,6},{15,7}} | collective-permute-start | bytes 786440 | tf_op jit(solution)/shard_map/ppermute | solution.py:318
  91.4 20.3 %collective-permute-start.21 = (f32[256,256]{1,0:T(8,128)S(1)}, f32[256,256]{1,0:T(8,128)S(1)}, u32[]{:S(2)}, u32[]{:S(2)}) collective-permute-start(f32[256,256]{1,0:T(8,128)S(1)} %add_select_fusion.4), channel_id=1, source_target_pairs={{0,224},{8,232},{16,240},{24,248},{96,64},{104,72},{112,80},{120,8... | collective-permute-start | bytes 786440 | tf_op jit(solution)/shard_map/ppermute | solution.py:329
  92.7 19.0 %collective-permute-start.20 = (f32[256,256]{1,0:T(8,128)S(1)}, f32[256,256]{1,0:T(8,128)}, u32[]{:S(2)}, u32[]{:S(2)}) collective-permute-start(f32[256,256]{1,0:T(8,128)S(1)} %add_select_fusion.4), channel_id=1, source_target_pairs={{0,32},{8,40},{16,48},{24,56},{96,128},{104,136},{112,144},{120,15... | collective-permute-start | bytes 786440 | tf_op jit(solution)/shard_map/ppermute | solution.py:328
  109.0 9.1 %collective-permute-start.26 = (f32[256,256]{1,0:T(8,128)S(1)}, f32[256,256]{1,0:T(8,128)S(1)}, u32[]{:S(2)}, u32[]{:S(2)}) collective-permute-start(f32[256,256]{1,0:T(8,128)S(1)} %add_select_fusion.2), channel_id=1, source_target_pairs={{0,160},{8,168},{16,176},{24,184},{1,161},{9,169},{17,177},{25,185... | collective-permute-start | bytes 786440 | tf_op jit(solution)/shard_map/ppermute | solution.py:323
  110.3 7.7 %collective-permute-start.25 = (f32[256,256]{1,0:T(8,128)S(1)}, f32[256,256]{1,0:T(8,128)S(1)}, u32[]{:S(2)}, u32[]{:S(2)}) collective-permute-start(f32[256,256]{1,0:T(8,128)S(1)} %add_select_fusion.2), channel_id=1, source_target_pairs={{0,96},{8,104},{16,112},{24,120},{1,97},{9,105},{17,113},{25,121},... | collective-permute-start | bytes 786440 | tf_op jit(solution)/shard_map/ppermute | solution.py:322
  112.7 10.2 %collective-permute-start.29 = (f32[256,256]{1,0:T(8,128)S(1)}, f32[256,256]{1,0:T(8,128)S(1)}, u32[]{:S(2)}, u32[]{:S(2)}) collective-permute-start(f32[256,256]{1,0:T(8,128)S(1)} %add_select_fusion.3.rest_0_), channel_id=1, source_target_pairs={{0,8},{8,16},{16,24},{24,0},{32,40},{40,48},{48,56},{56,32},{64,72... | collective-permute-start | bytes 786440 | tf_op jit(solution)/shard_map/ppermute | solution.py:334
  118.1 8.6 %collective-permute-start.27 = (f32[256,256]{1,0:T(8,128)S(1)}, f32[256,256]{1,0:T(8,128)S(1)}, u32[]{:S(2)}, u32[]{:S(2)}) collective-permute-start(f32[256,256]{1,0:T(8,128)S(1)} %add_select_fusion.3.rest_0_), channel_id=1, source_target_pairs={{8,0},{16,8},{24,16},{0,24},{40,32},{48,40},{56,48},{32,56},{72,64... | collective-permute-start | bytes 786440 | tf_op jit(solution)/shard_map/ppermute | solution.py:334
  118.1 8.9 %collective-permute-start.32 = (f32[256,256]{1,0:T(8,128)S(1)}, f32[256,256]{1,0:T(8,128)S(1)}, u32[]{:S(2)}, u32[]{:S(2)}) collective-permute-start(f32[256,256]{1,0:T(8,128)S(1)} %add_select_fusion.1), channel_id=1, source_target_pairs={{0,224},{8,232},{16,240},{24,248},{96,64},{104,72},{112,80},{120,8... | collective-permute-start | bytes 786440 | tf_op jit(solution)/shard_map/ppermute | solution.py:329
  119.5 7.6 %collective-permute-start.31 = (f32[256,256]{1,0:T(8,128)S(1)}, f32[256,256]{1,0:T(8,128)S(1)}, u32[]{:S(2)}, u32[]{:S(2)}) collective-permute-start(f32[256,256]{1,0:T(8,128)S(1)} %add_select_fusion.1), channel_id=1, source_target_pairs={{0,32},{8,40},{16,48},{24,56},{96,128},{104,136},{112,144},{120,15... | collective-permute-start | bytes 786440 | tf_op jit(solution)/shard_map/ppermute | solution.py:328
  122.9 7.5 %collective-permute-start.30 = (f32[128,256]{1,0:T(8,128)S(1)}, f32[128,256]{1,0:T(8,128)S(1)}, u32[]{:S(2)}, u32[]{:S(2)}) collective-permute-start(f32[128,256]{1,0:T(8,128)S(1)} %slice.26), channel_id=1, source_target_pairs={{0,8},{8,16},{16,24},{24,0},{32,40},{40,48},{48,56},{56,32},{64,72... | collective-permute-start | bytes 393224 | tf_op jit(solution)/shard_map/ppermute | solution.py:338
  126.7 7.9 %collective-permute-start.28 = (f32[128,256]{1,0:T(8,128)S(1)}, f32[128,256]{1,0:T(8,128)S(1)}, u32[]{:S(2)}, u32[]{:S(2)}) collective-permute-start(f32[128,256]{1,0:T(8,128)S(1)} %slice.25), channel_id=1, source_target_pairs={{8,0},{16,8},{24,16},{0,24},{40,32},{48,40},{56,48},{32,56},{72,64... | collective-permute-start | bytes 393224 | tf_op jit(solution)/shard_map/ppermute | solution.py:338
  127.1 13.0 %collective-permute-start.34 = (f32[256,256]{1,0:T(8,128)S(1)}, f32[256,256]{1,0:T(8,128)S(1)}, u32[]{:S(2)}, u32[]{:S(2)}) collective-permute-start(f32[256,256]{1,0:T(8,128)S(1)} %add_select_fusion.rest_0_), channel_id=1, source_target_pairs={{0,8},{8,16},{16,24},{24,0},{32,40},{40,48},{48,56},{56,32},{64,72... | collective-permute-start | bytes 786440 | tf_op jit(solution)/shard_map/ppermute | solution.py:334
  130.4 9.7 %collective-permute-start.33 = (f32[256,256]{1,0:T(8,128)S(1)}, f32[256,256]{1,0:T(8,128)S(1)}, u32[]{:S(2)}, u32[]{:S(2)}) collective-permute-start(f32[256,256]{1,0:T(8,128)S(1)} %add_select_fusion.rest_0_), channel_id=1, source_target_pairs={{8,0},{16,8},{24,16},{0,24},{40,32},{48,40},{56,48},{32,56},{72,64... | collective-permute-start | bytes 786440 | tf_op jit(solution)/shard_map/ppermute | solution.py:334
  140.2 7.6 %collective-permute-start.35 = (f32[128,256]{1,0:T(8,128)S(1)}, f32[128,256]{1,0:T(8,128)S(1)}, u32[]{:S(2)}, u32[]{:S(2)}) collective-permute-start(f32[128,256]{1,0:T(8,128)S(1)} %slice.22), channel_id=1, source_target_pairs={{8,0},{16,8},{24,16},{0,24},{40,32},{48,40},{56,48},{32,56},{72,64... | collective-permute-start | bytes 393224 | tf_op jit(solution)/shard_map/ppermute | solution.py:338
  140.3 7.6 %collective-permute-start.36 = (f32[128,256]{1,0:T(8,128)S(1)}, f32[128,256]{1,0:T(8,128)S(1)}, u32[]{:S(2)}, u32[]{:S(2)}) collective-permute-start(f32[128,256]{1,0:T(8,128)S(1)} %slice.23), channel_id=1, source_target_pairs={{0,8},{8,16},{16,24},{24,0},{32,40},{40,48},{48,56},{56,32},{64,72... | collective-permute-start | bytes 393224 | tf_op jit(solution)/shard_map/ppermute | solution.py:338

commit v4 on v3

--- a/solution.py
+++ b/solution.py
@@ -116,35 +116,31 @@
     return [x for value in values for x in (value, other_core(value))]
 
 
-def assemble_kernel(place, *rest):
-    arrays, (out, sem) = rest[: len(CHUNK)], rest[len(CHUNK) :]
-    blocks = jnp.where(place[ROW] == 0, PARTS, COLS)
-    for wait in (False, True):
-        for (step, same), array in zip(CHUNK, arrays):
+def place_blocks(place, arrays, chosen, out, sem):
+    def each(act):
+        for n, ((step, same), array) in enumerate(zip(CHUNK, arrays)):
             core = place[CORE] if same else 1 - place[CORE]
             block = 2 * ((place[PLACE_Y] + step) & (YS - 1)) + core
 
-            @pl.when(block < blocks)
+            @pl.when(chosen(block))
             def _():
-                copy = pltpu.make_async_copy(array, out.at[block], sem.at[block])
-                copy.wait() if wait else copy.start()
-
-
-def assemble(place, arrays):
-    in_hbm = [pl.BlockSpec(memory_space=pltpu.HBM)]
-    scratch = [pltpu.SemaphoreType.DMA((COLS,))]
-    shapes = [((COLS, HALF, Q), F32)]
-    return call(assemble_kernel, "assemble", shapes, scratch, (place, *arrays), out_specs=in_hbm)[0]
-
-
-def blocks_copies(top, bottom, base, buffer, sems):
-    copies = [
-        pltpu.make_async_copy(half.at[pl.ds(base, PARTS)], buffer.at[:, pl.ds(i * HALF, HALF)], sems.at[i])
-        for i, half in enumerate((top, bottom))
+                act(pltpu.make_async_copy(array, out(block), sem.at[n]))
+
+    each(lambda copy: copy.start())
+    return lambda: each(lambda copy: copy.wait())
+
+
+def place_panel(place, tops, bottoms, chosen, out, sem):
+    waits = [
+        place_blocks(place, arrays, chosen, lambda block, rows=pl.ds(k * HALF, HALF): out(block, rows), sem.at[k])
+        for k, arrays in enumerate((tops, bottoms))
     ]
-    for copy in copies:
-        copy.start()
-    return copies
+
+    def wait():
+        for one in waits:
+            one()
+
+    return wait
 
 
 def eliminate(triangle, targets, store):
@@ -156,13 +152,22 @@
             targets[k] = targets[k] - product(halves(triangle[i, pl.ds(k * Q, Q), :]), parts)
 
 
-def solve_kernel(place, rhs, top, bottom, whole, two, three, triangle, rhs_buf, sem, rhs_sem):
+def solve_kernel(place, rhs, *rest):
+    tops, bottoms, rest = rest[: len(CHUNK)], rest[len(CHUNK) : 2 * len(CHUNK)], rest[2 * len(CHUNK) :]
+    whole, two, three, triangle, rhs_buf, top_sem, bottom_sem, rhs_sem = rest
+
     @pl.when(place[ROW] == 0)
     def _():
         copy = pltpu.make_async_copy(rhs, rhs_buf, rhs_sem)
         copy.start()
-        for wait in blocks_copies(top, bottom, 0, triangle, sem):
-            wait.wait()
+        waits = [
+            place_blocks(place, tops, lambda block: block < 2, lambda block: triangle.at[block, pl.ds(0, HALF)], top_sem),
+            place_blocks(
+                place, bottoms, lambda block: block < PARTS, lambda block: triangle.at[block, pl.ds(HALF, HALF)], bottom_sem
+            ),
+        ]
+        for wait in waits:
+            wait()
         copy.wait()
 
         def store(i, value):
@@ -173,29 +178,35 @@
         eliminate(triangle, [rhs_buf[pl.ds(i * Q, Q), :] for i in range(PARTS)], store)
 
 
-def solve(place, rhs, top, bottom):
+def solve(place, rhs, tops, bottoms):
     scratch = [
         pltpu.VMEM((PARTS, NB, Q), F32),
         pltpu.VMEM((NB, Q), F32),
-        pltpu.SemaphoreType.DMA((2,)),
+        pltpu.SemaphoreType.DMA((COLS,)),
+        pltpu.SemaphoreType.DMA((COLS,)),
         pltpu.SemaphoreType.DMA,
     ]
     shapes = [((NB, Q), F32), ((Q, Q), F32), ((Q, Q), F32)]
-    return call(solve_kernel, "solve", shapes, scratch, (place, rhs, top, bottom))
-
-
-def prepare_kernel(place, rhs, top, bottom, w_high, w_low, y_out, triangle, targets, sem, left_sem, rhs_sem):
+    return call(solve_kernel, "solve", shapes, scratch, (place, rhs, *tops, *bottoms))
+
+
+def prepare_kernel(place, rhs, *rest):
+    tops, bottoms, rest = rest[: len(CHUNK)], rest[len(CHUNK) : 2 * len(CHUNK)], rest[2 * len(CHUNK) :]
+    w_high, w_low, y_out, triangle, left, targets, sem, left_sem, rhs_sem = rest
+
     @pl.when(place[ROW] == 1)
     def _():
-        copies = [pltpu.make_async_copy(rhs, targets.at[:, pl.ds(NB, Q)], rhs_sem)]
+        copy = pltpu.make_async_copy(rhs, targets.at[:, pl.ds(NB, Q)], rhs_sem)
+        copy.start()
+        waits = [
+            place_panel(place, tops, bottoms, lambda b: b < PARTS, lambda b, rows: left.at[b, rows], left_sem),
+            place_panel(place, tops, bottoms, lambda b: b >= PARTS, lambda b, rows: triangle.at[b - PARTS, rows], sem),
+            copy.wait,
+        ]
+        for wait in waits:
+            wait()
         for j in range(PARTS):
-            for i, half in enumerate((top, bottom)):
-                target = targets.at[pl.ds(i * HALF, HALF), pl.ds(j * Q, Q)]
-                copies.append(pltpu.make_async_copy(half.at[j], target, left_sem.at[2 * j + i]))
-        for copy in copies:
-            copy.start()
-        for copy in (*blocks_copies(top, bottom, PARTS, triangle, sem), *copies):
-            copy.wait()
+            targets[:, j * Q : (j + 1) * Q] = left[j]
         for i in range(PARTS):
             rows = pl.ds(i * Q, Q)
             value = product(halves(triangle[i, rows, :]), halves(targets[rows, :]))
@@ -207,16 +218,17 @@
                 targets[below, :] -= product(halves(triangle[i, below, :]), parts)
 
 
-def prepare(place, rhs, top, bottom):
+def prepare(place, rhs, tops, bottoms):
     scratch = [
         pltpu.VMEM((PARTS, NB, Q), F32),
+        pltpu.VMEM((PARTS, NB, Q), F32),
         pltpu.VMEM((NB, NB + Q), F32),
-        pltpu.SemaphoreType.DMA((2,)),
-        pltpu.SemaphoreType.DMA((2 * PARTS,)),
+        pltpu.SemaphoreType.DMA((2, COLS)),
+        pltpu.SemaphoreType.DMA((2, COLS)),
         pltpu.SemaphoreType.DMA,
     ]
     shapes = [((NB, NB), BF16)] * 2 + [((NB, Q), F32)]
-    return call(prepare_kernel, "prepare", shapes, scratch, (place, rhs, top, bottom), vmem=32)
+    return call(prepare_kernel, "prepare", shapes, scratch, (place, rhs, *tops, *bottoms), vmem=32)
 
 
 def combine_kernel(place, w_high, w_low, y_ref, first, *out):
@@ -237,8 +249,9 @@
 PIECES = ((0, Q), (Q, Q), (2 * Q, Q // 2), (2 * Q + Q // 2, Q // 2), (3 * Q, Q))
 
 
-def update_kernel(base, slots, last, place, target, top, bottom, *rest):
+def update_kernel(base, slots, last, place, target, *rest):
     used = [n for n, (at, _) in enumerate(PIECES) if at // Q in slots]
+    tops, bottoms, rest = rest[: len(CHUNK)], rest[len(CHUNK) : 2 * len(CHUNK)], rest[2 * len(CHUNK) :]
     pieces, rest = rest[: len(used)], rest[len(used) + int(base + len(slots) > PARTS) :]
     out, whole, blocks, target_buf, solved_buf, sem, target_sem, solved_sem, whole_sem = rest
     copies, kept = [], []
@@ -249,12 +262,21 @@
         start = pl.multiple_of(((at + place[TURN] * Q) & (NB - 1)) + base * Q, Q // 2)
         kept.append(pltpu.make_async_copy(solved_buf.at[here], whole.at[pl.ds(start, length)], whole_sem.at[i]))
     copies.append(pltpu.make_async_copy(target, target_buf, target_sem))
-    for i, slot in enumerate(slots):
-        block = base + ((slot + place[TURN]) & (PARTS - 1))
-        for k, half in enumerate((top, bottom)):
-            copies.append(
-                pltpu.make_async_copy(half.at[block], blocks.at[i, pl.ds(k * HALF, HALF)], sem.at[2 * i + k])
-            )
+
+    def slot_of(block):
+        return (block - place[TURN]) & (PARTS - 1)
+
+    def chosen(block):
+        here = (block >= base) & (block < base + PARTS)
+        for slot in set(range(PARTS)) - set(slots):
+            here &= slot_of(block) != slot
+        return here
+
+    def at_slot(block, rows):
+        slot = slot_of(block)
+        return blocks.at[jnp.where(slot > slots[-1], 0, sum(jnp.where(slot > other, 1, 0) for other in slots)), rows]
+
+    wait_panel = place_panel(place, tops, bottoms, chosen, at_slot, sem)
     for copy in copies:
         copy.start()
     for copy in copies[: len(used)]:
@@ -264,6 +286,7 @@
     solved = [halves(solved_buf[pl.ds(i * Q, Q), :]) for i in range(len(slots))]
     for copy in copies[len(used) :]:
         copy.wait()
+    wait_panel()
     for r in range(PARTS):
         rows = pl.ds(r * Q, Q)
         result = target_buf[rows, :]
@@ -274,17 +297,18 @@
         copy.wait()
 
 
-def update(name, base, slots, last, place, target, top, bottom, pieces, *before):
+def update(name, base, slots, last, place, target, tops, bottoms, pieces, *before):
     scratch = [
         pltpu.VMEM((len(slots), NB, Q), F32),
         pltpu.VMEM((NB, Q), F32),
         pltpu.VMEM((len(slots) * Q, Q), F32),
-        pltpu.SemaphoreType.DMA((2 * len(slots),)),
+        pltpu.SemaphoreType.DMA((2, COLS)),
         pltpu.SemaphoreType.DMA,
         pltpu.SemaphoreType.DMA((len(pieces),)),
         pltpu.SemaphoreType.DMA((len(pieces),)),
     ]
-    operands = (place, target, top, bottom, *pieces, *before)
+    tops, bottoms = ([pltpu.with_memory_space_constraint(x, pltpu.HBM) for x in half] for half in (tops, bottoms))
+    operands = (place, target, *tops, *bottoms, *pieces, *before)
     return call(
         functools.partial(update_kernel, base, slots, last),
         name,
@@ -354,13 +378,13 @@
     bottom_near = near_chips(bottom, lambda r, y: r > 0 or y <= 1)
     top_far = far_chip(top_near[0], None, lambda r, y: r > 0 or y == 0)
     bottom_far = far_chip(None, bottom_near[1], lambda r, y: r > 0 or y <= 1)
-    top = assemble(place(0), both_cores((top, *top_near, top_far)))
-    bottom = assemble(place(0), both_cores((bottom, *bottom_near, bottom_far)))
-
-    first, two, three = solve(place(0), rhs, top, bottom)
+    tops = both_cores((top, *top_near, top_far))
+    bottoms = both_cores((bottom, *bottom_near, bottom_far))
+
+    first, two, three = solve(place(0), rhs, tops, bottoms)
     ahead = lax.ppermute(first, "row", [(0, 1)])
     two_ahead, three_ahead = scatter_first(two, three)
-    w_high, w_low, y_value = prepare(place(0), rhs, top, bottom)
+    w_high, w_low, y_value = prepare(place(0), rhs, tops, bottoms)
     mine_one = jnp.where(row == 1, ahead[Q : 2 * Q], two_ahead + three_ahead)
     mine_one = far_z(after(jnp.where(row == 0, first[:Q], mine_one), w_high), z)
 
@@ -372,13 +396,13 @@
     across_one = across_x(*beside_one)
     mine_two = far_z(mine_two, z)
     pieces_one = [after(x, mine_two) for x in (mine_one, beside_one[0], *across_one, beside_one[1])]
-    updated, whole = update("update", 0, (0, 1, 2, 3), False, place(0), rhs, top, bottom, pieces_one)
+    updated, whole = update("update", 0, (0, 1, 2, 3), False, place(0), rhs, tops, bottoms, pieces_one)
     mine_two = near_z(mine_two, z)
     beside_two = [after(piece, updated) for piece in over_x(mine_two)]
     across_two = across_x(*beside_two)
     pieces_two = (mine_two, *beside_two)
-    updated, whole = update("most", PARTS, (0, 1, 3), False, place(1), updated, top, bottom, pieces_two, whole)
-    return tuple(update("last", PARTS, (2,), True, place(1), updated, top, bottom, across_two, whole))
+    updated, whole = update("most", PARTS, (0, 1, 3), False, place(1), updated, tops, bottoms, pieces_two, whole)
+    return tuple(update("last", PARTS, (2,), True, place(1), updated, tops, bottoms, across_two, whole))
 
 
 def solution(mesh):

time: 153 us -> 143 us (0.935)
  waiting for transfers between devices: 66 us -> 51.5 us
  local copies, waits for them, and re-layouts: 1.27 us -> 13 us
  Pallas kernels: 21.4 us -> 17.6 us
  other arithmetic: 4.46 us -> 1.69 us
  starting transfers between devices: 57.4 us -> 55.6 us
    unnamed x4 -> x60, local copies, waits for them, and re-layouts: 1.23 us -> 13 us
    ppermute x2, waiting for transfers between devices: 15.2 us -> 3.52 us  [near_chips(): return (lax.ppermute(chunk, BOTH, pairs(-1, 0, has)), behind)]
    ppermute x1, waiting for transfers between devices: 0.01 us -> 9.14 us  [far_chip(): return lax.ppermute(ahead, BOTH, pairs(-1, 1, has))]
    ppermute x3, waiting for transfers between devices: 13.3 us -> 7.41 us  [scatter_second(): lax.ppermute(pieces[i], 'row', [(1, (1 + i) % XS)])]
    pallas_call x9 -> x7, Pallas kernels: 21.4 us -> 17.6 us  [call(): pl.pallas_call(kernel, out_shape=[(pltpu.HBM if len(shape) == 3 else jax....]
    ppermute x1, waiting for transfers between devices: 2.37 us -> 0.01 us  [scatter_first(): lax.ppermute(three, 'row', [(0, 3)])]
    ppermute x8, waiting for transfers between devices: 0.02 us -> 1.85 us  [other_core(): return lax.ppermute(value, 'col', [(c, c ^ 1) for c in range(COLS)])]
    ppermute x2, waiting for transfers between devices: 8.43 us -> 6.71 us  [near_chips(): behind = lax.ppermute(chunk, BOTH, pairs(1, 0, has))]
  transfers between devices with their start and end apart: 37 -> 37, of which waited for: 10 -> 13; matrix products, arithmetic and copies ran while one was open for 2% -> 0% of each run, Pallas kernels for 9% -> 8%
where the time goes in v4:
time: 143 us; the launch traced here: 141 us
  starting transfers between devices  55.6 us (39%)
  waiting for transfers between devices  51.5 us (36%)
  Pallas kernels  17.6 us (12%)
  local copies, waits for them, and re-layouts  13 us (9%)
  other arithmetic  1.69 us (1%)
  between operations  1.52 us (1%)
    pallas_call x7, Pallas kernels, call(): pl.pallas_call(kernel, out_shape=[(pltpu.HBM if len(shape) == 3 else jax....  17.6 us
    ppermute x1, waiting for transfers between devices, scatter_first(): relay = lax.ppermute(two, 'row', [(0, 3)])  14.6 us
    unnamed x60, local copies, waits for them, and re-layouts  13 us
    ppermute x1, waiting for transfers between devices, far_chip(): return lax.ppermute(ahead, BOTH, pairs(-1, 1, has))  9.14 us
    ppermute x2, starting transfers between devices, near_chips(): return (lax.ppermute(chunk, BOTH, pairs(-1, 0, has)), behind)  8.35 us
    ppermute x3, waiting for transfers between devices, scatter_second(): lax.ppermute(pieces[i], 'row', [(1, (1 + i) % XS)])  7.41 us
    ppermute x2, starting transfers between devices, over_x(): lax.ppermute(mine, 'row', TO_NEXT)  7.16 us
    ppermute x2, starting transfers between devices, across_x(): lax.ppermute(before[Q // 2:], 'row', TO_NEXT)  6.99 us
  transfers between devices with their start and end apart: 37, of which 13 were waited for; matrix products, arithmetic and copies ran while one was open for 0% of the time, Pallas kernels for 8%

profile of v4, /device:TPU:6, one launch (start us, length us, event | category | flops | bytes accessed | tf_op | source)
XLA Modules:
  0.0 140.9 jit_solution(9642809586882248252)
XLA Ops:
  0.7 0.1 pad_add_fusion.2
  0.8 1.3 copy-done.29
  2.0 0.6 payload.1
  2.7 3.5 %collective-permute-start.3 = (f32[512,256]{1,0:T(8,128)S(1)}, f32[512,256]{1,0:T(8,128)S(1)}, u32[]{:S(2)}, u32[]{:S(2)}) collective-permute-start(f32[512,256]{1,0:T(8,128)S(1)} %get-tuple-element.28.rest_0_), channel_id=1, source_target_pairs={{0,2},{1,3},{8,10},{9,11},{10,12},{11,13},{12,14},{13,15},{14,8},{... | collective-permute-start | bytes 1572872 | tf_op jit(solution)/shard_map/ppermute | solution.py:105
  6.2 3.6 %collective-permute-start.1 = (f32[512,256]{1,0:T(8,128)S(1)}, f32[512,256]{1,0:T(8,128)S(1)}, u32[]{:S(2)}, u32[]{:S(2)}) collective-permute-start(f32[512,256]{1,0:T(8,128)S(1)} %get-tuple-element.28.rest_0_), channel_id=1, source_target_pairs={{0,6},{1,7},{8,14},{9,15},{10,8},{11,9},{12,10},{13,11},{14,12},{1... | collective-permute-start | bytes 1572872 | tf_op jit(solution)/shard_map/ppermute | solution.py:106
  9.8 0.1 collective-permute-start
  9.9 2.3 %collective-permute-start.10 = (f32[512,256]{1,0:T(8,128)S(1)}, f32[512,256]{1,0:T(8,128)S(1)}, u32[]{:S(2)}, u32[]{:S(2)}) collective-permute-start(f32[512,256]{1,0:T(8,128)S(1)} %get-tuple-element.29.rest_8_), channel_id=1, source_target_pairs={{0,2},{1,3},{2,4},{3,5},{8,10},{9,11},{10,12},{11,13},{12,14},{13,... | collective-permute-start | bytes 1572872 | tf_op jit(solution)/shard_map/ppermute | solution.py:105
  12.1 4.8 %collective-permute-start.8 = (f32[512,256]{1,0:T(8,128)S(1)}, f32[512,256]{1,0:T(8,128)S(1)}, u32[]{:S(2)}, u32[]{:S(2)}) collective-permute-start(f32[512,256]{1,0:T(8,128)S(1)} %get-tuple-element.29.rest_8_), channel_id=1, source_target_pairs={{0,6},{1,7},{2,0},{3,1},{8,14},{9,15},{10,8},{11,9},{12,10},{13,11... | collective-permute-start | bytes 1572872 | tf_op jit(solution)/shard_map/ppermute | solution.py:106
  16.9 3.7 %collective-permute-done.3.rest_4_ = f32[512,256]{1,0:T(8,128)S(1)} collective-permute-done((f32[512,256]{1,0:T(8,128)S(1)}, f32[512,256]{1,0:T(8,128)S(1)}, u32[]{:S(2)}, u32[]{:S(2)}) %collective-permute-start.3) | collective-permute-done | bytes 524320 | tf_op jit(solution)/shard_map/ppermute | solution.py:105
  20.6 2.3 %collective-permute-done.1.rest_2_ = f32[512,256]{1,0:T(8,128)S(1)} collective-permute-done((f32[512,256]{1,0:T(8,128)S(1)}, f32[512,256]{1,0:T(8,128)S(1)}, u32[]{:S(2)}, u32[]{:S(2)}) %collective-permute-start.1) | collective-permute-done | bytes 524320 | tf_op jit(solution)/shard_map/ppermute | solution.py:106
  22.9 4.8 %collective-permute-start.5 = (f32[512,256]{1,0:T(8,128)S(1)}, f32[512,256]{1,0:T(8,128)S(1)}, u32[]{:S(2)}, u32[]{:S(2)}) collective-permute-start(f32[512,256]{1,0:T(8,128)S(1)} %collective-permute-done.1.rest_2_), channel_id=1, source_target_pairs={{6,4},{7,5},{8,14},{9,15},{10,8},{11,9},{12,10},{13,11},{14,12},{1... | collective-permute-start | bytes 1572872 | tf_op jit(solution)/shard_map/ppermute | solution.py:111
  27.7 3.0 %collective-permute-done.10.rest_12_ = f32[512,256]{1,0:T(8,128)S(1)} collective-permute-done((f32[512,256]{1,0:T(8,128)S(1)}, f32[512,256]{1,0:T(8,128)S(1)}, u32[]{:S(2)}, u32[]{:S(2)}) %collective-permute-start.10) | collective-permute-done | bytes 524320 | tf_op jit(solution)/shard_map/ppermute | solution.py:105
  30.8 2.2 %collective-permute-start.12 = (f32[512,256]{1,0:T(8,128)S(1)}, f32[512,256]{1,0:T(8,128)S(1)}, u32[]{:S(2)}, u32[]{:S(2)}) collective-permute-start(f32[512,256]{1,0:T(8,128)S(1)} %collective-permute-done.10.rest_12_), channel_id=1, source_target_pairs={{2,4},{3,5},{4,6},{5,7},{8,10},{9,11},{10,12},{11,13},{12,14},{13,... | collective-permute-start | bytes 1572872 | tf_op jit(solution)/shard_map/ppermute | solution.py:112
  33.0 1.2 collective-permute-done.8.rest_10_
  34.2 0.5 collective-permute-start.11
  34.7 0.1 collective-permute-start.9
  34.8 9.1 %collective-permute-done.5.rest_6_ = f32[512,256]{1,0:T(8,128)S(1)} collective-permute-done((f32[512,256]{1,0:T(8,128)S(1)}, f32[512,256]{1,0:T(8,128)S(1)}, u32[]{:S(2)}, u32[]{:S(2)}) %collective-permute-start.5) | collective-permute-done | bytes 524320 | tf_op jit(solution)/shard_map/ppermute | solution.py:111
  43.9 2.8 %collective-permute-done.12.rest_14_ = f32[512,256]{1,0:T(8,128)S(1)} collective-permute-done((f32[512,256]{1,0:T(8,128)S(1)}, f32[512,256]{1,0:T(8,128)S(1)}, u32[]{:S(2)}, u32[]{:S(2)}) %collective-permute-start.12) | collective-permute-done | bytes 524320 | tf_op jit(solution)/shard_map/ppermute | solution.py:112
  46.8 1.8 %collective-permute-done.13.rest_15_ = f32[512,256]{1,0:T(8,128)S(1)} collective-permute-done((f32[512,256]{1,0:T(8,128)S(1)}, f32[512,256]{1,0:T(8,128)S(1)}, u32[]{:S(2)}, u32[]{:S(2)}) %collective-permute-start.13) | collective-permute-done | bytes 524320 | tf_op jit(solution)/shard_map/ppermute | solution.py:101
  48.6 1.7 %solve.1 = (f32[1024,256]{1,0:T(8,128)}, f32[256,256]{1,0:T(8,128)S(1)}, f32[256,256]{1,0:T(8,128)S(1)}) custom-call(s32[4]{0:T(128)S(1)} %get-tuple-element.54.place, f32[1024,256]{1,0:T(8,128)S(1)} %copy-done.26, f32[512,256]{1,0:T(8,128)S(1)} %get-tuple-element.28.rest_0_, f32[512,256]{1,0:T(8,128)S(1)} %collective-permute-done.rest_1_, ...), custom_call_target="tpu_custom_call" | custom-call | flops 536870912 | bytes 8388608 | tf_op jit(solution)/shard_map/solve/pallas_call | solution.py:37
  50.4 1.7 %collective-permute-start.14 = (f32[1024,256]{1,0:T(8,128)}, f32[1024,256]{1,0:T(8,128)}, u32[]{:S(2)}, u32[]{:S(2)}) collective-permute-start(f32[1024,256]{1,0:T(8,128)} %get-tuple-element.30), channel_id=1, source_target_pairs={{0,8},{1,9},{2,10},{3,11},{4,12},{5,13},{6,14},{7,15}} | collective-permute-start | bytes 3145736 | tf_op jit(solution)/shard_map/ppermute | solution.py:385
  52.1 1.3 collective-permute-start.15
  53.4 1.3 collective-permute-start.17
  54.7 14.6 %collective-permute-done.15 = f32[256,256]{1,0:T(8,128)} collective-permute-done((f32[256,256]{1,0:T(8,128)S(1)}, f32[256,256]{1,0:T(8,128)}, u32[]{:S(2)}, u32[]{:S(2)}) %collective-permute-start.15) | collective-permute-done | bytes 262176 | tf_op jit(solution)/shard_map/ppermute | solution.py:337
  69.3 2.0 %collective-permute-start.16 = (f32[256,256]{1,0:T(8,128)}, f32[256,256]{1,0:T(8,128)}, u32[]{:S(2)}, u32[]{:S(2)}) collective-permute-start(f32[256,256]{1,0:T(8,128)} %collective-permute-done.15), channel_id=1, source_target_pairs={{24,16},{25,17},{26,18},{27,19},{28,20},{29,21},{30,22},{31,23}} | collective-permute-start | bytes 786440 | tf_op jit(solution)/shard_map/ppermute | solution.py:338
  71.4 1.0 copy-done.7
  72.4 1.0 copy-done.9
  73.4 1.0 copy-done.11
  74.5 1.0 copy-done.13
  75.5 1.0 copy-done.15
  76.6 1.0 copy-done.17
  77.6 1.0 copy-done.19
  78.6 1.0 copy-done.21
  79.7 1.0 copy-done.23
  80.7 1.0 copy-done.25
  81.8 1.2 copy-done.27
  83.0 1.1 prepare.1
  84.1 1.3 fusion
  85.4 1.3 collective-permute-start.19
  86.7 1.3 collective-permute-start.18
  88.0 1.2 combine.1
  89.2 0.7 collective-permute-start.22
  89.9 1.3 collective-permute-start.23
  91.2 0.7 collective-permute-start.24
  91.9 0.5 collective-permute-done.18
  92.5 1.3 collective-permute-start.21
  93.8 1.3 collective-permute-start.20
  95.2 7.4 %collective-permute-done.23 = f32[256,256]{1,0:T(8,128)S(1)} collective-permute-done((f32[256,256]{1,0:T(8,128)S(1)}, f32[256,256]{1,0:T(8,128)S(1)}, u32[]{:S(2)}, u32[]{:S(2)}) %collective-permute-start.23) | collective-permute-done | bytes 262176 | tf_op jit(solution)/shard_map/ppermute | solution.py:342
  102.7 1.4 %collective-permute-start.26 = (f32[256,256]{1,0:T(8,128)S(1)}, f32[256,256]{1,0:T(8,128)S(1)}, u32[]{:S(2)}, u32[]{:S(2)}) collective-permute-start(f32[256,256]{1,0:T(8,128)S(1)} %add_select_fusion.2), channel_id=1, source_target_pairs={{0,160},{8,168},{16,176},{24,184},{1,161},{9,169},{17,177},{25,185... | collective-permute-start | bytes 786440 | tf_op jit(solution)/shard_map/ppermute | solution.py:347
  104.1 1.3 collective-permute-start.25
  105.5 3.9 %collective-permute-start.29 = (f32[256,256]{1,0:T(8,128)S(1)}, f32[256,256]{1,0:T(8,128)S(1)}, u32[]{:S(2)}, u32[]{:S(2)}) collective-permute-start(f32[256,256]{1,0:T(8,128)S(1)} %add_select_fusion.3.rest_16_), channel_id=1, source_target_pairs={{0,8},{8,16},{16,24},{24,0},{32,40},{40,48},{48,56},{56,32},{64,72... | collective-permute-start | bytes 786440 | tf_op jit(solution)/shard_map/ppermute | solution.py:358
  109.5 1.3 collective-permute-start.32
  110.8 1.3 collective-permute-start.31
  112.2 1.1 collective-permute-done.29.rest_20_
  113.3 3.8 %collective-permute-start.30 = (f32[128,256]{1,0:T(8,128)S(1)}, f32[128,256]{1,0:T(8,128)S(1)}, u32[]{:S(2)}, u32[]{:S(2)}) collective-permute-start(f32[128,256]{1,0:T(8,128)S(1)} %slice.26), channel_id=1, source_target_pairs={{0,8},{8,16},{16,24},{24,0},{32,40},{40,48},{48,56},{56,32},{64,72... | collective-permute-start | bytes 393224 | tf_op jit(solution)/shard_map/ppermute | solution.py:362
  117.1 0.1 collective-permute-start.28
  117.3 3.3 %collective-permute-start.34 = (f32[256,256]{1,0:T(8,128)S(1)}, f32[256,256]{1,0:T(8,128)S(1)}, u32[]{:S(2)}, u32[]{:S(2)}) collective-permute-start(f32[256,256]{1,0:T(8,128)S(1)} %add_select_fusion.rest_16_), channel_id=1, source_target_pairs={{0,8},{8,16},{16,24},{24,0},{32,40},{40,48},{48,56},{56,32},{64,72... | collective-permute-start | bytes 786440 | tf_op jit(solution)/shard_map/ppermute | solution.py:358
  120.5 0.4 collective-permute-done.30.rest_19_
  120.9 3.4 %collective-permute-done.28.rest_18_ = f32[128,256]{1,0:T(8,128)S(1)} collective-permute-done((f32[128,256]{1,0:T(8,128)S(1)}, f32[128,256]{1,0:T(8,128)S(1)}, u32[]{:S(2)}, u32[]{:S(2)}) %collective-permute-start.28) | collective-permute-done | bytes 131104 | tf_op jit(solution)/shard_map/ppermute | solution.py:362
  124.3 5.1 %update.1 = (f32[1024,256]{1,0:T(8,128)S(1)}, f32[2048,256]{1,0:T(8,128)}) custom-call(s32[4]{0:T(128)S(1)} %get-tuple-element.54.place, f32[1024,256]{1,0:T(8,128)S(1)} %copy-done.28, f32[512,256]{1,0:T(8,128)} %copy-done, f32[512,256]{1,0:T(8,128)} %copy-done.4, f32[512,256]{1,0:T(8,128)} %copy-done.3, f32[512,256]{1,0:T(8,128)} %copy-done.16, ...), custom_call_target="tpu_custom_call" | custom-call | flops 16106127360 | bytes 8388608 | tf_op jit(solution)/shard_map/update/pallas_call | solution.py:37
  129.5 0.1 collective-permute-start.35
  129.6 3.2 %collective-permute-start.36 = (f32[128,256]{1,0:T(8,128)S(1)}, f32[128,256]{1,0:T(8,128)S(1)}, u32[]{:S(2)}, u32[]{:S(2)}) collective-permute-start(f32[128,256]{1,0:T(8,128)S(1)} %slice.23), channel_id=1, source_target_pairs={{0,8},{8,16},{16,24},{24,0},{32,40},{40,48},{48,56},{56,32},{64,72... | collective-permute-start | bytes 393224 | tf_op jit(solution)/shard_map/ppermute | solution.py:362
  132.8 4.3 %most.1 = (f32[1024,256]{1,0:T(8,128)S(1)}, f32[2048,256]{1,0:T(8,128)}) custom-call(s32[4]{0:T(128)S(1)} %pad_add_fusion.place, f32[1024,256]{1,0:T(8,128)S(1)} %get-tuple-element.48.target, f32[512,256]{1,0:T(8,128)} %copy-done, f32[512,256]{1,0:T(8,128)} %copy-done.4, f32[512,256]{1,0:T(8,128)} %copy-done.3, ...), custom_call_target="tpu_custom_call", output_to_operand_aliasing={{1}: (21, {})} | custom-call | flops 1610612736 | bytes 8388608 | tf_op jit(solution)/shard_map/most/pallas_call | solution.py:37
  137.2 3.6 %last.1 = (f32[1024,256]{1,0:T(8,128)}, f32[2048,256]{1,0:T(8,128)}) custom-call(s32[4]{0:T(128)S(1)} %pad_add_fusion.place, f32[1024,256]{1,0:T(8,128)S(1)} %get-tuple-element.52.target, f32[512,256]{1,0:T(8,128)} %copy-done, f32[512,256]{1,0:T(8,128)} %copy-done.4, f32[512,256]{1,0:T(8,128)} %copy-done.3, ...), custom_call_target="tpu_custom_call", output_to_operand_aliasing={{1}: (20, {})} | custom-call | flops 1610612736 | bytes 8388608 | tf_op jit(solution)/shard_map/last/pallas_call | solution.py:37
  (89 shorter events, 0.6 us)
Async XLA Ops:
  0.7 48.0 %copy-start.26 = (f32[1024,256]{1,0:T(8,128)S(1)}, f32[1024,256]{1,0:T(8,128)}, u32[]{:S(2)}) copy-start(f32[1024,256]{1,0:T(8,128)} %target.1) | copy-start | bytes 3145732
  0.7 1.3 copy-start.29
  2.7 68.7 %copy-start = (f32[512,256]{1,0:T(8,128)}, f32[512,256]{1,0:T(8,128)S(1)}, u32[]{:S(2)}) copy-start(f32[512,256]{1,0:T(8,128)S(1)} %get-tuple-element.28.rest_0_) | copy-start | bytes 1572868
  2.7 68.6 %copy-start.1 = (f32[512,256]{1,0:T(8,128)}, f32[512,256]{1,0:T(8,128)S(1)}, u32[]{:S(2)}) copy-start(f32[512,256]{1,0:T(8,128)S(1)} %get-tuple-element.29.rest_8_) | copy-start | bytes 1572868
  2.7 17.9 %collective-permute-start.3 = (f32[512,256]{1,0:T(8,128)S(1)}, f32[512,256]{1,0:T(8,128)S(1)}, u32[]{:S(2)}, u32[]{:S(2)}) collective-permute-start(f32[512,256]{1,0:T(8,128)S(1)} %get-tuple-element.28.rest_0_), channel_id=1, source_target_pairs={{0,2},{1,3},{8,10},{9,11},{10,12},{11,13},{12,14},{13,15},{14,8},{... | collective-permute-start | bytes 1572872 | tf_op jit(solution)/shard_map/ppermute | solution.py:105
  6.2 16.7 %collective-permute-start.1 = (f32[512,256]{1,0:T(8,128)S(1)}, f32[512,256]{1,0:T(8,128)S(1)}, u32[]{:S(2)}, u32[]{:S(2)}) collective-permute-start(f32[512,256]{1,0:T(8,128)S(1)} %get-tuple-element.28.rest_0_), channel_id=1, source_target_pairs={{0,6},{1,7},{8,14},{9,15},{10,8},{11,9},{12,10},{13,11},{14,12},{1... | collective-permute-start | bytes 1572872 | tf_op jit(solution)/shard_map/ppermute | solution.py:106
  9.8 13.2 %collective-permute-start = (f32[512,256]{1,0:T(8,128)S(1)}, f32[512,256]{1,0:T(8,128)S(1)}, u32[]{:S(2)}, u32[]{:S(2)}) collective-permute-start(f32[512,256]{1,0:T(8,128)S(1)} %get-tuple-element.28.rest_0_), channel_id=1, source_target_pairs={{0,1},{1,0},{2,3},{3,2},{4,5},{5,4},{6,7},{7,6},{8,9},{9,8},{10,11... | collective-permute-start | bytes 1572872 | tf_op jit(solution)/shard_map/ppermute | solution.py:101
  9.9 20.9 %collective-permute-start.10 = (f32[512,256]{1,0:T(8,128)S(1)}, f32[512,256]{1,0:T(8,128)S(1)}, u32[]{:S(2)}, u32[]{:S(2)}) collective-permute-start(f32[512,256]{1,0:T(8,128)S(1)} %get-tuple-element.29.rest_8_), channel_id=1, source_target_pairs={{0,2},{1,3},{2,4},{3,5},{8,10},{9,11},{10,12},{11,13},{12,14},{13,... | collective-permute-start | bytes 1572872 | tf_op jit(solution)/shard_map/ppermute | solution.py:105
  12.1 22.0 %collective-permute-start.8 = (f32[512,256]{1,0:T(8,128)S(1)}, f32[512,256]{1,0:T(8,128)S(1)}, u32[]{:S(2)}, u32[]{:S(2)}) collective-permute-start(f32[512,256]{1,0:T(8,128)S(1)} %get-tuple-element.29.rest_8_), channel_id=1, source_target_pairs={{0,6},{1,7},{2,0},{3,1},{8,14},{9,15},{10,8},{11,9},{12,10},{13,11... | collective-permute-start | bytes 1572872 | tf_op jit(solution)/shard_map/ppermute | solution.py:106
  20.6 50.7 %copy-start.2 = (f32[512,256]{1,0:T(8,128)}, f32[512,256]{1,0:T(8,128)S(1)}, u32[]{:S(2)}) copy-start(f32[512,256]{1,0:T(8,128)S(1)} %collective-permute-done.3.rest_4_) | copy-start | bytes 1572868
  20.6 13.6 %collective-permute-start.7 = (f32[512,256]{1,0:T(8,128)S(1)}, f32[512,256]{1,0:T(8,128)S(1)}, u32[]{:S(2)}, u32[]{:S(2)}) collective-permute-start(f32[512,256]{1,0:T(8,128)S(1)} %get-tuple-element.29.rest_8_), channel_id=1, source_target_pairs={{0,1},{1,0},{2,3},{3,2},{4,5},{5,4},{6,7},{7,6},{8,9},{9,8},{10,11... | collective-permute-start | bytes 1572872 | tf_op jit(solution)/shard_map/ppermute | solution.py:101
  22.9 48.4 %copy-start.3 = (f32[512,256]{1,0:T(8,128)}, f32[512,256]{1,0:T(8,128)S(1)}, u32[]{:S(2)}) copy-start(f32[512,256]{1,0:T(8,128)S(1)} %collective-permute-done.1.rest_2_) | copy-start | bytes 1572868
  22.9 11.8 %collective-permute-start.4 = (f32[512,256]{1,0:T(8,128)S(1)}, f32[512,256]{1,0:T(8,128)S(1)}, u32[]{:S(2)}, u32[]{:S(2)}) collective-permute-start(f32[512,256]{1,0:T(8,128)S(1)} %collective-permute-done.3.rest_4_), channel_id=1, source_target_pairs={{0,1},{1,0},{2,3},{3,2},{4,5},{5,4},{6,7},{7,6},{8,9},{9,8},{10,11... | collective-permute-start | bytes 1572872 | tf_op jit(solution)/shard_map/ppermute | solution.py:101
  22.9 48.4 %copy-start.4 = (f32[512,256]{1,0:T(8,128)}, f32[512,256]{1,0:T(8,128)S(1)}, u32[]{:S(2)}) copy-start(f32[512,256]{1,0:T(8,128)S(1)} %collective-permute-done.rest_1_) | copy-start | bytes 1572868
  22.9 21.0 %collective-permute-start.5 = (f32[512,256]{1,0:T(8,128)S(1)}, f32[512,256]{1,0:T(8,128)S(1)}, u32[]{:S(2)}, u32[]{:S(2)}) collective-permute-start(f32[512,256]{1,0:T(8,128)S(1)} %collective-permute-done.1.rest_2_), channel_id=1, source_target_pairs={{6,4},{7,5},{8,14},{9,15},{10,8},{11,9},{12,10},{13,11},{14,12},{1... | collective-permute-start | bytes 1572872 | tf_op jit(solution)/shard_map/ppermute | solution.py:111
  30.8 40.6 %copy-start.5 = (f32[512,256]{1,0:T(8,128)}, f32[512,256]{1,0:T(8,128)S(1)}, u32[]{:S(2)}) copy-start(f32[512,256]{1,0:T(8,128)S(1)} %collective-permute-done.10.rest_12_) | copy-start | bytes 1572868
  30.8 16.0 %collective-permute-start.12 = (f32[512,256]{1,0:T(8,128)S(1)}, f32[512,256]{1,0:T(8,128)S(1)}, u32[]{:S(2)}, u32[]{:S(2)}) collective-permute-start(f32[512,256]{1,0:T(8,128)S(1)} %collective-permute-done.10.rest_12_), channel_id=1, source_target_pairs={{2,4},{3,5},{4,6},{5,7},{8,10},{9,11},{10,12},{11,13},{12,14},{13,... | collective-permute-start | bytes 1572872 | tf_op jit(solution)/shard_map/ppermute | solution.py:112
  34.2 16.2 %copy-start.6 = (f32[512,256]{1,0:T(8,128)}, f32[512,256]{1,0:T(8,128)S(1)}, u32[]{:S(2)}) copy-start(f32[512,256]{1,0:T(8,128)S(1)} %collective-permute-done.8.rest_10_) | copy-start | bytes 1572868
  34.2 12.6 %collective-permute-start.2 = (f32[512,256]{1,0:T(8,128)S(1)}, f32[512,256]{1,0:T(8,128)S(1)}, u32[]{:S(2)}, u32[]{:S(2)}) collective-permute-start(f32[512,256]{1,0:T(8,128)S(1)} %collective-permute-done.1.rest_2_), channel_id=1, source_target_pairs={{0,1},{1,0},{2,3},{3,2},{4,5},{5,4},{6,7},{7,6},{8,9},{9,8},{10,11... | collective-permute-start | bytes 1572872 | tf_op jit(solution)/shard_map/ppermute | solution.py:101
  34.2 16.2 %copy-start.8 = (f32[512,256]{1,0:T(8,128)}, f32[512,256]{1,0:T(8,128)S(1)}, u32[]{:S(2)}) copy-start(f32[512,256]{1,0:T(8,128)S(1)} %collective-permute-done.7.rest_9_) | copy-start | bytes 1572868
  34.2 12.6 %collective-permute-start.11 = (f32[512,256]{1,0:T(8,128)S(1)}, f32[512,256]{1,0:T(8,128)S(1)}, u32[]{:S(2)}, u32[]{:S(2)}) collective-permute-start(f32[512,256]{1,0:T(8,128)S(1)} %collective-permute-done.10.rest_12_), channel_id=1, source_target_pairs={{0,1},{1,0},{2,3},{3,2},{4,5},{5,4},{6,7},{7,6},{8,9},{9,8},{10,11... | collective-permute-start | bytes 1572872 | tf_op jit(solution)/shard_map/ppermute | solution.py:101
  34.7 15.7 %copy-start.10 = (f32[512,256]{1,0:T(8,128)}, f32[512,256]{1,0:T(8,128)S(1)}, u32[]{:S(2)}) copy-start(f32[512,256]{1,0:T(8,128)S(1)} %collective-permute-done.4.rest_5_) | copy-start | bytes 1572868
  34.7 12.1 %collective-permute-start.9 = (f32[512,256]{1,0:T(8,128)S(1)}, f32[512,256]{1,0:T(8,128)S(1)}, u32[]{:S(2)}, u32[]{:S(2)}) collective-permute-start(f32[512,256]{1,0:T(8,128)S(1)} %collective-permute-done.8.rest_10_), channel_id=1, source_target_pairs={{0,1},{1,0},{2,3},{3,2},{4,5},{5,4},{6,7},{7,6},{8,9},{9,8},{10,11... | collective-permute-start | bytes 1572872 | tf_op jit(solution)/shard_map/ppermute | solution.py:101
  43.9 6.4 %copy-start.12 = (f32[512,256]{1,0:T(8,128)}, f32[512,256]{1,0:T(8,128)S(1)}, u32[]{:S(2)}) copy-start(f32[512,256]{1,0:T(8,128)S(1)} %collective-permute-done.5.rest_6_) | copy-start | bytes 1572868
  43.9 2.9 %collective-permute-start.6 = (f32[512,256]{1,0:T(8,128)S(1)}, f32[512,256]{1,0:T(8,128)S(1)}, u32[]{:S(2)}, u32[]{:S(2)}) collective-permute-start(f32[512,256]{1,0:T(8,128)S(1)} %collective-permute-done.5.rest_6_), channel_id=1, source_target_pairs={{0,1},{1,0},{2,3},{3,2},{4,5},{5,4},{6,7},{7,6},{8,9},{9,8},{10,11... | collective-permute-start | bytes 1572872 | tf_op jit(solution)/shard_map/ppermute | solution.py:101
  46.7 3.6 %copy-start.14 = (f32[512,256]{1,0:T(8,128)}, f32[512,256]{1,0:T(8,128)S(1)}, u32[]{:S(2)}) copy-start(f32[512,256]{1,0:T(8,128)S(1)} %collective-permute-done.12.rest_14_) | copy-start | bytes 1572868
  46.7 1.9 %collective-permute-start.13 = (f32[512,256]{1,0:T(8,128)S(1)}, f32[512,256]{1,0:T(8,128)S(1)}, u32[]{:S(2)}, u32[]{:S(2)}) collective-permute-start(f32[512,256]{1,0:T(8,128)S(1)} %collective-permute-done.12.rest_14_), channel_id=1, source_target_pairs={{0,1},{1,0},{2,3},{3,2},{4,5},{5,4},{6,7},{7,6},{8,9},{9,8},{10,11... | collective-permute-start | bytes 1572872 | tf_op jit(solution)/shard_map/ppermute | solution.py:101
  46.7 3.6 %copy-start.16 = (f32[512,256]{1,0:T(8,128)}, f32[512,256]{1,0:T(8,128)S(1)}, u32[]{:S(2)}) copy-start(f32[512,256]{1,0:T(8,128)S(1)} %collective-permute-done.2.rest_3_) | copy-start | bytes 1572868
  46.8 3.6 %copy-start.18 = (f32[512,256]{1,0:T(8,128)}, f32[512,256]{1,0:T(8,128)S(1)}, u32[]{:S(2)}) copy-start(f32[512,256]{1,0:T(8,128)S(1)} %collective-permute-done.11.rest_13_) | copy-start | bytes 1572868
  46.8 3.6 %copy-start.20 = (f32[512,256]{1,0:T(8,128)}, f32[512,256]{1,0:T(8,128)S(1)}, u32[]{:S(2)}) copy-start(f32[512,256]{1,0:T(8,128)S(1)} %collective-permute-done.9.rest_11_) | copy-start | bytes 1572868
  46.8 3.6 %copy-start.22 = (f32[512,256]{1,0:T(8,128)}, f32[512,256]{1,0:T(8,128)S(1)}, u32[]{:S(2)}) copy-start(f32[512,256]{1,0:T(8,128)S(1)} %collective-permute-done.6.rest_7_) | copy-start | bytes 1572868
  48.6 1.8 %copy-start.24 = (f32[512,256]{1,0:T(8,128)}, f32[512,256]{1,0:T(8,128)S(1)}, u32[]{:S(2)}) copy-start(f32[512,256]{1,0:T(8,128)S(1)} %collective-permute-done.13.rest_15_) | copy-start | bytes 1572868
  50.4 33.7 %collective-permute-start.14 = (f32[1024,256]{1,0:T(8,128)}, f32[1024,256]{1,0:T(8,128)}, u32[]{:S(2)}, u32[]{:S(2)}) collective-permute-start(f32[1024,256]{1,0:T(8,128)} %get-tuple-element.30), channel_id=1, source_target_pairs={{0,8},{1,9},{2,10},{3,11},{4,12},{5,13},{6,14},{7,15}} | collective-permute-start | bytes 3145736 | tf_op jit(solution)/shard_map/ppermute | solution.py:385
  52.1 17.2 %collective-permute-start.15 = (f32[256,256]{1,0:T(8,128)S(1)}, f32[256,256]{1,0:T(8,128)}, u32[]{:S(2)}, u32[]{:S(2)}) collective-permute-start(f32[256,256]{1,0:T(8,128)S(1)} %get-tuple-element.31), channel_id=1, source_target_pairs={{0,24},{1,25},{2,26},{3,27},{4,28},{5,29},{6,30},{7,31}} | collective-permute-start | bytes 786440 | tf_op jit(solution)/shard_map/ppermute | solution.py:337
  53.4 30.7 %collective-permute-start.17 = (f32[256,256]{1,0:T(8,128)S(1)}, f32[256,256]{1,0:T(8,128)}, u32[]{:S(2)}, u32[]{:S(2)}) collective-permute-start(f32[256,256]{1,0:T(8,128)S(1)} %get-tuple-element.32), channel_id=1, source_target_pairs={{0,24},{1,25},{2,26},{3,27},{4,28},{5,29},{6,30},{7,31}} | collective-permute-start | bytes 786440 | tf_op jit(solution)/shard_map/ppermute | solution.py:338
  69.3 14.8 %collective-permute-start.16 = (f32[256,256]{1,0:T(8,128)}, f32[256,256]{1,0:T(8,128)}, u32[]{:S(2)}, u32[]{:S(2)}) collective-permute-start(f32[256,256]{1,0:T(8,128)} %collective-permute-done.15), channel_id=1, source_target_pairs={{24,16},{25,17},{26,18},{27,19},{28,20},{29,21},{30,22},{31,23}} | collective-permute-start | bytes 786440 | tf_op jit(solution)/shard_map/ppermute | solution.py:338
  71.3 1.0 copy-start.7
  72.4 1.0 copy-start.9
  73.4 1.0 copy-start.11
  74.5 1.0 copy-start.13
  75.5 1.0 copy-start.15
  76.6 1.0 copy-start.17
  77.6 1.0 copy-start.19
  81.8 1.2 copy-start.27
  85.4 6.6 %collective-permute-start.19 = (f32[256,256]{1,0:T(8,128)S(1)}, f32[256,256]{1,0:T(8,128)S(1)}, u32[]{:S(2)}, u32[]{:S(2)}) collective-permute-start(f32[256,256]{1,0:T(8,128)S(1)} %fusion), channel_id=1, source_target_pairs={{0,160},{8,168},{16,176},{24,184},{1,161},{9,169},{17,177},{25,185... | collective-permute-start | bytes 786440 | tf_op jit(solution)/shard_map/ppermute | solution.py:347
  86.7 5.8 %collective-permute-start.18 = (f32[256,256]{1,0:T(8,128)S(1)}, f32[256,256]{1,0:T(8,128)S(1)}, u32[]{:S(2)}, u32[]{:S(2)}) collective-permute-start(f32[256,256]{1,0:T(8,128)S(1)} %fusion), channel_id=1, source_target_pairs={{0,96},{8,104},{16,112},{24,120},{1,97},{9,105},{17,113},{25,121},... | collective-permute-start | bytes 786440 | tf_op jit(solution)/shard_map/ppermute | solution.py:346
  89.2 5.9 %collective-permute-start.22 = (f32[256,256]{1,0:T(8,128)S(1)}, f32[256,256]{1,0:T(8,128)S(1)}, u32[]{:S(2)}, u32[]{:S(2)}) collective-permute-start(f32[256,256]{1,0:T(8,128)S(1)} %get-tuple-element.38), channel_id=1, source_target_pairs={{8,16},{9,17},{10,18},{11,19},{12,20},{13,21},{14,22},{15,23}} | collective-permute-start | bytes 786440 | tf_op jit(solution)/shard_map/ppermute | solution.py:342
  89.9 12.6 %collective-permute-start.23 = (f32[256,256]{1,0:T(8,128)S(1)}, f32[256,256]{1,0:T(8,128)S(1)}, u32[]{:S(2)}, u32[]{:S(2)}) collective-permute-start(f32[256,256]{1,0:T(8,128)S(1)} %get-tuple-element.39), channel_id=1, source_target_pairs={{8,24},{9,25},{10,26},{11,27},{12,28},{13,29},{14,30},{15,31}} | collective-permute-start | bytes 786440 | tf_op jit(solution)/shard_map/ppermute | solution.py:342
  91.2 11.3 %collective-permute-start.24 = (f32[256,256]{1,0:T(8,128)S(1)}, f32[256,256]{1,0:T(8,128)S(1)}, u32[]{:S(2)}, u32[]{:S(2)}) collective-permute-start(f32[256,256]{1,0:T(8,128)S(1)} %get-tuple-element.40), channel_id=1, source_target_pairs={{8,0},{9,1},{10,2},{11,3},{12,4},{13,5},{14,6},{15,7}} | collective-permute-start | bytes 786440 | tf_op jit(solution)/shard_map/ppermute | solution.py:342
  92.5 12.9 %collective-permute-start.21 = (f32[256,256]{1,0:T(8,128)S(1)}, f32[256,256]{1,0:T(8,128)S(1)}, u32[]{:S(2)}, u32[]{:S(2)}) collective-permute-start(f32[256,256]{1,0:T(8,128)S(1)} %add_select_fusion.4), channel_id=1, source_target_pairs={{0,224},{8,232},{16,240},{24,248},{96,64},{104,72},{112,80},{120,8... | collective-permute-start | bytes 786440 | tf_op jit(solution)/shard_map/ppermute | solution.py:353
  93.8 11.6 %collective-permute-start.20 = (f32[256,256]{1,0:T(8,128)S(1)}, f32[256,256]{1,0:T(8,128)S(1)}, u32[]{:S(2)}, u32[]{:S(2)}) collective-permute-start(f32[256,256]{1,0:T(8,128)S(1)} %add_select_fusion.4), channel_id=1, source_target_pairs={{0,32},{8,40},{16,48},{24,56},{96,128},{104,136},{112,144},{120,15... | collective-permute-start | bytes 786440 | tf_op jit(solution)/shard_map/ppermute | solution.py:352
  102.6 21.7 %copy-start.28 = (f32[1024,256]{1,0:T(8,128)S(1)}, f32[1024,256]{1,0:T(8,128)}, u32[]{:S(2)}) copy-start(f32[1024,256]{1,0:T(8,128)} %target.1) | copy-start | bytes 3145732
  102.7 6.7 %collective-permute-start.26 = (f32[256,256]{1,0:T(8,128)S(1)}, f32[256,256]{1,0:T(8,128)S(1)}, u32[]{:S(2)}, u32[]{:S(2)}) collective-permute-start(f32[256,256]{1,0:T(8,128)S(1)} %add_select_fusion.2), channel_id=1, source_target_pairs={{0,160},{8,168},{16,176},{24,184},{1,161},{9,169},{17,177},{25,185... | collective-permute-start | bytes 786440 | tf_op jit(solution)/shard_map/ppermute | solution.py:347
  104.1 5.3 %collective-permute-start.25 = (f32[256,256]{1,0:T(8,128)S(1)}, f32[256,256]{1,0:T(8,128)S(1)}, u32[]{:S(2)}, u32[]{:S(2)}) collective-permute-start(f32[256,256]{1,0:T(8,128)S(1)} %add_select_fusion.2), channel_id=1, source_target_pairs={{0,96},{8,104},{16,112},{24,120},{1,97},{9,105},{17,113},{25,121},... | collective-permute-start | bytes 786440 | tf_op jit(solution)/shard_map/ppermute | solution.py:346
  105.5 7.8 %collective-permute-start.29 = (f32[256,256]{1,0:T(8,128)S(1)}, f32[256,256]{1,0:T(8,128)S(1)}, u32[]{:S(2)}, u32[]{:S(2)}) collective-permute-start(f32[256,256]{1,0:T(8,128)S(1)} %add_select_fusion.3.rest_16_), channel_id=1, source_target_pairs={{0,8},{8,16},{16,24},{24,0},{32,40},{40,48},{48,56},{56,32},{64,72... | collective-permute-start | bytes 786440 | tf_op jit(solution)/shard_map/ppermute | solution.py:358
  109.4 7.7 %collective-permute-start.27 = (f32[256,256]{1,0:T(8,128)S(1)}, f32[256,256]{1,0:T(8,128)S(1)}, u32[]{:S(2)}, u32[]{:S(2)}) collective-permute-start(f32[256,256]{1,0:T(8,128)S(1)} %add_select_fusion.3.rest_16_), channel_id=1, source_target_pairs={{8,0},{16,8},{24,16},{0,24},{40,32},{48,40},{56,48},{32,56},{72,64... | collective-permute-start | bytes 786440 | tf_op jit(solution)/shard_map/ppermute | solution.py:358
  109.5 7.7 %collective-permute-start.32 = (f32[256,256]{1,0:T(8,128)S(1)}, f32[256,256]{1,0:T(8,128)S(1)}, u32[]{:S(2)}, u32[]{:S(2)}) collective-permute-start(f32[256,256]{1,0:T(8,128)S(1)} %add_select_fusion.1), channel_id=1, source_target_pairs={{0,224},{8,232},{16,240},{24,248},{96,64},{104,72},{112,80},{120,8... | collective-permute-start | bytes 786440 | tf_op jit(solution)/shard_map/ppermute | solution.py:353
  110.8 6.4 %collective-permute-start.31 = (f32[256,256]{1,0:T(8,128)S(1)}, f32[256,256]{1,0:T(8,128)S(1)}, u32[]{:S(2)}, u32[]{:S(2)}) collective-permute-start(f32[256,256]{1,0:T(8,128)S(1)} %add_select_fusion.1), channel_id=1, source_target_pairs={{0,32},{8,40},{16,48},{24,56},{96,128},{104,136},{112,144},{120,15... | collective-permute-start | bytes 786440 | tf_op jit(solution)/shard_map/ppermute | solution.py:352
  113.3 7.6 %collective-permute-start.30 = (f32[128,256]{1,0:T(8,128)S(1)}, f32[128,256]{1,0:T(8,128)S(1)}, u32[]{:S(2)}, u32[]{:S(2)}) collective-permute-start(f32[128,256]{1,0:T(8,128)S(1)} %slice.26), channel_id=1, source_target_pairs={{0,8},{8,16},{16,24},{24,0},{32,40},{40,48},{48,56},{56,32},{64,72... | collective-permute-start | bytes 393224 | tf_op jit(solution)/shard_map/ppermute | solution.py:362
  117.1 7.2 %collective-permute-start.28 = (f32[128,256]{1,0:T(8,128)S(1)}, f32[128,256]{1,0:T(8,128)S(1)}, u32[]{:S(2)}, u32[]{:S(2)}) collective-permute-start(f32[128,256]{1,0:T(8,128)S(1)} %slice.25), channel_id=1, source_target_pairs={{8,0},{16,8},{24,16},{0,24},{40,32},{48,40},{56,48},{32,56},{72,64... | collective-permute-start | bytes 393224 | tf_op jit(solution)/shard_map/ppermute | solution.py:362
  117.3 12.2 %collective-permute-start.34 = (f32[256,256]{1,0:T(8,128)S(1)}, f32[256,256]{1,0:T(8,128)S(1)}, u32[]{:S(2)}, u32[]{:S(2)}) collective-permute-start(f32[256,256]{1,0:T(8,128)S(1)} %add_select_fusion.rest_16_), channel_id=1, source_target_pairs={{0,8},{8,16},{16,24},{24,0},{32,40},{40,48},{48,56},{56,32},{64,72... | collective-permute-start | bytes 786440 | tf_op jit(solution)/shard_map/ppermute | solution.py:358
  120.5 8.9 %collective-permute-start.33 = (f32[256,256]{1,0:T(8,128)S(1)}, f32[256,256]{1,0:T(8,128)S(1)}, u32[]{:S(2)}, u32[]{:S(2)}) collective-permute-start(f32[256,256]{1,0:T(8,128)S(1)} %add_select_fusion.rest_16_), channel_id=1, source_target_pairs={{8,0},{16,8},{24,16},{0,24},{40,32},{48,40},{56,48},{32,56},{72,64... | collective-permute-start | bytes 786440 | tf_op jit(solution)/shard_map/ppermute | solution.py:358
  129.5 7.6 %collective-permute-start.35 = (f32[128,256]{1,0:T(8,128)S(1)}, f32[128,256]{1,0:T(8,128)S(1)}, u32[]{:S(2)}, u32[]{:S(2)}) collective-permute-start(f32[128,256]{1,0:T(8,128)S(1)} %slice.22), channel_id=1, source_target_pairs={{8,0},{16,8},{24,16},{0,24},{40,32},{48,40},{56,48},{32,56},{72,64... | collective-permute-start | bytes 393224 | tf_op jit(solution)/shard_map/ppermute | solution.py:362
  129.6 7.6 %collective-permute-start.36 = (f32[128,256]{1,0:T(8,128)S(1)}, f32[128,256]{1,0:T(8,128)S(1)}, u32[]{:S(2)}, u32[]{:S(2)}) collective-permute-start(f32[128,256]{1,0:T(8,128)S(1)} %slice.23), channel_id=1, source_target_pairs={{0,8},{8,16},{16,24},{24,0},{32,40},{40,48},{48,56},{56,32},{64,72... | collective-permute-start | bytes 393224 | tf_op jit(solution)/shard_map/ppermute | solution.py:362
  (3 other events, 3.1 us)

commit v5 on v4

--- a/solution.py
+++ b/solution.py
@@ -63,7 +63,10 @@
         cols = lax.broadcasted_iota(jnp.int32, (Q, Q), 1)
         block = panel_ref[pl.ds(pl.multiple_of(number * Q, Q), Q), :]
         inverse = jnp.where(rows == cols, 1.0 / jnp.where(rows == cols, block, 1.0), 0.0)
-        level = 0
+        down, across = jnp.sum(inverse, axis=1, keepdims=True), jnp.sum(inverse, axis=0, keepdims=True)
+        pair = ((rows >> 1) == (cols >> 1)) & (rows > cols)
+        inverse = inverse - down * jnp.where(pair, block, 0.0) * across
+        level = 1
         while (1 << level) < Q:
             pair = (rows >> (level + 1)) == (cols >> (level + 1))
             below = pair & (((rows >> level) & 1) == 1) & (((cols >> level) & 1) == 0)
@@ -249,78 +252,123 @@
 PIECES = ((0, Q), (Q, Q), (2 * Q, Q // 2), (2 * Q + Q // 2, Q // 2), (3 * Q, Q))
 
 
-def update_kernel(base, slots, last, place, target, *rest):
-    used = [n for n, (at, _) in enumerate(PIECES) if at // Q in slots]
-    tops, bottoms, rest = rest[: len(CHUNK)], rest[len(CHUNK) : 2 * len(CHUNK)], rest[2 * len(CHUNK) :]
-    pieces, rest = rest[: len(used)], rest[len(used) + int(base + len(slots) > PARTS) :]
-    out, whole, blocks, target_buf, solved_buf, sem, target_sem, solved_sem, whole_sem = rest
-    copies, kept = [], []
-    for i, (n, piece) in enumerate(zip(used, pieces)):
-        at, length = PIECES[n]
-        here = pl.ds(slots.index(at // Q) * Q + at % Q, length)
-        copies.append(pltpu.make_async_copy(piece, solved_buf.at[here], solved_sem.at[i]))
-        start = pl.multiple_of(((at + place[TURN] * Q) & (NB - 1)) + base * Q, Q // 2)
-        kept.append(pltpu.make_async_copy(solved_buf.at[here], whole.at[pl.ds(start, length)], whole_sem.at[i]))
-    copies.append(pltpu.make_async_copy(target, target_buf, target_sem))
-
+def turned(place, root):
+    return (place[TURN] - root) & (PARTS - 1)
+
+
+def piece_rows(place, root, at):
+    return pl.multiple_of(((at + turned(place, root) * Q) & (NB - 1)) + root * NB, Q // 2)
+
+
+def panel_blocks(place, root, slots, out):
     def slot_of(block):
-        return (block - place[TURN]) & (PARTS - 1)
+        return (block - turned(place, root)) & (PARTS - 1)
 
     def chosen(block):
-        here = (block >= base) & (block < base + PARTS)
+        here = (block >= root * PARTS) & (block < (root + 1) * PARTS)
         for slot in set(range(PARTS)) - set(slots):
             here &= slot_of(block) != slot
         return here
 
-    def at_slot(block, rows):
-        slot = slot_of(block)
-        return blocks.at[jnp.where(slot > slots[-1], 0, sum(jnp.where(slot > other, 1, 0) for other in slots)), rows]
-
-    wait_panel = place_panel(place, tops, bottoms, chosen, at_slot, sem)
+    return chosen, lambda block, rows: out(sum(jnp.where(slot_of(block) > other, 1, 0) for other in slots), rows)
+
+
+def update_kernel(root, slots, ahead, place, target, *rest):
+    tops, bottoms, rest = rest[: len(CHUNK)], rest[len(CHUNK) : 2 * len(CHUNK)], rest[2 * len(CHUNK) :]
+    used = [(at, length) for at, length in PIECES if at // Q in slots]
+    pieces, rest = rest[: len(used)], rest[len(used) + root :]
+    out, whole, *rest = rest
+    if ahead:
+        (next_block, *rest) = rest
+    blocks, target_buf, solved_buf, sem, target_sem, solved_sem, whole_sem = rest
+    copies, kept = [], []
+    for i, ((at, length), piece) in enumerate(zip(used, pieces)):
+        here = pl.ds(slots.index(at // Q) * Q + at % Q, length)
+        copies.append(pltpu.make_async_copy(piece, solved_buf.at[here], solved_sem.at[i]))
+        there = whole.at[pl.ds(piece_rows(place, root, at), length)]
+        kept.append(pltpu.make_async_copy(solved_buf.at[here], there, whole_sem.at[i]))
+    copies.append(pltpu.make_async_copy(target, target_buf, target_sem))
     for copy in copies:
         copy.start()
+    wait_panel = place_panel(
+        place, tops, bottoms, *panel_blocks(place, root, slots, lambda n, rows: blocks.at[n, rows]), sem.at[0]
+    )
+    if ahead:
+        chosen, there = panel_blocks(place, root, (ahead,), lambda _, rows: next_block.at[rows])
+        wait_ahead = place_panel(place, tops, bottoms, chosen, there, sem.at[1])
     for copy in copies[: len(used)]:
         copy.wait()
     for copy in kept:
         copy.start()
     solved = [halves(solved_buf[pl.ds(i * Q, Q), :]) for i in range(len(slots))]
-    for copy in copies[len(used) :]:
-        copy.wait()
+    copies[-1].wait()
     wait_panel()
     for r in range(PARTS):
         rows = pl.ds(r * Q, Q)
         result = target_buf[rows, :]
         for i in range(len(slots)):
             result = result - product(halves(blocks[i, rows, :]), solved[i])
-        out[rows, :] = jnp.where(place[ROW] >= 2, result, 0.0) if last else result
+        out[rows, :] = result
+    if ahead:
+        wait_ahead()
     for copy in kept:
         copy.wait()
 
 
-def update(name, base, slots, last, place, target, tops, bottoms, pieces, *before):
+def update(name, root, slots, ahead, place, target, tops, bottoms, pieces, *before):
     scratch = [
         pltpu.VMEM((len(slots), NB, Q), F32),
         pltpu.VMEM((NB, Q), F32),
         pltpu.VMEM((len(slots) * Q, Q), F32),
-        pltpu.SemaphoreType.DMA((2, COLS)),
+        pltpu.SemaphoreType.DMA((2, 2, COLS)),
         pltpu.SemaphoreType.DMA,
         pltpu.SemaphoreType.DMA((len(pieces),)),
         pltpu.SemaphoreType.DMA((len(pieces),)),
     ]
     tops, bottoms = ([pltpu.with_memory_space_constraint(x, pltpu.HBM) for x in half] for half in (tops, bottoms))
     operands = (place, target, *tops, *bottoms, *pieces, *before)
+    vmem, anywhere = pl.BlockSpec(memory_space=pltpu.VMEM), pl.BlockSpec(memory_space=pl.ANY)
     return call(
-        functools.partial(update_kernel, base, slots, last),
+        functools.partial(update_kernel, root, slots, ahead),
         name,
-        [((NB, Q), F32), ((2 * NB, Q), F32)],
+        [((NB, Q), F32), ((2 * NB, Q), F32)] + [((NB, Q), F32)] * bool(ahead),
         scratch,
         operands,
-        out_specs=[pl.BlockSpec(memory_space=pltpu.VMEM), pl.BlockSpec(memory_space=pl.ANY)],
+        out_specs=[vmem, anywhere] + [vmem] * bool(ahead),
         input_output_aliases={len(operands) - 1: 1} if before else {},
         flops=(6 if before else UPDATE_COST) * NB * NB * Q,
     )
 
 
+def last_kernel(place, target, block, upper, lower, before, out, whole, sems):
+    kept = []
+    for i, (piece, at) in enumerate(((upper, 2 * Q), (lower, 2 * Q + Q // 2))):
+        there = whole.at[pl.ds(piece_rows(place, 1, at), Q // 2)]
+        kept.append(pltpu.make_async_copy(piece, there, sems.at[i]))
+        kept[-1].start()
+    solved = halves(jnp.concatenate([upper[...], lower[...]], axis=0))
+    for r in range(PARTS):
+        rows = pl.ds(r * Q, Q)
+        result = target[rows, :] - product(halves(block[rows, :]), solved)
+        out[rows, :] = jnp.where(place[ROW] >= 2, result, 0.0)
+    for copy in kept:
+        copy.wait()
+
+
+def last(place, target, block, across, whole):
+    vmem, anywhere = pl.BlockSpec(memory_space=pltpu.VMEM), pl.BlockSpec(memory_space=pl.ANY)
+    return call(
+        last_kernel,
+        "last",
+        [((NB, Q), F32), ((2 * NB, Q), F32)],
+        [pltpu.SemaphoreType.DMA((2,))],
+        (place, target, block, *across, whole),
+        in_specs=[vmem] * 4 + [anywhere],
+        out_specs=[vmem, anywhere],
+        input_output_aliases={5: 1},
+    )
+
+
 def along_z(moves):
     return [(a * XS + x, b * XS + x) for a, b in moves for x in range(XS)]
 
@@ -339,7 +387,7 @@
 
 
 def scatter_second(pieces):
-    return [lax.ppermute(pieces[i], "row", [(1, (1 + i) % XS)]) for i in (1, 2, 3)]
+    return [lax.ppermute(pieces[i], "row", [(1, (1 + i) % XS)]) for i in (2, 3, 1)]
 
 
 def far_z(mine, z):
@@ -367,13 +415,13 @@
     col = lax.axis_index("col")
     z = row // XS
 
-    def place(root):
-        return jnp.stack([row, col // 2, col % 2, (row - root) % XS])
+    def place():
+        return jnp.stack([row, col // 2, col % 2, row % XS])
 
     def after(value, *others):
         return lax.optimization_barrier((value, *others))[0]
 
-    top, bottom = payload(place(0), panel)
+    top, bottom = payload(place(), panel)
     top_near = near_chips(top, lambda r, y: r > 0 or y == 0)
     bottom_near = near_chips(bottom, lambda r, y: r > 0 or y <= 1)
     top_far = far_chip(top_near[0], None, lambda r, y: r > 0 or y == 0)
@@ -381,14 +429,14 @@
     tops = both_cores((top, *top_near, top_far))
     bottoms = both_cores((bottom, *bottom_near, bottom_far))
 
-    first, two, three = solve(place(0), rhs, tops, bottoms)
+    first, two, three = solve(place(), rhs, tops, bottoms)
     ahead = lax.ppermute(first, "row", [(0, 1)])
     two_ahead, three_ahead = scatter_first(two, three)
-    w_high, w_low, y_value = prepare(place(0), rhs, tops, bottoms)
+    w_high, w_low, y_value = prepare(place(), rhs, tops, bottoms)
     mine_one = jnp.where(row == 1, ahead[Q : 2 * Q], two_ahead + three_ahead)
     mine_one = far_z(after(jnp.where(row == 0, first[:Q], mine_one), w_high), z)
 
-    pieces = combine(place(0), w_high, w_low, y_value, ahead)
+    pieces = combine(place(), w_high, w_low, y_value, ahead)
     got = scatter_second(pieces)
     mine_one = near_z(after(mine_one, *pieces), z)
     mine_two = jnp.where(row == 1, pieces[0], got[0] + got[1] + got[2])
@@ -396,13 +444,13 @@
     across_one = across_x(*beside_one)
     mine_two = far_z(mine_two, z)
     pieces_one = [after(x, mine_two) for x in (mine_one, beside_one[0], *across_one, beside_one[1])]
-    updated, whole = update("update", 0, (0, 1, 2, 3), False, place(0), rhs, tops, bottoms, pieces_one)
     mine_two = near_z(mine_two, z)
+    updated, whole = update("update", 0, (0, 1, 2, 3), None, place(), rhs, tops, bottoms, pieces_one)
     beside_two = [after(piece, updated) for piece in over_x(mine_two)]
     across_two = across_x(*beside_two)
-    pieces_two = (mine_two, *beside_two)
-    updated, whole = update("most", PARTS, (0, 1, 3), False, place(1), updated, tops, bottoms, pieces_two, whole)
-    return tuple(update("last", PARTS, (2,), True, place(1), updated, tops, bottoms, across_two, whole))
+    pieces = (mine_two, *beside_two)
+    updated, whole, block = update("most", 1, (0, 1, 3), 2, place(), updated, tops, bottoms, pieces, whole)
+    return tuple(last(place(), updated, block, across_two, whole))
 
 
 def solution(mesh):

time: 143 us -> 142 us (level)
  transfers between devices with their start and end apart: 37 -> 37, of which waited for: 13 -> 13; matrix products, arithmetic and copies ran while one was open for 0% -> 0% of each run, Pallas kernels for 8% -> 9%
where the time goes in v5:
time: 142 us; the launch traced here: 140 us
  starting transfers between devices  55.6 us (39%)
  waiting for transfers between devices  51 us (36%)
  Pallas kernels  17.6 us (12%)
  local copies, waits for them, and re-layouts  13 us (9%)
  other arithmetic  1.61 us (1%)
  between operations  1.5 us (1%)
    pallas_call x7, Pallas kernels, call(): pl.pallas_call(kernel, out_shape=[(pltpu.HBM if len(shape) == 3 else jax....  17.6 us
    ppermute x1, waiting for transfers between devices, scatter_first(): relay = lax.ppermute(two, 'row', [(0, 3)])  14 us
    unnamed x60, local copies, waits for them, and re-layouts  13 us
    ppermute x1, waiting for transfers between devices, far_chip(): return lax.ppermute(ahead, BOTH, pairs(-1, 1, has))  9.14 us
    ppermute x2, starting transfers between devices, near_chips(): return (lax.ppermute(chunk, BOTH, pairs(-1, 0, has)), behind)  8.35 us
    ppermute x3, waiting for transfers between devices, scatter_second(): lax.ppermute(pieces[i], 'row', [(1, (1 + i) % XS)])  7.41 us
    ppermute x2, starting transfers between devices, over_x(): lax.ppermute(mine, 'row', TO_NEXT)  7.16 us
    ppermute x2, starting transfers between devices, across_x(): lax.ppermute(before[Q // 2:], 'row', TO_NEXT)  6.99 us
  transfers between devices with their start and end apart: 37, of which 13 were waited for; matrix products, arithmetic and copies ran while one was open for 0% of the time, Pallas kernels for 9%

profile of v5, /device:TPU:6, one launch (start us, length us, event | category | flops | bytes accessed | tf_op | source)
XLA Modules:
  0.0 140.4 jit_solution(5330072952963006723)
XLA Ops:
  0.7 0.1 pad_add_fusion.place
  0.8 1.3 copy-done.29
  2.0 0.6 payload.1
  2.7 3.5 %collective-permute-start.3 = (f32[512,256]{1,0:T(8,128)S(1)}, f32[512,256]{1,0:T(8,128)S(1)}, u32[]{:S(2)}, u32[]{:S(2)}) collective-permute-start(f32[512,256]{1,0:T(8,128)S(1)} %get-tuple-element.29.rest_0_), channel_id=1, source_target_pairs={{0,2},{1,3},{8,10},{9,11},{10,12},{11,13},{12,14},{13,15},{14,8},{... | collective-permute-start | bytes 1572872 | tf_op jit(solution)/shard_map/ppermute | solution.py:108
  6.2 3.6 %collective-permute-start.1 = (f32[512,256]{1,0:T(8,128)S(1)}, f32[512,256]{1,0:T(8,128)S(1)}, u32[]{:S(2)}, u32[]{:S(2)}) collective-permute-start(f32[512,256]{1,0:T(8,128)S(1)} %get-tuple-element.29.rest_0_), channel_id=1, source_target_pairs={{0,6},{1,7},{8,14},{9,15},{10,8},{11,9},{12,10},{13,11},{14,12},{1... | collective-permute-start | bytes 1572872 | tf_op jit(solution)/shard_map/ppermute | solution.py:109
  9.8 0.1 collective-permute-start
  9.9 2.3 %collective-permute-start.10 = (f32[512,256]{1,0:T(8,128)S(1)}, f32[512,256]{1,0:T(8,128)S(1)}, u32[]{:S(2)}, u32[]{:S(2)}) collective-permute-start(f32[512,256]{1,0:T(8,128)S(1)} %get-tuple-element.30.rest_8_), channel_id=1, source_target_pairs={{0,2},{1,3},{2,4},{3,5},{8,10},{9,11},{10,12},{11,13},{12,14},{13,... | collective-permute-start | bytes 1572872 | tf_op jit(solution)/shard_map/ppermute | solution.py:108
  12.1 4.8 %collective-permute-start.8 = (f32[512,256]{1,0:T(8,128)S(1)}, f32[512,256]{1,0:T(8,128)S(1)}, u32[]{:S(2)}, u32[]{:S(2)}) collective-permute-start(f32[512,256]{1,0:T(8,128)S(1)} %get-tuple-element.30.rest_8_), channel_id=1, source_target_pairs={{0,6},{1,7},{2,0},{3,1},{8,14},{9,15},{10,8},{11,9},{12,10},{13,11... | collective-permute-start | bytes 1572872 | tf_op jit(solution)/shard_map/ppermute | solution.py:109
  16.9 3.7 %collective-permute-done.3.rest_4_ = f32[512,256]{1,0:T(8,128)S(1)} collective-permute-done((f32[512,256]{1,0:T(8,128)S(1)}, f32[512,256]{1,0:T(8,128)S(1)}, u32[]{:S(2)}, u32[]{:S(2)}) %collective-permute-start.3) | collective-permute-done | bytes 524320 | tf_op jit(solution)/shard_map/ppermute | solution.py:108
  20.6 2.3 %collective-permute-done.1.rest_2_ = f32[512,256]{1,0:T(8,128)S(1)} collective-permute-done((f32[512,256]{1,0:T(8,128)S(1)}, f32[512,256]{1,0:T(8,128)S(1)}, u32[]{:S(2)}, u32[]{:S(2)}) %collective-permute-start.1) | collective-permute-done | bytes 524320 | tf_op jit(solution)/shard_map/ppermute | solution.py:109
  22.9 4.8 %collective-permute-start.5 = (f32[512,256]{1,0:T(8,128)S(1)}, f32[512,256]{1,0:T(8,128)S(1)}, u32[]{:S(2)}, u32[]{:S(2)}) collective-permute-start(f32[512,256]{1,0:T(8,128)S(1)} %collective-permute-done.1.rest_2_), channel_id=1, source_target_pairs={{6,4},{7,5},{8,14},{9,15},{10,8},{11,9},{12,10},{13,11},{14,12},{1... | collective-permute-start | bytes 1572872 | tf_op jit(solution)/shard_map/ppermute | solution.py:114
  27.7 3.0 %collective-permute-done.10.rest_12_ = f32[512,256]{1,0:T(8,128)S(1)} collective-permute-done((f32[512,256]{1,0:T(8,128)S(1)}, f32[512,256]{1,0:T(8,128)S(1)}, u32[]{:S(2)}, u32[]{:S(2)}) %collective-permute-start.10) | collective-permute-done | bytes 524320 | tf_op jit(solution)/shard_map/ppermute | solution.py:108
  30.8 2.2 %collective-permute-start.12 = (f32[512,256]{1,0:T(8,128)S(1)}, f32[512,256]{1,0:T(8,128)S(1)}, u32[]{:S(2)}, u32[]{:S(2)}) collective-permute-start(f32[512,256]{1,0:T(8,128)S(1)} %collective-permute-done.10.rest_12_), channel_id=1, source_target_pairs={{2,4},{3,5},{4,6},{5,7},{8,10},{9,11},{10,12},{11,13},{12,14},{13,... | collective-permute-start | bytes 1572872 | tf_op jit(solution)/shard_map/ppermute | solution.py:115
  33.0 1.2 collective-permute-done.8.rest_10_
  34.2 0.5 collective-permute-start.11
  34.7 0.1 collective-permute-start.9
  34.8 9.1 %collective-permute-done.5.rest_6_ = f32[512,256]{1,0:T(8,128)S(1)} collective-permute-done((f32[512,256]{1,0:T(8,128)S(1)}, f32[512,256]{1,0:T(8,128)S(1)}, u32[]{:S(2)}, u32[]{:S(2)}) %collective-permute-start.5) | collective-permute-done | bytes 524320 | tf_op jit(solution)/shard_map/ppermute | solution.py:114
  43.9 2.8 %collective-permute-done.12.rest_14_ = f32[512,256]{1,0:T(8,128)S(1)} collective-permute-done((f32[512,256]{1,0:T(8,128)S(1)}, f32[512,256]{1,0:T(8,128)S(1)}, u32[]{:S(2)}, u32[]{:S(2)}) %collective-permute-start.12) | collective-permute-done | bytes 524320 | tf_op jit(solution)/shard_map/ppermute | solution.py:115
  46.8 1.8 %collective-permute-done.13.rest_15_ = f32[512,256]{1,0:T(8,128)S(1)} collective-permute-done((f32[512,256]{1,0:T(8,128)S(1)}, f32[512,256]{1,0:T(8,128)S(1)}, u32[]{:S(2)}, u32[]{:S(2)}) %collective-permute-start.13) | collective-permute-done | bytes 524320 | tf_op jit(solution)/shard_map/ppermute | solution.py:104
  48.6 1.7 %solve.1 = (f32[1024,256]{1,0:T(8,128)}, f32[256,256]{1,0:T(8,128)S(1)}, f32[256,256]{1,0:T(8,128)S(1)}) custom-call(s32[4]{0:T(128)S(1)} %pad_add_fusion.place, f32[1024,256]{1,0:T(8,128)S(1)} %copy-done.26, f32[512,256]{1,0:T(8,128)S(1)} %get-tuple-element.29.rest_0_, f32[512,256]{1,0:T(8,128)S(1)} %collective-permute-done.rest_1_, ...), custom_call_target="tpu_custom_call" | custom-call | flops 536870912 | bytes 8388608 | tf_op jit(solution)/shard_map/solve/pallas_call | solution.py:37
  50.4 1.7 %collective-permute-start.14 = (f32[1024,256]{1,0:T(8,128)}, f32[1024,256]{1,0:T(8,128)}, u32[]{:S(2)}, u32[]{:S(2)}) collective-permute-start(f32[1024,256]{1,0:T(8,128)} %get-tuple-element.31), channel_id=1, source_target_pairs={{0,8},{1,9},{2,10},{3,11},{4,12},{5,13},{6,14},{7,15}} | collective-permute-start | bytes 3145736 | tf_op jit(solution)/shard_map/ppermute | solution.py:433
  52.1 1.3 collective-permute-start.15
  53.4 1.3 collective-permute-start.17
  54.7 14.0 %collective-permute-done.15 = f32[256,256]{1,0:T(8,128)} collective-permute-done((f32[256,256]{1,0:T(8,128)S(1)}, f32[256,256]{1,0:T(8,128)}, u32[]{:S(2)}, u32[]{:S(2)}) %collective-permute-start.15) | collective-permute-done | bytes 262176 | tf_op jit(solution)/shard_map/ppermute | solution.py:385
  68.7 2.0 %collective-permute-start.16 = (f32[256,256]{1,0:T(8,128)}, f32[256,256]{1,0:T(8,128)}, u32[]{:S(2)}, u32[]{:S(2)}) collective-permute-start(f32[256,256]{1,0:T(8,128)} %collective-permute-done.15), channel_id=1, source_target_pairs={{24,16},{25,17},{26,18},{27,19},{28,20},{29,21},{30,22},{31,23}} | collective-permute-start | bytes 786440 | tf_op jit(solution)/shard_map/ppermute | solution.py:386
  70.8 1.0 copy-done.7
  71.8 1.0 copy-done.9
  72.8 1.0 copy-done.11
  73.9 1.0 copy-done.13
  74.9 1.0 copy-done.15
  76.0 1.0 copy-done.17
  77.0 1.0 copy-done.19
  78.1 1.0 copy-done.21
  79.1 1.0 copy-done.23
  80.1 1.0 copy-done.25
  81.2 1.2 copy-done.27
  82.4 1.1 prepare.1
  83.5 1.3 fusion
  84.8 1.3 collective-permute-start.19
  86.1 1.3 collective-permute-start.18
  87.4 1.2 combine.1
  88.7 0.7 collective-permute-start.24
  89.3 1.3 collective-permute-start.22
  90.6 0.7 collective-permute-start.23
  91.4 0.5 collective-permute-done.18
  91.9 1.3 collective-permute-start.21
  93.3 1.3 collective-permute-start.20
  94.6 7.4 %collective-permute-done.22 = f32[256,256]{1,0:T(8,128)S(1)} collective-permute-done((f32[256,256]{1,0:T(8,128)S(1)}, f32[256,256]{1,0:T(8,128)S(1)}, u32[]{:S(2)}, u32[]{:S(2)}) %collective-permute-start.22) | collective-permute-done | bytes 262176 | tf_op jit(solution)/shard_map/ppermute | solution.py:390
  102.1 1.4 %collective-permute-start.26 = (f32[256,256]{1,0:T(8,128)S(1)}, f32[256,256]{1,0:T(8,128)S(1)}, u32[]{:S(2)}, u32[]{:S(2)}) collective-permute-start(f32[256,256]{1,0:T(8,128)S(1)} %add_select_fusion.2), channel_id=1, source_target_pairs={{0,160},{8,168},{16,176},{24,184},{1,161},{9,169},{17,177},{25,185... | collective-permute-start | bytes 786440 | tf_op jit(solution)/shard_map/ppermute | solution.py:395
  103.5 1.3 collective-permute-start.25
  104.9 3.9 %collective-permute-start.29 = (f32[256,256]{1,0:T(8,128)S(1)}, f32[256,256]{1,0:T(8,128)S(1)}, u32[]{:S(2)}, u32[]{:S(2)}) collective-permute-start(f32[256,256]{1,0:T(8,128)S(1)} %add_select_fusion.3.rest_16_), channel_id=1, source_target_pairs={{0,8},{8,16},{16,24},{24,0},{32,40},{40,48},{48,56},{56,32},{64,72... | collective-permute-start | bytes 786440 | tf_op jit(solution)/shard_map/ppermute | solution.py:406
  108.9 1.3 collective-permute-start.32
  110.2 1.3 collective-permute-start.31
  111.5 1.2 collective-permute-done.29.rest_20_
  112.7 3.8 %collective-permute-start.30 = (f32[128,256]{1,0:T(8,128)S(1)}, f32[128,256]{1,0:T(8,128)S(1)}, u32[]{:S(2)}, u32[]{:S(2)}) collective-permute-start(f32[128,256]{1,0:T(8,128)S(1)} %slice.26), channel_id=1, source_target_pairs={{0,8},{8,16},{16,24},{24,0},{32,40},{40,48},{48,56},{56,32},{64,72... | collective-permute-start | bytes 393224 | tf_op jit(solution)/shard_map/ppermute | solution.py:410
  116.5 0.1 collective-permute-start.28
  116.7 3.3 %collective-permute-start.34 = (f32[256,256]{1,0:T(8,128)S(1)}, f32[256,256]{1,0:T(8,128)S(1)}, u32[]{:S(2)}, u32[]{:S(2)}) collective-permute-start(f32[256,256]{1,0:T(8,128)S(1)} %add_select_fusion.rest_16_), channel_id=1, source_target_pairs={{0,8},{8,16},{16,24},{24,0},{32,40},{40,48},{48,56},{56,32},{64,72... | collective-permute-start | bytes 786440 | tf_op jit(solution)/shard_map/ppermute | solution.py:406
  120.0 0.4 collective-permute-done.30.rest_19_
  120.3 3.4 %collective-permute-done.28.rest_18_ = f32[128,256]{1,0:T(8,128)S(1)} collective-permute-done((f32[128,256]{1,0:T(8,128)S(1)}, f32[128,256]{1,0:T(8,128)S(1)}, u32[]{:S(2)}, u32[]{:S(2)}) %collective-permute-start.28) | collective-permute-done | bytes 131104 | tf_op jit(solution)/shard_map/ppermute | solution.py:410
  123.7 5.8 %update.1 = (f32[1024,256]{1,0:T(8,128)S(1)}, f32[2048,256]{1,0:T(8,128)}) custom-call(s32[4]{0:T(128)S(1)} %pad_add_fusion.place, f32[1024,256]{1,0:T(8,128)S(1)} %copy-done.28, f32[512,256]{1,0:T(8,128)} %copy-done, f32[512,256]{1,0:T(8,128)} %copy-done.4, f32[512,256]{1,0:T(8,128)} %copy-done.3, f32[512,256]{1,0:T(8,128)} %copy-done.16, ...), custom_call_target="tpu_custom_call" | custom-call | flops 16106127360 | bytes 8388608 | tf_op jit(solution)/shard_map/update/pallas_call | solution.py:37
  129.5 0.1 collective-permute-start.35
  129.6 3.2 %collective-permute-start.36 = (f32[128,256]{1,0:T(8,128)S(1)}, f32[128,256]{1,0:T(8,128)S(1)}, u32[]{:S(2)}, u32[]{:S(2)}) collective-permute-start(f32[128,256]{1,0:T(8,128)S(1)} %slice.23), channel_id=1, source_target_pairs={{0,8},{8,16},{16,24},{24,0},{32,40},{40,48},{48,56},{56,32},{64,72... | collective-permute-start | bytes 393224 | tf_op jit(solution)/shard_map/ppermute | solution.py:410
  132.9 4.7 %most.1 = (f32[1024,256]{1,0:T(8,128)S(1)}, f32[2048,256]{1,0:T(8,128)}, f32[1024,256]{1,0:T(8,128)S(1)}) custom-call(s32[4]{0:T(128)S(1)} %pad_add_fusion.place, f32[1024,256]{1,0:T(8,128)S(1)} %get-tuple-element.49.target, f32[512,256]{1,0:T(8,128)} %copy-done, f32[512,256]{1,0:T(8,128)} %copy-done.4, ...), custom_call_target="tpu_custom_call", output_to_operand_aliasing={{1}: (21, {})} | custom-call | flops 1610612736 | bytes 8388608 | tf_op jit(solution)/shard_map/most/pallas_call | solution.py:37
  137.6 2.5 %last.1 = (f32[1024,256]{1,0:T(8,128)}, f32[2048,256]{1,0:T(8,128)}) custom-call(s32[4]{0:T(128)S(1)} %pad_add_fusion.place, f32[1024,256]{1,0:T(8,128)S(1)} %get-tuple-element.53.target, f32[1024,256]{1,0:T(8,128)S(1)} %get-tuple-element.54.block, f32[128,256]{1,0:T(8,128)S(1)} %collective-permute-done.35.upper, ...), custom_call_target="tpu_custom_call", output_to_operand_aliasing={{1}: (5, {})} | custom-call | flops 536870912 | bytes 8388608 | tf_op jit(solution)/shard_map/last/pallas_call | solution.py:37
  (88 shorter events, 0.5 us)
Async XLA Ops:
  0.7 48.0 %copy-start.26 = (f32[1024,256]{1,0:T(8,128)S(1)}, f32[1024,256]{1,0:T(8,128)}, u32[]{:S(2)}) copy-start(f32[1024,256]{1,0:T(8,128)} %target.1) | copy-start | bytes 3145732
  0.7 1.3 copy-start.29
  2.7 68.1 %copy-start = (f32[512,256]{1,0:T(8,128)}, f32[512,256]{1,0:T(8,128)S(1)}, u32[]{:S(2)}) copy-start(f32[512,256]{1,0:T(8,128)S(1)} %get-tuple-element.29.rest_0_) | copy-start | bytes 1572868
  2.7 68.1 %copy-start.1 = (f32[512,256]{1,0:T(8,128)}, f32[512,256]{1,0:T(8,128)S(1)}, u32[]{:S(2)}) copy-start(f32[512,256]{1,0:T(8,128)S(1)} %get-tuple-element.30.rest_8_) | copy-start | bytes 1572868
  2.7 17.9 %collective-permute-start.3 = (f32[512,256]{1,0:T(8,128)S(1)}, f32[512,256]{1,0:T(8,128)S(1)}, u32[]{:S(2)}, u32[]{:S(2)}) collective-permute-start(f32[512,256]{1,0:T(8,128)S(1)} %get-tuple-element.29.rest_0_), channel_id=1, source_target_pairs={{0,2},{1,3},{8,10},{9,11},{10,12},{11,13},{12,14},{13,15},{14,8},{... | collective-permute-start | bytes 1572872 | tf_op jit(solution)/shard_map/ppermute | solution.py:108
  6.2 16.7 %collective-permute-start.1 = (f32[512,256]{1,0:T(8,128)S(1)}, f32[512,256]{1,0:T(8,128)S(1)}, u32[]{:S(2)}, u32[]{:S(2)}) collective-permute-start(f32[512,256]{1,0:T(8,128)S(1)} %get-tuple-element.29.rest_0_), channel_id=1, source_target_pairs={{0,6},{1,7},{8,14},{9,15},{10,8},{11,9},{12,10},{13,11},{14,12},{1... | collective-permute-start | bytes 1572872 | tf_op jit(solution)/shard_map/ppermute | solution.py:109
  9.8 13.2 %collective-permute-start = (f32[512,256]{1,0:T(8,128)S(1)}, f32[512,256]{1,0:T(8,128)S(1)}, u32[]{:S(2)}, u32[]{:S(2)}) collective-permute-start(f32[512,256]{1,0:T(8,128)S(1)} %get-tuple-element.29.rest_0_), channel_id=1, source_target_pairs={{0,1},{1,0},{2,3},{3,2},{4,5},{5,4},{6,7},{7,6},{8,9},{9,8},{10,11... | collective-permute-start | bytes 1572872 | tf_op jit(solution)/shard_map/ppermute | solution.py:104
  9.9 20.9 %collective-permute-start.10 = (f32[512,256]{1,0:T(8,128)S(1)}, f32[512,256]{1,0:T(8,128)S(1)}, u32[]{:S(2)}, u32[]{:S(2)}) collective-permute-start(f32[512,256]{1,0:T(8,128)S(1)} %get-tuple-element.30.rest_8_), channel_id=1, source_target_pairs={{0,2},{1,3},{2,4},{3,5},{8,10},{9,11},{10,12},{11,13},{12,14},{13,... | collective-permute-start | bytes 1572872 | tf_op jit(solution)/shard_map/ppermute | solution.py:108
  12.1 22.0 %collective-permute-start.8 = (f32[512,256]{1,0:T(8,128)S(1)}, f32[512,256]{1,0:T(8,128)S(1)}, u32[]{:S(2)}, u32[]{:S(2)}) collective-permute-start(f32[512,256]{1,0:T(8,128)S(1)} %get-tuple-element.30.rest_8_), channel_id=1, source_target_pairs={{0,6},{1,7},{2,0},{3,1},{8,14},{9,15},{10,8},{11,9},{12,10},{13,11... | collective-permute-start | bytes 1572872 | tf_op jit(solution)/shard_map/ppermute | solution.py:109
  20.6 50.1 %copy-start.2 = (f32[512,256]{1,0:T(8,128)}, f32[512,256]{1,0:T(8,128)S(1)}, u32[]{:S(2)}) copy-start(f32[512,256]{1,0:T(8,128)S(1)} %collective-permute-done.3.rest_4_) | copy-start | bytes 1572868
  20.6 13.6 %collective-permute-start.7 = (f32[512,256]{1,0:T(8,128)S(1)}, f32[512,256]{1,0:T(8,128)S(1)}, u32[]{:S(2)}, u32[]{:S(2)}) collective-permute-start(f32[512,256]{1,0:T(8,128)S(1)} %get-tuple-element.30.rest_8_), channel_id=1, source_target_pairs={{0,1},{1,0},{2,3},{3,2},{4,5},{5,4},{6,7},{7,6},{8,9},{9,8},{10,11... | collective-permute-start | bytes 1572872 | tf_op jit(solution)/shard_map/ppermute | solution.py:104
  22.9 47.8 %copy-start.3 = (f32[512,256]{1,0:T(8,128)}, f32[512,256]{1,0:T(8,128)S(1)}, u32[]{:S(2)}) copy-start(f32[512,256]{1,0:T(8,128)S(1)} %collective-permute-done.1.rest_2_) | copy-start | bytes 1572868
  22.9 11.8 %collective-permute-start.4 = (f32[512,256]{1,0:T(8,128)S(1)}, f32[512,256]{1,0:T(8,128)S(1)}, u32[]{:S(2)}, u32[]{:S(2)}) collective-permute-start(f32[512,256]{1,0:T(8,128)S(1)} %collective-permute-done.3.rest_4_), channel_id=1, source_target_pairs={{0,1},{1,0},{2,3},{3,2},{4,5},{5,4},{6,7},{7,6},{8,9},{9,8},{10,11... | collective-permute-start | bytes 1572872 | tf_op jit(solution)/shard_map/ppermute | solution.py:104
  22.9 47.8 %copy-start.4 = (f32[512,256]{1,0:T(8,128)}, f32[512,256]{1,0:T(8,128)S(1)}, u32[]{:S(2)}) copy-start(f32[512,256]{1,0:T(8,128)S(1)} %collective-permute-done.rest_1_) | copy-start | bytes 1572868
  22.9 21.0 %collective-permute-start.5 = (f32[512,256]{1,0:T(8,128)S(1)}, f32[512,256]{1,0:T(8,128)S(1)}, u32[]{:S(2)}, u32[]{:S(2)}) collective-permute-start(f32[512,256]{1,0:T(8,128)S(1)} %collective-permute-done.1.rest_2_), channel_id=1, source_target_pairs={{6,4},{7,5},{8,14},{9,15},{10,8},{11,9},{12,10},{13,11},{14,12},{1... | collective-permute-start | bytes 1572872 | tf_op jit(solution)/shard_map/ppermute | solution.py:114
  30.8 40.0 %copy-start.5 = (f32[512,256]{1,0:T(8,128)}, f32[512,256]{1,0:T(8,128)S(1)}, u32[]{:S(2)}) copy-start(f32[512,256]{1,0:T(8,128)S(1)} %collective-permute-done.10.rest_12_) | copy-start | bytes 1572868
  30.8 16.0 %collective-permute-start.12 = (f32[512,256]{1,0:T(8,128)S(1)}, f32[512,256]{1,0:T(8,128)S(1)}, u32[]{:S(2)}, u32[]{:S(2)}) collective-permute-start(f32[512,256]{1,0:T(8,128)S(1)} %collective-permute-done.10.rest_12_), channel_id=1, source_target_pairs={{2,4},{3,5},{4,6},{5,7},{8,10},{9,11},{10,12},{11,13},{12,14},{13,... | collective-permute-start | bytes 1572872 | tf_op jit(solution)/shard_map/ppermute | solution.py:115
  34.2 16.2 %copy-start.6 = (f32[512,256]{1,0:T(8,128)}, f32[512,256]{1,0:T(8,128)S(1)}, u32[]{:S(2)}) copy-start(f32[512,256]{1,0:T(8,128)S(1)} %collective-permute-done.8.rest_10_) | copy-start | bytes 1572868
  34.2 12.6 %collective-permute-start.2 = (f32[512,256]{1,0:T(8,128)S(1)}, f32[512,256]{1,0:T(8,128)S(1)}, u32[]{:S(2)}, u32[]{:S(2)}) collective-permute-start(f32[512,256]{1,0:T(8,128)S(1)} %collective-permute-done.1.rest_2_), channel_id=1, source_target_pairs={{0,1},{1,0},{2,3},{3,2},{4,5},{5,4},{6,7},{7,6},{8,9},{9,8},{10,11... | collective-permute-start | bytes 1572872 | tf_op jit(solution)/shard_map/ppermute | solution.py:104
  34.2 16.2 %copy-start.8 = (f32[512,256]{1,0:T(8,128)}, f32[512,256]{1,0:T(8,128)S(1)}, u32[]{:S(2)}) copy-start(f32[512,256]{1,0:T(8,128)S(1)} %collective-permute-done.7.rest_9_) | copy-start | bytes 1572868
  34.2 12.6 %collective-permute-start.11 = (f32[512,256]{1,0:T(8,128)S(1)}, f32[512,256]{1,0:T(8,128)S(1)}, u32[]{:S(2)}, u32[]{:S(2)}) collective-permute-start(f32[512,256]{1,0:T(8,128)S(1)} %collective-permute-done.10.rest_12_), channel_id=1, source_target_pairs={{0,1},{1,0},{2,3},{3,2},{4,5},{5,4},{6,7},{7,6},{8,9},{9,8},{10,11... | collective-permute-start | bytes 1572872 | tf_op jit(solution)/shard_map/ppermute | solution.py:104
  34.7 15.7 %copy-start.10 = (f32[512,256]{1,0:T(8,128)}, f32[512,256]{1,0:T(8,128)S(1)}, u32[]{:S(2)}) copy-start(f32[512,256]{1,0:T(8,128)S(1)} %collective-permute-done.4.rest_5_) | copy-start | bytes 1572868
  34.7 12.1 %collective-permute-start.9 = (f32[512,256]{1,0:T(8,128)S(1)}, f32[512,256]{1,0:T(8,128)S(1)}, u32[]{:S(2)}, u32[]{:S(2)}) collective-permute-start(f32[512,256]{1,0:T(8,128)S(1)} %collective-permute-done.8.rest_10_), channel_id=1, source_target_pairs={{0,1},{1,0},{2,3},{3,2},{4,5},{5,4},{6,7},{7,6},{8,9},{9,8},{10,11... | collective-permute-start | bytes 1572872 | tf_op jit(solution)/shard_map/ppermute | solution.py:104
  43.9 6.4 %copy-start.12 = (f32[512,256]{1,0:T(8,128)}, f32[512,256]{1,0:T(8,128)S(1)}, u32[]{:S(2)}) copy-start(f32[512,256]{1,0:T(8,128)S(1)} %collective-permute-done.5.rest_6_) | copy-start | bytes 1572868
  43.9 2.9 %collective-permute-start.6 = (f32[512,256]{1,0:T(8,128)S(1)}, f32[512,256]{1,0:T(8,128)S(1)}, u32[]{:S(2)}, u32[]{:S(2)}) collective-permute-start(f32[512,256]{1,0:T(8,128)S(1)} %collective-permute-done.5.rest_6_), channel_id=1, source_target_pairs={{0,1},{1,0},{2,3},{3,2},{4,5},{5,4},{6,7},{7,6},{8,9},{9,8},{10,11... | collective-permute-start | bytes 1572872 | tf_op jit(solution)/shard_map/ppermute | solution.py:104
  46.7 3.6 %copy-start.14 = (f32[512,256]{1,0:T(8,128)}, f32[512,256]{1,0:T(8,128)S(1)}, u32[]{:S(2)}) copy-start(f32[512,256]{1,0:T(8,128)S(1)} %collective-permute-done.12.rest_14_) | copy-start | bytes 1572868
  46.7 1.9 %collective-permute-start.13 = (f32[512,256]{1,0:T(8,128)S(1)}, f32[512,256]{1,0:T(8,128)S(1)}, u32[]{:S(2)}, u32[]{:S(2)}) collective-permute-start(f32[512,256]{1,0:T(8,128)S(1)} %collective-permute-done.12.rest_14_), channel_id=1, source_target_pairs={{0,1},{1,0},{2,3},{3,2},{4,5},{5,4},{6,7},{7,6},{8,9},{9,8},{10,11... | collective-permute-start | bytes 1572872 | tf_op jit(solution)/shard_map/ppermute | solution.py:104
  46.7 3.6 %copy-start.16 = (f32[512,256]{1,0:T(8,128)}, f32[512,256]{1,0:T(8,128)S(1)}, u32[]{:S(2)}) copy-start(f32[512,256]{1,0:T(8,128)S(1)} %collective-permute-done.2.rest_3_) | copy-start | bytes 1572868
  46.8 3.6 %copy-start.18 = (f32[512,256]{1,0:T(8,128)}, f32[512,256]{1,0:T(8,128)S(1)}, u32[]{:S(2)}) copy-start(f32[512,256]{1,0:T(8,128)S(1)} %collective-permute-done.11.rest_13_) | copy-start | bytes 1572868
  46.8 3.6 %copy-start.20 = (f32[512,256]{1,0:T(8,128)}, f32[512,256]{1,0:T(8,128)S(1)}, u32[]{:S(2)}) copy-start(f32[512,256]{1,0:T(8,128)S(1)} %collective-permute-done.9.rest_11_) | copy-start | bytes 1572868
  46.8 3.6 %copy-start.22 = (f32[512,256]{1,0:T(8,128)}, f32[512,256]{1,0:T(8,128)S(1)}, u32[]{:S(2)}) copy-start(f32[512,256]{1,0:T(8,128)S(1)} %collective-permute-done.6.rest_7_) | copy-start | bytes 1572868
  48.6 1.8 %copy-start.24 = (f32[512,256]{1,0:T(8,128)}, f32[512,256]{1,0:T(8,128)S(1)}, u32[]{:S(2)}) copy-start(f32[512,256]{1,0:T(8,128)S(1)} %collective-permute-done.13.rest_15_) | copy-start | bytes 1572868
  50.4 33.1 %collective-permute-start.14 = (f32[1024,256]{1,0:T(8,128)}, f32[1024,256]{1,0:T(8,128)}, u32[]{:S(2)}, u32[]{:S(2)}) collective-permute-start(f32[1024,256]{1,0:T(8,128)} %get-tuple-element.31), channel_id=1, source_target_pairs={{0,8},{1,9},{2,10},{3,11},{4,12},{5,13},{6,14},{7,15}} | collective-permute-start | bytes 3145736 | tf_op jit(solution)/shard_map/ppermute | solution.py:433
  52.1 16.6 %collective-permute-start.15 = (f32[256,256]{1,0:T(8,128)S(1)}, f32[256,256]{1,0:T(8,128)}, u32[]{:S(2)}, u32[]{:S(2)}) collective-permute-start(f32[256,256]{1,0:T(8,128)S(1)} %get-tuple-element.32), channel_id=1, source_target_pairs={{0,24},{1,25},{2,26},{3,27},{4,28},{5,29},{6,30},{7,31}} | collective-permute-start | bytes 786440 | tf_op jit(solution)/shard_map/ppermute | solution.py:385
  53.4 30.1 %collective-permute-start.17 = (f32[256,256]{1,0:T(8,128)S(1)}, f32[256,256]{1,0:T(8,128)}, u32[]{:S(2)}, u32[]{:S(2)}) collective-permute-start(f32[256,256]{1,0:T(8,128)S(1)} %get-tuple-element.33), channel_id=1, source_target_pairs={{0,24},{1,25},{2,26},{3,27},{4,28},{5,29},{6,30},{7,31}} | collective-permute-start | bytes 786440 | tf_op jit(solution)/shard_map/ppermute | solution.py:386
  68.7 14.7 %collective-permute-start.16 = (f32[256,256]{1,0:T(8,128)}, f32[256,256]{1,0:T(8,128)}, u32[]{:S(2)}, u32[]{:S(2)}) collective-permute-start(f32[256,256]{1,0:T(8,128)} %collective-permute-done.15), channel_id=1, source_target_pairs={{24,16},{25,17},{26,18},{27,19},{28,20},{29,21},{30,22},{31,23}} | collective-permute-start | bytes 786440 | tf_op jit(solution)/shard_map/ppermute | solution.py:386
  70.8 1.0 copy-start.7
  71.8 1.0 copy-start.9
  72.8 1.0 copy-start.11
  73.9 1.0 copy-start.13
  74.9 1.0 copy-start.15
  76.0 1.0 copy-start.17
  77.0 1.0 copy-start.19
  81.2 1.2 copy-start.27
  84.8 6.6 %collective-permute-start.19 = (f32[256,256]{1,0:T(8,128)S(1)}, f32[256,256]{1,0:T(8,128)S(1)}, u32[]{:S(2)}, u32[]{:S(2)}) collective-permute-start(f32[256,256]{1,0:T(8,128)S(1)} %fusion), channel_id=1, source_target_pairs={{0,160},{8,168},{16,176},{24,184},{1,161},{9,169},{17,177},{25,185... | collective-permute-start | bytes 786440 | tf_op jit(solution)/shard_map/ppermute | solution.py:395
  86.1 5.8 %collective-permute-start.18 = (f32[256,256]{1,0:T(8,128)S(1)}, f32[256,256]{1,0:T(8,128)S(1)}, u32[]{:S(2)}, u32[]{:S(2)}) collective-permute-start(f32[256,256]{1,0:T(8,128)S(1)} %fusion), channel_id=1, source_target_pairs={{0,96},{8,104},{16,112},{24,120},{1,97},{9,105},{17,113},{25,121},... | collective-permute-start | bytes 786440 | tf_op jit(solution)/shard_map/ppermute | solution.py:394
  88.7 5.9 %collective-permute-start.24 = (f32[256,256]{1,0:T(8,128)S(1)}, f32[256,256]{1,0:T(8,128)S(1)}, u32[]{:S(2)}, u32[]{:S(2)}) collective-permute-start(f32[256,256]{1,0:T(8,128)S(1)} %get-tuple-element.39), channel_id=1, source_target_pairs={{8,16},{9,17},{10,18},{11,19},{12,20},{13,21},{14,22},{15,23}} | collective-permute-start | bytes 786440 | tf_op jit(solution)/shard_map/ppermute | solution.py:390
  89.3 12.6 %collective-permute-start.22 = (f32[256,256]{1,0:T(8,128)S(1)}, f32[256,256]{1,0:T(8,128)S(1)}, u32[]{:S(2)}, u32[]{:S(2)}) collective-permute-start(f32[256,256]{1,0:T(8,128)S(1)} %get-tuple-element.40), channel_id=1, source_target_pairs={{8,24},{9,25},{10,26},{11,27},{12,28},{13,29},{14,30},{15,31}} | collective-permute-start | bytes 786440 | tf_op jit(solution)/shard_map/ppermute | solution.py:390
  90.6 11.3 %collective-permute-start.23 = (f32[256,256]{1,0:T(8,128)S(1)}, f32[256,256]{1,0:T(8,128)S(1)}, u32[]{:S(2)}, u32[]{:S(2)}) collective-permute-start(f32[256,256]{1,0:T(8,128)S(1)} %get-tuple-element.41), channel_id=1, source_target_pairs={{8,0},{9,1},{10,2},{11,3},{12,4},{13,5},{14,6},{15,7}} | collective-permute-start | bytes 786440 | tf_op jit(solution)/shard_map/ppermute | solution.py:390
  91.9 12.9 %collective-permute-start.21 = (f32[256,256]{1,0:T(8,128)S(1)}, f32[256,256]{1,0:T(8,128)S(1)}, u32[]{:S(2)}, u32[]{:S(2)}) collective-permute-start(f32[256,256]{1,0:T(8,128)S(1)} %add_select_fusion.4), channel_id=1, source_target_pairs={{0,224},{8,232},{16,240},{24,248},{96,64},{104,72},{112,80},{120,8... | collective-permute-start | bytes 786440 | tf_op jit(solution)/shard_map/ppermute | solution.py:401
  93.3 11.6 %collective-permute-start.20 = (f32[256,256]{1,0:T(8,128)S(1)}, f32[256,256]{1,0:T(8,128)S(1)}, u32[]{:S(2)}, u32[]{:S(2)}) collective-permute-start(f32[256,256]{1,0:T(8,128)S(1)} %add_select_fusion.4), channel_id=1, source_target_pairs={{0,32},{8,40},{16,48},{24,56},{96,128},{104,136},{112,144},{120,15... | collective-permute-start | bytes 786440 | tf_op jit(solution)/shard_map/ppermute | solution.py:400
  102.1 21.7 %copy-start.28 = (f32[1024,256]{1,0:T(8,128)S(1)}, f32[1024,256]{1,0:T(8,128)}, u32[]{:S(2)}) copy-start(f32[1024,256]{1,0:T(8,128)} %target.1) | copy-start | bytes 3145732
  102.1 6.7 %collective-permute-start.26 = (f32[256,256]{1,0:T(8,128)S(1)}, f32[256,256]{1,0:T(8,128)S(1)}, u32[]{:S(2)}, u32[]{:S(2)}) collective-permute-start(f32[256,256]{1,0:T(8,128)S(1)} %add_select_fusion.2), channel_id=1, source_target_pairs={{0,160},{8,168},{16,176},{24,184},{1,161},{9,169},{17,177},{25,185... | collective-permute-start | bytes 786440 | tf_op jit(solution)/shard_map/ppermute | solution.py:395
  103.5 5.3 %collective-permute-start.25 = (f32[256,256]{1,0:T(8,128)S(1)}, f32[256,256]{1,0:T(8,128)S(1)}, u32[]{:S(2)}, u32[]{:S(2)}) collective-permute-start(f32[256,256]{1,0:T(8,128)S(1)} %add_select_fusion.2), channel_id=1, source_target_pairs={{0,96},{8,104},{16,112},{24,120},{1,97},{9,105},{17,113},{25,121},... | collective-permute-start | bytes 786440 | tf_op jit(solution)/shard_map/ppermute | solution.py:394
  104.9 7.8 %collective-permute-start.29 = (f32[256,256]{1,0:T(8,128)S(1)}, f32[256,256]{1,0:T(8,128)S(1)}, u32[]{:S(2)}, u32[]{:S(2)}) collective-permute-start(f32[256,256]{1,0:T(8,128)S(1)} %add_select_fusion.3.rest_16_), channel_id=1, source_target_pairs={{0,8},{8,16},{16,24},{24,0},{32,40},{40,48},{48,56},{56,32},{64,72... | collective-permute-start | bytes 786440 | tf_op jit(solution)/shard_map/ppermute | solution.py:406
  108.8 7.7 %collective-permute-start.27 = (f32[256,256]{1,0:T(8,128)S(1)}, f32[256,256]{1,0:T(8,128)S(1)}, u32[]{:S(2)}, u32[]{:S(2)}) collective-permute-start(f32[256,256]{1,0:T(8,128)S(1)} %add_select_fusion.3.rest_16_), channel_id=1, source_target_pairs={{8,0},{16,8},{24,16},{0,24},{40,32},{48,40},{56,48},{32,56},{72,64... | collective-permute-start | bytes 786440 | tf_op jit(solution)/shard_map/ppermute | solution.py:406
  108.9 7.7 %collective-permute-start.32 = (f32[256,256]{1,0:T(8,128)S(1)}, f32[256,256]{1,0:T(8,128)S(1)}, u32[]{:S(2)}, u32[]{:S(2)}) collective-permute-start(f32[256,256]{1,0:T(8,128)S(1)} %add_select_fusion.1), channel_id=1, source_target_pairs={{0,224},{8,232},{16,240},{24,248},{96,64},{104,72},{112,80},{120,8... | collective-permute-start | bytes 786440 | tf_op jit(solution)/shard_map/ppermute | solution.py:401
  110.2 6.4 %collective-permute-start.31 = (f32[256,256]{1,0:T(8,128)S(1)}, f32[256,256]{1,0:T(8,128)S(1)}, u32[]{:S(2)}, u32[]{:S(2)}) collective-permute-start(f32[256,256]{1,0:T(8,128)S(1)} %add_select_fusion.1), channel_id=1, source_target_pairs={{0,32},{8,40},{16,48},{24,56},{96,128},{104,136},{112,144},{120,15... | collective-permute-start | bytes 786440 | tf_op jit(solution)/shard_map/ppermute | solution.py:400
  112.7 7.6 %collective-permute-start.30 = (f32[128,256]{1,0:T(8,128)S(1)}, f32[128,256]{1,0:T(8,128)S(1)}, u32[]{:S(2)}, u32[]{:S(2)}) collective-permute-start(f32[128,256]{1,0:T(8,128)S(1)} %slice.26), channel_id=1, source_target_pairs={{0,8},{8,16},{16,24},{24,0},{32,40},{40,48},{48,56},{56,32},{64,72... | collective-permute-start | bytes 393224 | tf_op jit(solution)/shard_map/ppermute | solution.py:410
  116.5 7.2 %collective-permute-start.28 = (f32[128,256]{1,0:T(8,128)S(1)}, f32[128,256]{1,0:T(8,128)S(1)}, u32[]{:S(2)}, u32[]{:S(2)}) collective-permute-start(f32[128,256]{1,0:T(8,128)S(1)} %slice.25), channel_id=1, source_target_pairs={{8,0},{16,8},{24,16},{0,24},{40,32},{48,40},{56,48},{32,56},{72,64... | collective-permute-start | bytes 393224 | tf_op jit(solution)/shard_map/ppermute | solution.py:410
  116.7 12.8 %collective-permute-start.34 = (f32[256,256]{1,0:T(8,128)S(1)}, f32[256,256]{1,0:T(8,128)S(1)}, u32[]{:S(2)}, u32[]{:S(2)}) collective-permute-start(f32[256,256]{1,0:T(8,128)S(1)} %add_select_fusion.rest_16_), channel_id=1, source_target_pairs={{0,8},{8,16},{16,24},{24,0},{32,40},{40,48},{48,56},{56,32},{64,72... | collective-permute-start | bytes 786440 | tf_op jit(solution)/shard_map/ppermute | solution.py:406
  120.0 9.5 %collective-permute-start.33 = (f32[256,256]{1,0:T(8,128)S(1)}, f32[256,256]{1,0:T(8,128)S(1)}, u32[]{:S(2)}, u32[]{:S(2)}) collective-permute-start(f32[256,256]{1,0:T(8,128)S(1)} %add_select_fusion.rest_16_), channel_id=1, source_target_pairs={{8,0},{16,8},{24,16},{0,24},{40,32},{48,40},{56,48},{32,56},{72,64... | collective-permute-start | bytes 786440 | tf_op jit(solution)/shard_map/ppermute | solution.py:406
  129.5 8.1 %collective-permute-start.35 = (f32[128,256]{1,0:T(8,128)S(1)}, f32[128,256]{1,0:T(8,128)S(1)}, u32[]{:S(2)}, u32[]{:S(2)}) collective-permute-start(f32[128,256]{1,0:T(8,128)S(1)} %slice.22), channel_id=1, source_target_pairs={{8,0},{16,8},{24,16},{0,24},{40,32},{48,40},{56,48},{32,56},{72,64... | collective-permute-start | bytes 393224 | tf_op jit(solution)/shard_map/ppermute | solution.py:410
  129.6 8.0 %collective-permute-start.36 = (f32[128,256]{1,0:T(8,128)S(1)}, f32[128,256]{1,0:T(8,128)S(1)}, u32[]{:S(2)}, u32[]{:S(2)}) collective-permute-start(f32[128,256]{1,0:T(8,128)S(1)} %slice.23), channel_id=1, source_target_pairs={{0,8},{8,16},{16,24},{24,0},{32,40},{40,48},{48,56},{56,32},{64,72... | collective-permute-start | bytes 393224 | tf_op jit(solution)/shard_map/ppermute | solution.py:410
  (3 other events, 3.1 us)

commit v6 on v5

--- a/solution.py
+++ b/solution.py
@@ -19,6 +19,8 @@
 F32 = jnp.float32
 BF16 = jnp.bfloat16
 BOTH = ("row", "col")
+AROUND = 160
+DIRECT = NB - 2 * AROUND
 UPDATE_COST = 60
 
 
@@ -157,7 +159,7 @@
 
 def solve_kernel(place, rhs, *rest):
     tops, bottoms, rest = rest[: len(CHUNK)], rest[len(CHUNK) : 2 * len(CHUNK)], rest[2 * len(CHUNK) :]
-    whole, two, three, triangle, rhs_buf, top_sem, bottom_sem, rhs_sem = rest
+    direct, up, down, two, three, triangle, rhs_buf, top_sem, bottom_sem, rhs_sem = rest
 
     @pl.when(place[ROW] == 0)
     def _():
@@ -174,7 +176,10 @@
         copy.wait()
 
         def store(i, value):
-            whole[pl.ds(i * Q, Q), :] = value
+            for array, start, count in ((direct, 0, DIRECT), (up, DIRECT, AROUND), (down, DIRECT + AROUND, AROUND)):
+                low, high = max(start, i * Q), min(start + count, (i + 1) * Q)
+                if low < high:
+                    array[pl.ds(low - start, high - low), :] = value[low - i * Q : high - i * Q]
             if i >= 2:
                 (two, three)[i - 2][...] = value
 
@@ -189,7 +194,7 @@
         pltpu.SemaphoreType.DMA((COLS,)),
         pltpu.SemaphoreType.DMA,
     ]
-    shapes = [((NB, Q), F32), ((Q, Q), F32), ((Q, Q), F32)]
+    shapes = [((rows, Q), F32) for rows in (DIRECT, AROUND, AROUND, Q, Q)]
     return call(solve_kernel, "solve", shapes, scratch, (place, rhs, *tops, *bottoms))
 
 
@@ -231,21 +236,22 @@
         pltpu.SemaphoreType.DMA,
     ]
     shapes = [((NB, NB), BF16)] * 2 + [((NB, Q), F32)]
-    return call(prepare_kernel, "prepare", shapes, scratch, (place, rhs, *tops, *bottoms), vmem=32)
-
-
-def combine_kernel(place, w_high, w_low, y_ref, first, *out):
+    held = [pltpu.with_memory_space_constraint(x, pltpu.HBM) for x in (*tops, *bottoms)]
+    return call(prepare_kernel, "prepare", shapes, scratch, (place, rhs, *held), vmem=32)
+
+
+def combine_kernel(place, w_high, w_low, y_ref, direct, up, down, *out):
     @pl.when(place[ROW] == 1)
     def _():
-        solved = halves(first[...])
+        solved = halves(jnp.concatenate([direct[...], up[...], down[...]], axis=0))
         for i in range(PARTS):
             rows = pl.ds(i * Q, Q)
             out[i][...] = y_ref[rows, :] - product((w_high[rows, :], w_low[rows, :]), solved)
 
 
-def combine(place, w_high, w_low, y_value, first):
-    vmem = [pl.BlockSpec(memory_space=pltpu.VMEM)] * 4
-    operands = (place, w_high, w_low, y_value, first)
+def combine(place, w_high, w_low, y_value, *first):
+    vmem = [pl.BlockSpec(memory_space=pltpu.VMEM)] * 6
+    operands = (place, w_high, w_low, y_value, *first)
     return call(combine_kernel, "combine", [((Q, Q), F32)] * PARTS, [], operands, in_specs=vmem)
 
 
@@ -429,14 +435,21 @@
     tops = both_cores((top, *top_near, top_far))
     bottoms = both_cores((bottom, *bottom_near, bottom_far))
 
-    first, two, three = solve(place(), rhs, tops, bottoms)
+    first, up, down, two, three = solve(place(), rhs, tops, bottoms)
+    last_z = (ZS - 1) * XS
+    up = up_sent = lax.ppermute(up, "row", [(0, XS)])
+    down = down_sent = lax.ppermute(down, "row", [(0, last_z)])
+    for a, b in ((XS, XS + 1), (XS + 1, 1)):
+        up = lax.ppermute(up, "row", [(a, b)])
+    for a, b in ((last_z, last_z + 1), (last_z + 1, 1)):
+        down = lax.ppermute(down, "row", [(a, b)])
     ahead = lax.ppermute(first, "row", [(0, 1)])
-    two_ahead, three_ahead = scatter_first(two, three)
+    two_ahead, three_ahead = scatter_first(after(two, down_sent), after(three, up_sent))
     w_high, w_low, y_value = prepare(place(), rhs, tops, bottoms)
     mine_one = jnp.where(row == 1, ahead[Q : 2 * Q], two_ahead + three_ahead)
-    mine_one = far_z(after(jnp.where(row == 0, first[:Q], mine_one), w_high), z)
-
-    pieces = combine(place(), w_high, w_low, y_value, ahead)
+    mine_one = far_z(after(jnp.where(row == 0, first[:Q], mine_one), w_high, up, down), z)
+
+    pieces = combine(place(), w_high, w_low, y_value, ahead, up, down)
     got = scatter_second(pieces)
     mine_one = near_z(after(mine_one, *pieces), z)
     mine_two = jnp.where(row == 1, pieces[0], got[0] + got[1] + got[2])

time: 142 us -> 141 us (level)
  local copies, waits for them, and re-layouts: 13 us -> 2.63 us
  waiting for transfers between devices: 51 us -> 58.8 us
  starting transfers between devices: 55.6 us -> 59 us
    unnamed x60 -> x40, local copies, waits for them, and re-layouts: 13 us -> 2.59 us
    ppermute x0 -> x6, starting transfers between devices: none -> 4.03 us  [the longest x2 1.34 us: body(): up = lax.ppermute(up, 'row', [(a, b)])]
    ppermute x3, waiting for transfers between devices: 7.41 us -> 11.3 us  [scatter_second(): lax.ppermute(pieces[i], 'row', [(1, (1 + i) % XS)])]
    ppermute x1, waiting for transfers between devices: 14 us -> 16.6 us  [scatter_first(): relay = lax.ppermute(two, 'row', [(0, 3)])]
  transfers between devices with their start and end apart: 37 -> 43, of which waited for: 13 -> 13; matrix products, arithmetic and copies ran while one was open for 0% -> 1% of each run, Pallas kernels for 9% -> 9%
where the time goes in v6:
time: 141 us; the launch traced here: 140 us
  starting transfers between devices  59 us (42%)
  waiting for transfers between devices  58.8 us (42%)
  Pallas kernels  16.8 us (12%)
  local copies, waits for them, and re-layouts  2.63 us (2%)
  between operations  1.64 us (1%)
    pallas_call x7, Pallas kernels, call(): pl.pallas_call(kernel, out_shape=[(pltpu.HBM if len(shape) == 3 else jax....  16.8 us
    ppermute x1, waiting for transfers between devices, scatter_first(): relay = lax.ppermute(two, 'row', [(0, 3)])  16.6 us
    ppermute x3, waiting for transfers between devices, scatter_second(): lax.ppermute(pieces[i], 'row', [(1, (1 + i) % XS)])  11.3 us
    ppermute x1, waiting for transfers between devices, far_chip(): return lax.ppermute(ahead, BOTH, pairs(-1, 1, has))  9.14 us
    ppermute x2, starting transfers between devices, near_chips(): return (lax.ppermute(chunk, BOTH, pairs(-1, 0, has)), behind)  8.35 us
    ppermute x2, starting transfers between devices, over_x(): lax.ppermute(mine, 'row', TO_NEXT)  8 us
    ppermute x2, starting transfers between devices, across_x(): lax.ppermute(before[Q // 2:], 'row', TO_NEXT)  6.99 us
    ppermute x2, waiting for transfers between devices, near_chips(): behind = lax.ppermute(chunk, BOTH, pairs(1, 0, has))  6.71 us
  transfers between devices with their start and end apart: 43, of which 13 were waited for; matrix products, arithmetic and copies ran while one was open for 1% of the time, Pallas kernels for 9%

profile of v6, /device:TPU:6, one launch (start us, length us, event | category | flops | bytes accessed | tf_op | source)
XLA Modules:
  0.0 140.2 jit_solution(11102214204598332703)
XLA Ops:
  0.7 0.1 pad_add_fusion.place
  0.8 1.3 copy-done.19
  2.0 0.6 payload.1
  2.7 3.5 %collective-permute-start.3 = (f32[512,256]{1,0:T(8,128)S(1)}, f32[512,256]{1,0:T(8,128)S(1)}, u32[]{:S(2)}, u32[]{:S(2)}) collective-permute-start(f32[512,256]{1,0:T(8,128)S(1)} %get-tuple-element.33.rest_0_), channel_id=1, source_target_pairs={{0,2},{1,3},{8,10},{9,11},{10,12},{11,13},{12,14},{13,15},{14,8},{... | collective-permute-start | bytes 1572872 | tf_op jit(solution)/shard_map/ppermute | solution.py:110
  6.2 3.6 %collective-permute-start.1 = (f32[512,256]{1,0:T(8,128)S(1)}, f32[512,256]{1,0:T(8,128)S(1)}, u32[]{:S(2)}, u32[]{:S(2)}) collective-permute-start(f32[512,256]{1,0:T(8,128)S(1)} %get-tuple-element.33.rest_0_), channel_id=1, source_target_pairs={{0,6},{1,7},{8,14},{9,15},{10,8},{11,9},{12,10},{13,11},{14,12},{1... | collective-permute-start | bytes 1572872 | tf_op jit(solution)/shard_map/ppermute | solution.py:111
  9.8 0.1 collective-permute-start
  9.9 2.3 %collective-permute-start.10 = (f32[512,256]{1,0:T(8,128)S(1)}, f32[512,256]{1,0:T(8,128)S(1)}, u32[]{:S(2)}, u32[]{:S(2)}) collective-permute-start(f32[512,256]{1,0:T(8,128)S(1)} %get-tuple-element.34.rest_8_), channel_id=1, source_target_pairs={{0,2},{1,3},{2,4},{3,5},{8,10},{9,11},{10,12},{11,13},{12,14},{13,... | collective-permute-start | bytes 1572872 | tf_op jit(solution)/shard_map/ppermute | solution.py:110
  12.1 4.8 %collective-permute-start.8 = (f32[512,256]{1,0:T(8,128)S(1)}, f32[512,256]{1,0:T(8,128)S(1)}, u32[]{:S(2)}, u32[]{:S(2)}) collective-permute-start(f32[512,256]{1,0:T(8,128)S(1)} %get-tuple-element.34.rest_8_), channel_id=1, source_target_pairs={{0,6},{1,7},{2,0},{3,1},{8,14},{9,15},{10,8},{11,9},{12,10},{13,11... | collective-permute-start | bytes 1572872 | tf_op jit(solution)/shard_map/ppermute | solution.py:111
  16.9 3.7 %collective-permute-done.3.rest_4_ = f32[512,256]{1,0:T(8,128)S(1)} collective-permute-done((f32[512,256]{1,0:T(8,128)S(1)}, f32[512,256]{1,0:T(8,128)S(1)}, u32[]{:S(2)}, u32[]{:S(2)}) %collective-permute-start.3) | collective-permute-done | bytes 524320 | tf_op jit(solution)/shard_map/ppermute | solution.py:110
  20.6 2.3 %collective-permute-done.1.rest_2_ = f32[512,256]{1,0:T(8,128)S(1)} collective-permute-done((f32[512,256]{1,0:T(8,128)S(1)}, f32[512,256]{1,0:T(8,128)S(1)}, u32[]{:S(2)}, u32[]{:S(2)}) %collective-permute-start.1) | collective-permute-done | bytes 524320 | tf_op jit(solution)/shard_map/ppermute | solution.py:111
  22.9 4.8 %collective-permute-start.5 = (f32[512,256]{1,0:T(8,128)S(1)}, f32[512,256]{1,0:T(8,128)S(1)}, u32[]{:S(2)}, u32[]{:S(2)}) collective-permute-start(f32[512,256]{1,0:T(8,128)S(1)} %collective-permute-done.1.rest_2_), channel_id=1, source_target_pairs={{6,4},{7,5},{8,14},{9,15},{10,8},{11,9},{12,10},{13,11},{14,12},{1... | collective-permute-start | bytes 1572872 | tf_op jit(solution)/shard_map/ppermute | solution.py:116
  27.7 3.0 %collective-permute-done.10.rest_12_ = f32[512,256]{1,0:T(8,128)S(1)} collective-permute-done((f32[512,256]{1,0:T(8,128)S(1)}, f32[512,256]{1,0:T(8,128)S(1)}, u32[]{:S(2)}, u32[]{:S(2)}) %collective-permute-start.10) | collective-permute-done | bytes 524320 | tf_op jit(solution)/shard_map/ppermute | solution.py:110
  30.8 2.2 %collective-permute-start.12 = (f32[512,256]{1,0:T(8,128)S(1)}, f32[512,256]{1,0:T(8,128)S(1)}, u32[]{:S(2)}, u32[]{:S(2)}) collective-permute-start(f32[512,256]{1,0:T(8,128)S(1)} %collective-permute-done.10.rest_12_), channel_id=1, source_target_pairs={{2,4},{3,5},{4,6},{5,7},{8,10},{9,11},{10,12},{11,13},{12,14},{13,... | collective-permute-start | bytes 1572872 | tf_op jit(solution)/shard_map/ppermute | solution.py:117
  33.0 1.2 collective-permute-done.8.rest_10_
  34.2 0.5 collective-permute-start.11
  34.7 0.1 collective-permute-start.9
  34.8 9.1 %collective-permute-done.5.rest_6_ = f32[512,256]{1,0:T(8,128)S(1)} collective-permute-done((f32[512,256]{1,0:T(8,128)S(1)}, f32[512,256]{1,0:T(8,128)S(1)}, u32[]{:S(2)}, u32[]{:S(2)}) %collective-permute-start.5) | collective-permute-done | bytes 524320 | tf_op jit(solution)/shard_map/ppermute | solution.py:116
  43.9 2.8 %collective-permute-done.12.rest_14_ = f32[512,256]{1,0:T(8,128)S(1)} collective-permute-done((f32[512,256]{1,0:T(8,128)S(1)}, f32[512,256]{1,0:T(8,128)S(1)}, u32[]{:S(2)}, u32[]{:S(2)}) %collective-permute-start.12) | collective-permute-done | bytes 524320 | tf_op jit(solution)/shard_map/ppermute | solution.py:117
  46.8 1.8 %collective-permute-done.13.rest_15_ = f32[512,256]{1,0:T(8,128)S(1)} collective-permute-done((f32[512,256]{1,0:T(8,128)S(1)}, f32[512,256]{1,0:T(8,128)S(1)}, u32[]{:S(2)}, u32[]{:S(2)}) %collective-permute-start.13) | collective-permute-done | bytes 524320 | tf_op jit(solution)/shard_map/ppermute | solution.py:106
  48.6 1.6 %solve.1 = (f32[704,256]{1,0:T(8,128)}, f32[160,256]{1,0:T(8,128)S(1)}, f32[160,256]{1,0:T(8,128)S(1)}, f32[256,256]{1,0:T(8,128)S(1)}, f32[256,256]{1,0:T(8,128)S(1)}) custom-call(s32[4]{0:T(128)S(1)} %pad_add_fusion.place, f32[1024,256]{1,0:T(8,128)S(1)} %copy-done.16, f32[512,256]{1,0:T(8,128)S(1)} %get-tuple-element.33.rest_0_, ...), custom_call_target="tpu_custom_call" | custom-call | flops 536870912 | bytes 8388608 | tf_op jit(solution)/shard_map/solve/pallas_call | solution.py:39
  50.4 0.7 collective-permute-start.14
  51.1 0.7 collective-permute-start.15
  51.8 1.3 collective-permute-start.16
  53.1 0.7 collective-permute-start.18
  53.8 1.3 collective-permute-start.19
  55.1 16.6 %collective-permute-done.16 = f32[256,256]{1,0:T(8,128)S(1)} collective-permute-done((f32[256,256]{1,0:T(8,128)S(1)}, f32[256,256]{1,0:T(8,128)S(1)}, u32[]{:S(2)}, u32[]{:S(2)}) %collective-permute-start.16) | collective-permute-done | bytes 262176 | tf_op jit(solution)/shard_map/ppermute | solution.py:391
  71.7 1.3 collective-permute-start.17
  73.0 0.7 collective-permute-start.22
  73.7 0.7 collective-permute-start.20
  74.4 1.2 copy-done.17
  75.6 1.0 prepare.1
  76.6 0.7 collective-permute-start.23
  77.3 0.7 collective-permute-start.21
  78.0 1.0 fusion
  79.1 1.3 collective-permute-start.25
  80.4 1.3 collective-permute-start.24
  81.7 0.6 combine.1
  82.2 0.7 collective-permute-start.30
  82.9 1.3 collective-permute-start.28
  84.2 0.7 collective-permute-start.29
  84.9 1.0 collective-permute-done.24
  86.0 1.3 collective-permute-start.27
  87.3 1.3 collective-permute-start.26
  88.7 11.3 %collective-permute-done.28 = f32[256,256]{1,0:T(8,128)S(1)} collective-permute-done((f32[256,256]{1,0:T(8,128)S(1)}, f32[256,256]{1,0:T(8,128)S(1)}, u32[]{:S(2)}, u32[]{:S(2)}) %collective-permute-start.28) | collective-permute-done | bytes 262176 | tf_op jit(solution)/shard_map/ppermute | solution.py:396
  100.0 0.1 add_select_fusion.2
  100.1 1.4 %collective-permute-start.32 = (f32[256,256]{1,0:T(8,128)S(1)}, f32[256,256]{1,0:T(8,128)S(1)}, u32[]{:S(2)}, u32[]{:S(2)}) collective-permute-start(f32[256,256]{1,0:T(8,128)S(1)} %add_select_fusion.2), channel_id=1, source_target_pairs={{0,160},{8,168},{16,176},{24,184},{1,161},{9,169},{17,177},{25,185... | collective-permute-start | bytes 786440 | tf_op jit(solution)/shard_map/ppermute | solution.py:401
  101.5 1.3 collective-permute-start.31
  102.9 0.1 add_select_fusion.3.rest_16_
  102.9 4.7 %collective-permute-start.35 = (f32[256,256]{1,0:T(8,128)S(1)}, f32[256,256]{1,0:T(8,128)S(1)}, u32[]{:S(2)}, u32[]{:S(2)}) collective-permute-start(f32[256,256]{1,0:T(8,128)S(1)} %add_select_fusion.3.rest_16_), channel_id=1, source_target_pairs={{0,8},{8,16},{16,24},{24,0},{32,40},{40,48},{48,56},{56,32},{64,72... | collective-permute-start | bytes 786440 | tf_op jit(solution)/shard_map/ppermute | solution.py:412
  107.7 0.1 add_select_fusion.1
  107.7 1.3 collective-permute-start.38
  109.0 1.3 collective-permute-start.37
  110.3 1.6 %collective-permute-done.35.rest_20_ = f32[256,256]{1,0:T(8,128)S(1)} collective-permute-done((f32[256,256]{1,0:T(8,128)S(1)}, f32[256,256]{1,0:T(8,128)S(1)}, u32[]{:S(2)}, u32[]{:S(2)}) %collective-permute-start.35) | collective-permute-done | bytes 262176 | tf_op jit(solution)/shard_map/ppermute | solution.py:412
  112.0 3.8 %collective-permute-start.36 = (f32[128,256]{1,0:T(8,128)S(1)}, f32[128,256]{1,0:T(8,128)S(1)}, u32[]{:S(2)}, u32[]{:S(2)}) collective-permute-start(f32[128,256]{1,0:T(8,128)S(1)} %slice.26), channel_id=1, source_target_pairs={{0,8},{8,16},{16,24},{24,0},{32,40},{40,48},{48,56},{56,32},{64,72... | collective-permute-start | bytes 393224 | tf_op jit(solution)/shard_map/ppermute | solution.py:416
  115.8 0.3 collective-permute-start.34
  116.1 0.1 add_select_fusion.rest_16_
  116.2 3.3 %collective-permute-start.40 = (f32[256,256]{1,0:T(8,128)S(1)}, f32[256,256]{1,0:T(8,128)S(1)}, u32[]{:S(2)}, u32[]{:S(2)}) collective-permute-start(f32[256,256]{1,0:T(8,128)S(1)} %add_select_fusion.rest_16_), channel_id=1, source_target_pairs={{0,8},{8,16},{16,24},{24,0},{32,40},{40,48},{48,56},{56,32},{64,72... | collective-permute-start | bytes 786440 | tf_op jit(solution)/shard_map/ppermute | solution.py:412
  119.4 0.2 collective-permute-done.36.rest_19_
  119.6 4.0 %collective-permute-done.34.rest_18_ = f32[128,256]{1,0:T(8,128)S(1)} collective-permute-done((f32[128,256]{1,0:T(8,128)S(1)}, f32[128,256]{1,0:T(8,128)S(1)}, u32[]{:S(2)}, u32[]{:S(2)}) %collective-permute-start.34) | collective-permute-done | bytes 131104 | tf_op jit(solution)/shard_map/ppermute | solution.py:416
  123.6 5.8 %update.1 = (f32[1024,256]{1,0:T(8,128)S(1)}, f32[2048,256]{1,0:T(8,128)}) custom-call(s32[4]{0:T(128)S(1)} %pad_add_fusion.place, f32[1024,256]{1,0:T(8,128)S(1)} %copy-done.18, f32[512,256]{1,0:T(8,128)} %copy-done, f32[512,256]{1,0:T(8,128)} %copy-done.4, f32[512,256]{1,0:T(8,128)} %copy-done.3, f32[512,256]{1,0:T(8,128)} %copy-done.11, ...), custom_call_target="tpu_custom_call" | custom-call | flops 16106127360 | bytes 8388608 | tf_op jit(solution)/shard_map/update/pallas_call | solution.py:39
  129.4 0.1 collective-permute-start.41
  129.5 3.2 %collective-permute-start.42 = (f32[128,256]{1,0:T(8,128)S(1)}, f32[128,256]{1,0:T(8,128)S(1)}, u32[]{:S(2)}, u32[]{:S(2)}) collective-permute-start(f32[128,256]{1,0:T(8,128)S(1)} %slice.23), channel_id=1, source_target_pairs={{0,8},{8,16},{16,24},{24,0},{32,40},{40,48},{48,56},{56,32},{64,72... | collective-permute-start | bytes 393224 | tf_op jit(solution)/shard_map/ppermute | solution.py:416
  132.7 4.7 %most.1 = (f32[1024,256]{1,0:T(8,128)S(1)}, f32[2048,256]{1,0:T(8,128)}, f32[1024,256]{1,0:T(8,128)S(1)}) custom-call(s32[4]{0:T(128)S(1)} %pad_add_fusion.place, f32[1024,256]{1,0:T(8,128)S(1)} %get-tuple-element.57.target, f32[512,256]{1,0:T(8,128)} %copy-done, f32[512,256]{1,0:T(8,128)} %copy-done.4, ...), custom_call_target="tpu_custom_call", output_to_operand_aliasing={{1}: (21, {})} | custom-call | flops 1610612736 | bytes 8388608 | tf_op jit(solution)/shard_map/most/pallas_call | solution.py:39
  137.5 2.5 %last.1 = (f32[1024,256]{1,0:T(8,128)}, f32[2048,256]{1,0:T(8,128)}) custom-call(s32[4]{0:T(128)S(1)} %pad_add_fusion.place, f32[1024,256]{1,0:T(8,128)S(1)} %get-tuple-element.61.target, f32[1024,256]{1,0:T(8,128)S(1)} %get-tuple-element.62.block, f32[128,256]{1,0:T(8,128)S(1)} %collective-permute-done.41.upper, ...), custom_call_target="tpu_custom_call", output_to_operand_aliasing={{1}: (5, {})} | custom-call | flops 536870912 | bytes 8388608 | tf_op jit(solution)/shard_map/last/pallas_call | solution.py:39
  (80 shorter events, 0.3 us)
Async XLA Ops:
  0.7 48.0 %copy-start.16 = (f32[1024,256]{1,0:T(8,128)S(1)}, f32[1024,256]{1,0:T(8,128)}, u32[]{:S(2)}) copy-start(f32[1024,256]{1,0:T(8,128)} %target.1) | copy-start | bytes 3145732
  0.7 1.3 copy-start.19
  2.7 47.5 %copy-start = (f32[512,256]{1,0:T(8,128)}, f32[512,256]{1,0:T(8,128)S(1)}, u32[]{:S(2)}) copy-start(f32[512,256]{1,0:T(8,128)S(1)} %get-tuple-element.33.rest_0_) | copy-start | bytes 1572868
  2.7 47.5 %copy-start.1 = (f32[512,256]{1,0:T(8,128)}, f32[512,256]{1,0:T(8,128)S(1)}, u32[]{:S(2)}) copy-start(f32[512,256]{1,0:T(8,128)S(1)} %get-tuple-element.34.rest_8_) | copy-start | bytes 1572868
  2.7 17.9 %collective-permute-start.3 = (f32[512,256]{1,0:T(8,128)S(1)}, f32[512,256]{1,0:T(8,128)S(1)}, u32[]{:S(2)}, u32[]{:S(2)}) collective-permute-start(f32[512,256]{1,0:T(8,128)S(1)} %get-tuple-element.33.rest_0_), channel_id=1, source_target_pairs={{0,2},{1,3},{8,10},{9,11},{10,12},{11,13},{12,14},{13,15},{14,8},{... | collective-permute-start | bytes 1572872 | tf_op jit(solution)/shard_map/ppermute | solution.py:110
  6.2 16.7 %collective-permute-start.1 = (f32[512,256]{1,0:T(8,128)S(1)}, f32[512,256]{1,0:T(8,128)S(1)}, u32[]{:S(2)}, u32[]{:S(2)}) collective-permute-start(f32[512,256]{1,0:T(8,128)S(1)} %get-tuple-element.33.rest_0_), channel_id=1, source_target_pairs={{0,6},{1,7},{8,14},{9,15},{10,8},{11,9},{12,10},{13,11},{14,12},{1... | collective-permute-start | bytes 1572872 | tf_op jit(solution)/shard_map/ppermute | solution.py:111
  9.8 13.2 %collective-permute-start = (f32[512,256]{1,0:T(8,128)S(1)}, f32[512,256]{1,0:T(8,128)S(1)}, u32[]{:S(2)}, u32[]{:S(2)}) collective-permute-start(f32[512,256]{1,0:T(8,128)S(1)} %get-tuple-element.33.rest_0_), channel_id=1, source_target_pairs={{0,1},{1,0},{2,3},{3,2},{4,5},{5,4},{6,7},{7,6},{8,9},{9,8},{10,11... | collective-permute-start | bytes 1572872 | tf_op jit(solution)/shard_map/ppermute | solution.py:106
  9.9 20.9 %collective-permute-start.10 = (f32[512,256]{1,0:T(8,128)S(1)}, f32[512,256]{1,0:T(8,128)S(1)}, u32[]{:S(2)}, u32[]{:S(2)}) collective-permute-start(f32[512,256]{1,0:T(8,128)S(1)} %get-tuple-element.34.rest_8_), channel_id=1, source_target_pairs={{0,2},{1,3},{2,4},{3,5},{8,10},{9,11},{10,12},{11,13},{12,14},{13,... | collective-permute-start | bytes 1572872 | tf_op jit(solution)/shard_map/ppermute | solution.py:110
  12.1 22.0 %collective-permute-start.8 = (f32[512,256]{1,0:T(8,128)S(1)}, f32[512,256]{1,0:T(8,128)S(1)}, u32[]{:S(2)}, u32[]{:S(2)}) collective-permute-start(f32[512,256]{1,0:T(8,128)S(1)} %get-tuple-element.34.rest_8_), channel_id=1, source_target_pairs={{0,6},{1,7},{2,0},{3,1},{8,14},{9,15},{10,8},{11,9},{12,10},{13,11... | collective-permute-start | bytes 1572872 | tf_op jit(solution)/shard_map/ppermute | solution.py:111
  20.6 29.6 %copy-start.2 = (f32[512,256]{1,0:T(8,128)}, f32[512,256]{1,0:T(8,128)S(1)}, u32[]{:S(2)}) copy-start(f32[512,256]{1,0:T(8,128)S(1)} %collective-permute-done.3.rest_4_) | copy-start | bytes 1572868
  20.6 13.6 %collective-permute-start.7 = (f32[512,256]{1,0:T(8,128)S(1)}, f32[512,256]{1,0:T(8,128)S(1)}, u32[]{:S(2)}, u32[]{:S(2)}) collective-permute-start(f32[512,256]{1,0:T(8,128)S(1)} %get-tuple-element.34.rest_8_), channel_id=1, source_target_pairs={{0,1},{1,0},{2,3},{3,2},{4,5},{5,4},{6,7},{7,6},{8,9},{9,8},{10,11... | collective-permute-start | bytes 1572872 | tf_op jit(solution)/shard_map/ppermute | solution.py:106
  22.9 27.3 %copy-start.3 = (f32[512,256]{1,0:T(8,128)}, f32[512,256]{1,0:T(8,128)S(1)}, u32[]{:S(2)}) copy-start(f32[512,256]{1,0:T(8,128)S(1)} %collective-permute-done.1.rest_2_) | copy-start | bytes 1572868
  22.9 11.8 %collective-permute-start.4 = (f32[512,256]{1,0:T(8,128)S(1)}, f32[512,256]{1,0:T(8,128)S(1)}, u32[]{:S(2)}, u32[]{:S(2)}) collective-permute-start(f32[512,256]{1,0:T(8,128)S(1)} %collective-permute-done.3.rest_4_), channel_id=1, source_target_pairs={{0,1},{1,0},{2,3},{3,2},{4,5},{5,4},{6,7},{7,6},{8,9},{9,8},{10,11... | collective-permute-start | bytes 1572872 | tf_op jit(solution)/shard_map/ppermute | solution.py:106
  22.9 27.3 %copy-start.4 = (f32[512,256]{1,0:T(8,128)}, f32[512,256]{1,0:T(8,128)S(1)}, u32[]{:S(2)}) copy-start(f32[512,256]{1,0:T(8,128)S(1)} %collective-permute-done.rest_1_) | copy-start | bytes 1572868
  22.9 21.0 %collective-permute-start.5 = (f32[512,256]{1,0:T(8,128)S(1)}, f32[512,256]{1,0:T(8,128)S(1)}, u32[]{:S(2)}, u32[]{:S(2)}) collective-permute-start(f32[512,256]{1,0:T(8,128)S(1)} %collective-permute-done.1.rest_2_), channel_id=1, source_target_pairs={{6,4},{7,5},{8,14},{9,15},{10,8},{11,9},{12,10},{13,11},{14,12},{1... | collective-permute-start | bytes 1572872 | tf_op jit(solution)/shard_map/ppermute | solution.py:116
  30.8 19.5 %copy-start.5 = (f32[512,256]{1,0:T(8,128)}, f32[512,256]{1,0:T(8,128)S(1)}, u32[]{:S(2)}) copy-start(f32[512,256]{1,0:T(8,128)S(1)} %collective-permute-done.10.rest_12_) | copy-start | bytes 1572868
  30.8 16.0 %collective-permute-start.12 = (f32[512,256]{1,0:T(8,128)S(1)}, f32[512,256]{1,0:T(8,128)S(1)}, u32[]{:S(2)}, u32[]{:S(2)}) collective-permute-start(f32[512,256]{1,0:T(8,128)S(1)} %collective-permute-done.10.rest_12_), channel_id=1, source_target_pairs={{2,4},{3,5},{4,6},{5,7},{8,10},{9,11},{10,12},{11,13},{12,14},{13,... | collective-permute-start | bytes 1572872 | tf_op jit(solution)/shard_map/ppermute | solution.py:117
  34.2 16.1 %copy-start.6 = (f32[512,256]{1,0:T(8,128)}, f32[512,256]{1,0:T(8,128)S(1)}, u32[]{:S(2)}) copy-start(f32[512,256]{1,0:T(8,128)S(1)} %collective-permute-done.8.rest_10_) | copy-start | bytes 1572868
  34.2 12.6 %collective-permute-start.2 = (f32[512,256]{1,0:T(8,128)S(1)}, f32[512,256]{1,0:T(8,128)S(1)}, u32[]{:S(2)}, u32[]{:S(2)}) collective-permute-start(f32[512,256]{1,0:T(8,128)S(1)} %collective-permute-done.1.rest_2_), channel_id=1, source_target_pairs={{0,1},{1,0},{2,3},{3,2},{4,5},{5,4},{6,7},{7,6},{8,9},{9,8},{10,11... | collective-permute-start | bytes 1572872 | tf_op jit(solution)/shard_map/ppermute | solution.py:106
  34.2 16.1 %copy-start.7 = (f32[512,256]{1,0:T(8,128)}, f32[512,256]{1,0:T(8,128)S(1)}, u32[]{:S(2)}) copy-start(f32[512,256]{1,0:T(8,128)S(1)} %collective-permute-done.7.rest_9_) | copy-start | bytes 1572868
  34.2 12.6 %collective-permute-start.11 = (f32[512,256]{1,0:T(8,128)S(1)}, f32[512,256]{1,0:T(8,128)S(1)}, u32[]{:S(2)}, u32[]{:S(2)}) collective-permute-start(f32[512,256]{1,0:T(8,128)S(1)} %collective-permute-done.10.rest_12_), channel_id=1, source_target_pairs={{0,1},{1,0},{2,3},{3,2},{4,5},{5,4},{6,7},{7,6},{8,9},{9,8},{10,11... | collective-permute-start | bytes 1572872 | tf_op jit(solution)/shard_map/ppermute | solution.py:106
  34.7 15.6 %copy-start.8 = (f32[512,256]{1,0:T(8,128)}, f32[512,256]{1,0:T(8,128)S(1)}, u32[]{:S(2)}) copy-start(f32[512,256]{1,0:T(8,128)S(1)} %collective-permute-done.4.rest_5_) | copy-start | bytes 1572868
  34.7 12.1 %collective-permute-start.9 = (f32[512,256]{1,0:T(8,128)S(1)}, f32[512,256]{1,0:T(8,128)S(1)}, u32[]{:S(2)}, u32[]{:S(2)}) collective-permute-start(f32[512,256]{1,0:T(8,128)S(1)} %collective-permute-done.8.rest_10_), channel_id=1, source_target_pairs={{0,1},{1,0},{2,3},{3,2},{4,5},{5,4},{6,7},{7,6},{8,9},{9,8},{10,11... | collective-permute-start | bytes 1572872 | tf_op jit(solution)/shard_map/ppermute | solution.py:106
  43.9 6.4 %copy-start.9 = (f32[512,256]{1,0:T(8,128)}, f32[512,256]{1,0:T(8,128)S(1)}, u32[]{:S(2)}) copy-start(f32[512,256]{1,0:T(8,128)S(1)} %collective-permute-done.5.rest_6_) | copy-start | bytes 1572868
  43.9 2.9 %collective-permute-start.6 = (f32[512,256]{1,0:T(8,128)S(1)}, f32[512,256]{1,0:T(8,128)S(1)}, u32[]{:S(2)}, u32[]{:S(2)}) collective-permute-start(f32[512,256]{1,0:T(8,128)S(1)} %collective-permute-done.5.rest_6_), channel_id=1, source_target_pairs={{0,1},{1,0},{2,3},{3,2},{4,5},{5,4},{6,7},{7,6},{8,9},{9,8},{10,11... | collective-permute-start | bytes 1572872 | tf_op jit(solution)/shard_map/ppermute | solution.py:106
  46.7 3.6 %copy-start.10 = (f32[512,256]{1,0:T(8,128)}, f32[512,256]{1,0:T(8,128)S(1)}, u32[]{:S(2)}) copy-start(f32[512,256]{1,0:T(8,128)S(1)} %collective-permute-done.12.rest_14_) | copy-start | bytes 1572868
  46.7 1.9 %collective-permute-start.13 = (f32[512,256]{1,0:T(8,128)S(1)}, f32[512,256]{1,0:T(8,128)S(1)}, u32[]{:S(2)}, u32[]{:S(2)}) collective-permute-start(f32[512,256]{1,0:T(8,128)S(1)} %collective-permute-done.12.rest_14_), channel_id=1, source_target_pairs={{0,1},{1,0},{2,3},{3,2},{4,5},{5,4},{6,7},{7,6},{8,9},{9,8},{10,11... | collective-permute-start | bytes 1572872 | tf_op jit(solution)/shard_map/ppermute | solution.py:106
  46.7 3.6 %copy-start.11 = (f32[512,256]{1,0:T(8,128)}, f32[512,256]{1,0:T(8,128)S(1)}, u32[]{:S(2)}) copy-start(f32[512,256]{1,0:T(8,128)S(1)} %collective-permute-done.2.rest_3_) | copy-start | bytes 1572868
  46.8 3.6 %copy-start.12 = (f32[512,256]{1,0:T(8,128)}, f32[512,256]{1,0:T(8,128)S(1)}, u32[]{:S(2)}) copy-start(f32[512,256]{1,0:T(8,128)S(1)} %collective-permute-done.11.rest_13_) | copy-start | bytes 1572868
  46.8 3.6 %copy-start.13 = (f32[512,256]{1,0:T(8,128)}, f32[512,256]{1,0:T(8,128)S(1)}, u32[]{:S(2)}) copy-start(f32[512,256]{1,0:T(8,128)S(1)} %collective-permute-done.9.rest_11_) | copy-start | bytes 1572868
  46.8 3.6 %copy-start.14 = (f32[512,256]{1,0:T(8,128)}, f32[512,256]{1,0:T(8,128)S(1)}, u32[]{:S(2)}) copy-start(f32[512,256]{1,0:T(8,128)S(1)} %collective-permute-done.6.rest_7_) | copy-start | bytes 1572868
  48.6 1.7 %copy-start.15 = (f32[512,256]{1,0:T(8,128)}, f32[512,256]{1,0:T(8,128)S(1)}, u32[]{:S(2)}) copy-start(f32[512,256]{1,0:T(8,128)S(1)} %collective-permute-done.13.rest_15_) | copy-start | bytes 1572868
  50.4 27.6 %collective-permute-start.14 = (f32[704,256]{1,0:T(8,128)}, f32[704,256]{1,0:T(8,128)S(1)}, u32[]{:S(2)}, u32[]{:S(2)}) collective-permute-start(f32[704,256]{1,0:T(8,128)} %get-tuple-element.35), channel_id=1, source_target_pairs={{0,8},{1,9},{2,10},{3,11},{4,12},{5,13},{6,14},{7,15}} | collective-permute-start | bytes 2162696 | tf_op jit(solution)/shard_map/ppermute | solution.py:446
  51.1 0.7 collective-permute-start.15
  51.8 19.9 %collective-permute-start.16 = (f32[256,256]{1,0:T(8,128)S(1)}, f32[256,256]{1,0:T(8,128)S(1)}, u32[]{:S(2)}, u32[]{:S(2)}) collective-permute-start(f32[256,256]{1,0:T(8,128)S(1)} %get-tuple-element.38), channel_id=1, source_target_pairs={{0,24},{1,25},{2,26},{3,27},{4,28},{5,29},{6,30},{7,31}} | collective-permute-start | bytes 786440 | tf_op jit(solution)/shard_map/ppermute | solution.py:391
  53.1 0.7 collective-permute-start.18
  53.8 24.2 %collective-permute-start.19 = (f32[256,256]{1,0:T(8,128)S(1)}, f32[256,256]{1,0:T(8,128)S(1)}, u32[]{:S(2)}, u32[]{:S(2)}) collective-permute-start(f32[256,256]{1,0:T(8,128)S(1)} %get-tuple-element.41), channel_id=1, source_target_pairs={{0,24},{1,25},{2,26},{3,27},{4,28},{5,29},{6,30},{7,31}} | collective-permute-start | bytes 786440 | tf_op jit(solution)/shard_map/ppermute | solution.py:392
  71.7 6.3 %collective-permute-start.17 = (f32[256,256]{1,0:T(8,128)S(1)}, f32[256,256]{1,0:T(8,128)S(1)}, u32[]{:S(2)}, u32[]{:S(2)}) collective-permute-start(f32[256,256]{1,0:T(8,128)S(1)} %collective-permute-done.16), channel_id=1, source_target_pairs={{24,16},{25,17},{26,18},{27,19},{28,20},{29,21},{30,22},{31,23}} | collective-permute-start | bytes 786440 | tf_op jit(solution)/shard_map/ppermute | solution.py:392
  73.0 3.6 %collective-permute-start.22 = (f32[160,256]{1,0:T(8,128)S(1)}, f32[160,256]{1,0:T(8,128)S(1)}, u32[]{:S(2)}, u32[]{:S(2)}) collective-permute-start(f32[160,256]{1,0:T(8,128)S(1)} %collective-permute-done.15), channel_id=1, source_target_pairs={{224,232},{225,233},{226,234},{227,235},{228,236},{229,237},{230,2... | collective-permute-start | bytes 491528 | tf_op jit(solution)/shard_map/ppermute | solution.py:445
  73.7 3.6 %collective-permute-start.20 = (f32[160,256]{1,0:T(8,128)S(1)}, f32[160,256]{1,0:T(8,128)S(1)}, u32[]{:S(2)}, u32[]{:S(2)}) collective-permute-start(f32[160,256]{1,0:T(8,128)S(1)} %collective-permute-done.18), channel_id=1, source_target_pairs={{32,40},{33,41},{34,42},{35,43},{36,44},{37,45},{38,46},{39,47}} | collective-permute-start | bytes 491528 | tf_op jit(solution)/shard_map/ppermute | solution.py:443
  74.3 1.2 copy-start.17
  76.6 2.4 %collective-permute-start.23 = (f32[160,256]{1,0:T(8,128)S(1)}, f32[160,256]{1,0:T(8,128)S(1)}, u32[]{:S(2)}, u32[]{:S(2)}) collective-permute-start(f32[160,256]{1,0:T(8,128)S(1)} %collective-permute-done.22), channel_id=1, source_target_pairs={{232,8},{233,9},{234,10},{235,11},{236,12},{237,13},{238,14},{239,... | collective-permute-start | bytes 491528 | tf_op jit(solution)/shard_map/ppermute | solution.py:445
  77.3 1.7 %collective-permute-start.21 = (f32[160,256]{1,0:T(8,128)S(1)}, f32[160,256]{1,0:T(8,128)S(1)}, u32[]{:S(2)}, u32[]{:S(2)}) collective-permute-start(f32[160,256]{1,0:T(8,128)S(1)} %collective-permute-done.20), channel_id=1, source_target_pairs={{40,8},{41,9},{42,10},{43,11},{44,12},{45,13},{46,14},{47,15}} | collective-permute-start | bytes 491528 | tf_op jit(solution)/shard_map/ppermute | solution.py:443
  79.1 5.9 %collective-permute-start.25 = (f32[256,256]{1,0:T(8,128)S(1)}, f32[256,256]{1,0:T(8,128)S(1)}, u32[]{:S(2)}, u32[]{:S(2)}) collective-permute-start(f32[256,256]{1,0:T(8,128)S(1)} %fusion), channel_id=1, source_target_pairs={{0,160},{8,168},{16,176},{24,184},{1,161},{9,169},{17,177},{25,185... | collective-permute-start | bytes 786440 | tf_op jit(solution)/shard_map/ppermute | solution.py:401
  80.4 5.6 %collective-permute-start.24 = (f32[256,256]{1,0:T(8,128)S(1)}, f32[256,256]{1,0:T(8,128)S(1)}, u32[]{:S(2)}, u32[]{:S(2)}) collective-permute-start(f32[256,256]{1,0:T(8,128)S(1)} %fusion), channel_id=1, source_target_pairs={{0,96},{8,104},{16,112},{24,120},{1,97},{9,105},{17,113},{25,121},... | collective-permute-start | bytes 786440 | tf_op jit(solution)/shard_map/ppermute | solution.py:400
  82.2 6.4 %collective-permute-start.30 = (f32[256,256]{1,0:T(8,128)S(1)}, f32[256,256]{1,0:T(8,128)S(1)}, u32[]{:S(2)}, u32[]{:S(2)}) collective-permute-start(f32[256,256]{1,0:T(8,128)S(1)} %get-tuple-element.47), channel_id=1, source_target_pairs={{8,16},{9,17},{10,18},{11,19},{12,20},{13,21},{14,22},{15,23}} | collective-permute-start | bytes 786440 | tf_op jit(solution)/shard_map/ppermute | solution.py:396
  82.9 17.1 %collective-permute-start.28 = (f32[256,256]{1,0:T(8,128)S(1)}, f32[256,256]{1,0:T(8,128)S(1)}, u32[]{:S(2)}, u32[]{:S(2)}) collective-permute-start(f32[256,256]{1,0:T(8,128)S(1)} %get-tuple-element.48), channel_id=1, source_target_pairs={{8,24},{9,25},{10,26},{11,27},{12,28},{13,29},{14,30},{15,31}} | collective-permute-start | bytes 786440 | tf_op jit(solution)/shard_map/ppermute | solution.py:396
  84.2 15.8 %collective-permute-start.29 = (f32[256,256]{1,0:T(8,128)S(1)}, f32[256,256]{1,0:T(8,128)S(1)}, u32[]{:S(2)}, u32[]{:S(2)}) collective-permute-start(f32[256,256]{1,0:T(8,128)S(1)} %get-tuple-element.49), channel_id=1, source_target_pairs={{8,0},{9,1},{10,2},{11,3},{12,4},{13,5},{14,6},{15,7}} | collective-permute-start | bytes 786440 | tf_op jit(solution)/shard_map/ppermute | solution.py:396
  86.0 16.8 %collective-permute-start.27 = (f32[256,256]{1,0:T(8,128)S(1)}, f32[256,256]{1,0:T(8,128)S(1)}, u32[]{:S(2)}, u32[]{:S(2)}) collective-permute-start(f32[256,256]{1,0:T(8,128)S(1)} %add_select_fusion.4), channel_id=1, source_target_pairs={{0,224},{8,232},{16,240},{24,248},{96,64},{104,72},{112,80},{120,8... | collective-permute-start | bytes 786440 | tf_op jit(solution)/shard_map/ppermute | solution.py:407
  87.3 15.5 %collective-permute-start.26 = (f32[256,256]{1,0:T(8,128)S(1)}, f32[256,256]{1,0:T(8,128)S(1)}, u32[]{:S(2)}, u32[]{:S(2)}) collective-permute-start(f32[256,256]{1,0:T(8,128)S(1)} %add_select_fusion.4), channel_id=1, source_target_pairs={{0,32},{8,40},{16,48},{24,56},{96,128},{104,136},{112,144},{120,15... | collective-permute-start | bytes 786440 | tf_op jit(solution)/shard_map/ppermute | solution.py:406
  100.1 23.5 %copy-start.18 = (f32[1024,256]{1,0:T(8,128)S(1)}, f32[1024,256]{1,0:T(8,128)}, u32[]{:S(2)}) copy-start(f32[1024,256]{1,0:T(8,128)} %target.1) | copy-start | bytes 3145732
  100.1 7.6 %collective-permute-start.32 = (f32[256,256]{1,0:T(8,128)S(1)}, f32[256,256]{1,0:T(8,128)S(1)}, u32[]{:S(2)}, u32[]{:S(2)}) collective-permute-start(f32[256,256]{1,0:T(8,128)S(1)} %add_select_fusion.2), channel_id=1, source_target_pairs={{0,160},{8,168},{16,176},{24,184},{1,161},{9,169},{17,177},{25,185... | collective-permute-start | bytes 786440 | tf_op jit(solution)/shard_map/ppermute | solution.py:401
  101.5 6.1 %collective-permute-start.31 = (f32[256,256]{1,0:T(8,128)S(1)}, f32[256,256]{1,0:T(8,128)S(1)}, u32[]{:S(2)}, u32[]{:S(2)}) collective-permute-start(f32[256,256]{1,0:T(8,128)S(1)} %add_select_fusion.2), channel_id=1, source_target_pairs={{0,96},{8,104},{16,112},{24,120},{1,97},{9,105},{17,113},{25,121},... | collective-permute-start | bytes 786440 | tf_op jit(solution)/shard_map/ppermute | solution.py:400
  102.9 9.0 %collective-permute-start.35 = (f32[256,256]{1,0:T(8,128)S(1)}, f32[256,256]{1,0:T(8,128)S(1)}, u32[]{:S(2)}, u32[]{:S(2)}) collective-permute-start(f32[256,256]{1,0:T(8,128)S(1)} %add_select_fusion.3.rest_16_), channel_id=1, source_target_pairs={{0,8},{8,16},{16,24},{24,0},{32,40},{40,48},{48,56},{56,32},{64,72... | collective-permute-start | bytes 786440 | tf_op jit(solution)/shard_map/ppermute | solution.py:412
  107.7 8.1 %collective-permute-start.33 = (f32[256,256]{1,0:T(8,128)S(1)}, f32[256,256]{1,0:T(8,128)S(1)}, u32[]{:S(2)}, u32[]{:S(2)}) collective-permute-start(f32[256,256]{1,0:T(8,128)S(1)} %add_select_fusion.3.rest_16_), channel_id=1, source_target_pairs={{8,0},{16,8},{24,16},{0,24},{40,32},{48,40},{56,48},{32,56},{72,64... | collective-permute-start | bytes 786440 | tf_op jit(solution)/shard_map/ppermute | solution.py:412
  107.7 8.4 %collective-permute-start.38 = (f32[256,256]{1,0:T(8,128)S(1)}, f32[256,256]{1,0:T(8,128)S(1)}, u32[]{:S(2)}, u32[]{:S(2)}) collective-permute-start(f32[256,256]{1,0:T(8,128)S(1)} %add_select_fusion.1), channel_id=1, source_target_pairs={{0,224},{8,232},{16,240},{24,248},{96,64},{104,72},{112,80},{120,8... | collective-permute-start | bytes 786440 | tf_op jit(solution)/shard_map/ppermute | solution.py:407
  109.0 7.0 %collective-permute-start.37 = (f32[256,256]{1,0:T(8,128)S(1)}, f32[256,256]{1,0:T(8,128)S(1)}, u32[]{:S(2)}, u32[]{:S(2)}) collective-permute-start(f32[256,256]{1,0:T(8,128)S(1)} %add_select_fusion.1), channel_id=1, source_target_pairs={{0,32},{8,40},{16,48},{24,56},{96,128},{104,136},{112,144},{120,15... | collective-permute-start | bytes 786440 | tf_op jit(solution)/shard_map/ppermute | solution.py:406
  112.0 7.7 %collective-permute-start.36 = (f32[128,256]{1,0:T(8,128)S(1)}, f32[128,256]{1,0:T(8,128)S(1)}, u32[]{:S(2)}, u32[]{:S(2)}) collective-permute-start(f32[128,256]{1,0:T(8,128)S(1)} %slice.26), channel_id=1, source_target_pairs={{0,8},{8,16},{16,24},{24,0},{32,40},{40,48},{48,56},{56,32},{64,72... | collective-permute-start | bytes 393224 | tf_op jit(solution)/shard_map/ppermute | solution.py:416
  115.8 7.8 %collective-permute-start.34 = (f32[128,256]{1,0:T(8,128)S(1)}, f32[128,256]{1,0:T(8,128)S(1)}, u32[]{:S(2)}, u32[]{:S(2)}) collective-permute-start(f32[128,256]{1,0:T(8,128)S(1)} %slice.25), channel_id=1, source_target_pairs={{8,0},{16,8},{24,16},{0,24},{40,32},{48,40},{56,48},{32,56},{72,64... | collective-permute-start | bytes 393224 | tf_op jit(solution)/shard_map/ppermute | solution.py:416
  116.2 13.2 %collective-permute-start.40 = (f32[256,256]{1,0:T(8,128)S(1)}, f32[256,256]{1,0:T(8,128)S(1)}, u32[]{:S(2)}, u32[]{:S(2)}) collective-permute-start(f32[256,256]{1,0:T(8,128)S(1)} %add_select_fusion.rest_16_), channel_id=1, source_target_pairs={{0,8},{8,16},{16,24},{24,0},{32,40},{40,48},{48,56},{56,32},{64,72... | collective-permute-start | bytes 786440 | tf_op jit(solution)/shard_map/ppermute | solution.py:412
  119.4 9.9 %collective-permute-start.39 = (f32[256,256]{1,0:T(8,128)S(1)}, f32[256,256]{1,0:T(8,128)S(1)}, u32[]{:S(2)}, u32[]{:S(2)}) collective-permute-start(f32[256,256]{1,0:T(8,128)S(1)} %add_select_fusion.rest_16_), channel_id=1, source_target_pairs={{8,0},{16,8},{24,16},{0,24},{40,32},{48,40},{56,48},{32,56},{72,64... | collective-permute-start | bytes 786440 | tf_op jit(solution)/shard_map/ppermute | solution.py:412
  129.4 8.1 %collective-permute-start.41 = (f32[128,256]{1,0:T(8,128)S(1)}, f32[128,256]{1,0:T(8,128)S(1)}, u32[]{:S(2)}, u32[]{:S(2)}) collective-permute-start(f32[128,256]{1,0:T(8,128)S(1)} %slice.22), channel_id=1, source_target_pairs={{8,0},{16,8},{24,16},{0,24},{40,32},{48,40},{56,48},{32,56},{72,64... | collective-permute-start | bytes 393224 | tf_op jit(solution)/shard_map/ppermute | solution.py:416
  129.5 8.0 %collective-permute-start.42 = (f32[128,256]{1,0:T(8,128)S(1)}, f32[128,256]{1,0:T(8,128)S(1)}, u32[]{:S(2)}, u32[]{:S(2)}) collective-permute-start(f32[128,256]{1,0:T(8,128)S(1)} %slice.23), channel_id=1, source_target_pairs={{0,8},{8,16},{16,24},{24,0},{32,40},{40,48},{48,56},{56,32},{64,72... | collective-permute-start | bytes 393224 | tf_op jit(solution)/shard_map/ppermute | solution.py:416

commit v7 on v6

--- a/solution.py
+++ b/solution.py
@@ -19,7 +19,7 @@
 F32 = jnp.float32
 BF16 = jnp.bfloat16
 BOTH = ("row", "col")
-AROUND = 160
+AROUND = 96
 DIRECT = NB - 2 * AROUND
 UPDATE_COST = 60
 

time: 141 us -> 140 us (level)
  waiting for transfers between devices: 58.8 us -> 56.5 us
  transfers between devices with their start and end apart: 43 -> 43, of which waited for: 13 -> 12; matrix products, arithmetic and copies ran while one was open for 1% -> 2% of each run, Pallas kernels for 9% -> 9%
where the time goes in v7:
time: 140 us
  starting transfers between devices  59.8 us (43%)
  waiting for transfers between devices  56.5 us (40%)
  Pallas kernels  16.8 us (12%)
  local copies, waits for them, and re-layouts  2.63 us (2%)
  other arithmetic  2.34 us (2%)
  between operations  1.63 us (1%)
    pallas_call x7, Pallas kernels, call(): pl.pallas_call(kernel, out_shape=[(pltpu.HBM if len(shape) == 3 else jax....  16.8 us
    ppermute x1, waiting for transfers between devices, scatter_first(): relay = lax.ppermute(two, 'row', [(0, 3)])  16.2 us
    ppermute x3, waiting for transfers between devices, scatter_second(): lax.ppermute(pieces[i], 'row', [(1, (1 + i) % XS)])  10.4 us
    ppermute x1, waiting for transfers between devices, far_chip(): return lax.ppermute(ahead, BOTH, pairs(-1, 1, has))  9.14 us
    ppermute x2, starting transfers between devices, near_chips(): return (lax.ppermute(chunk, BOTH, pairs(-1, 0, has)), behind)  8.35 us
    ppermute x2, starting transfers between devices, over_x(): lax.ppermute(mine, 'row', TO_NEXT)  8.12 us
    ppermute x2, starting transfers between devices, across_x(): lax.ppermute(before[Q // 2:], 'row', TO_NEXT)  6.99 us
    ppermute x2, waiting for transfers between devices, near_chips(): behind = lax.ppermute(chunk, BOTH, pairs(1, 0, has))  6.71 us
  transfers between devices with their start and end apart: 43, of which 12 were waited for; matrix products, arithmetic and copies ran while one was open for 2% of the time, Pallas kernels for 9%

profile of v7, /device:TPU:6, one launch (start us, length us, event | category | flops | bytes accessed | tf_op | source)
XLA Modules:
  0.0 139.7 jit_solution(9064287062064617490)
XLA Ops:
  0.7 0.1 pad_add_fusion.place
  0.8 1.3 copy-done.19
  2.0 0.6 payload.1
  2.7 3.5 %collective-permute-start.3 = (f32[512,256]{1,0:T(8,128)S(1)}, f32[512,256]{1,0:T(8,128)S(1)}, u32[]{:S(2)}, u32[]{:S(2)}) collective-permute-start(f32[512,256]{1,0:T(8,128)S(1)} %get-tuple-element.33.rest_0_), channel_id=1, source_target_pairs={{0,2},{1,3},{8,10},{9,11},{10,12},{11,13},{12,14},{13,15},{14,8},{... | collective-permute-start | bytes 1572872 | tf_op jit(solution)/shard_map/ppermute | solution.py:110
  6.2 3.6 %collective-permute-start.1 = (f32[512,256]{1,0:T(8,128)S(1)}, f32[512,256]{1,0:T(8,128)S(1)}, u32[]{:S(2)}, u32[]{:S(2)}) collective-permute-start(f32[512,256]{1,0:T(8,128)S(1)} %get-tuple-element.33.rest_0_), channel_id=1, source_target_pairs={{0,6},{1,7},{8,14},{9,15},{10,8},{11,9},{12,10},{13,11},{14,12},{1... | collective-permute-start | bytes 1572872 | tf_op jit(solution)/shard_map/ppermute | solution.py:111
  9.8 0.1 collective-permute-start
  9.9 2.3 %collective-permute-start.10 = (f32[512,256]{1,0:T(8,128)S(1)}, f32[512,256]{1,0:T(8,128)S(1)}, u32[]{:S(2)}, u32[]{:S(2)}) collective-permute-start(f32[512,256]{1,0:T(8,128)S(1)} %get-tuple-element.34.rest_8_), channel_id=1, source_target_pairs={{0,2},{1,3},{2,4},{3,5},{8,10},{9,11},{10,12},{11,13},{12,14},{13,... | collective-permute-start | bytes 1572872 | tf_op jit(solution)/shard_map/ppermute | solution.py:110
  12.1 4.8 %collective-permute-start.8 = (f32[512,256]{1,0:T(8,128)S(1)}, f32[512,256]{1,0:T(8,128)S(1)}, u32[]{:S(2)}, u32[]{:S(2)}) collective-permute-start(f32[512,256]{1,0:T(8,128)S(1)} %get-tuple-element.34.rest_8_), channel_id=1, source_target_pairs={{0,6},{1,7},{2,0},{3,1},{8,14},{9,15},{10,8},{11,9},{12,10},{13,11... | collective-permute-start | bytes 1572872 | tf_op jit(solution)/shard_map/ppermute | solution.py:111
  16.9 3.7 %collective-permute-done.3.rest_4_ = f32[512,256]{1,0:T(8,128)S(1)} collective-permute-done((f32[512,256]{1,0:T(8,128)S(1)}, f32[512,256]{1,0:T(8,128)S(1)}, u32[]{:S(2)}, u32[]{:S(2)}) %collective-permute-start.3) | collective-permute-done | bytes 524320 | tf_op jit(solution)/shard_map/ppermute | solution.py:110
  20.6 2.3 %collective-permute-done.1.rest_2_ = f32[512,256]{1,0:T(8,128)S(1)} collective-permute-done((f32[512,256]{1,0:T(8,128)S(1)}, f32[512,256]{1,0:T(8,128)S(1)}, u32[]{:S(2)}, u32[]{:S(2)}) %collective-permute-start.1) | collective-permute-done | bytes 524320 | tf_op jit(solution)/shard_map/ppermute | solution.py:111
  22.9 4.8 %collective-permute-start.5 = (f32[512,256]{1,0:T(8,128)S(1)}, f32[512,256]{1,0:T(8,128)S(1)}, u32[]{:S(2)}, u32[]{:S(2)}) collective-permute-start(f32[512,256]{1,0:T(8,128)S(1)} %collective-permute-done.1.rest_2_), channel_id=1, source_target_pairs={{6,4},{7,5},{8,14},{9,15},{10,8},{11,9},{12,10},{13,11},{14,12},{1... | collective-permute-start | bytes 1572872 | tf_op jit(solution)/shard_map/ppermute | solution.py:116
  27.7 3.0 %collective-permute-done.10.rest_12_ = f32[512,256]{1,0:T(8,128)S(1)} collective-permute-done((f32[512,256]{1,0:T(8,128)S(1)}, f32[512,256]{1,0:T(8,128)S(1)}, u32[]{:S(2)}, u32[]{:S(2)}) %collective-permute-start.10) | collective-permute-done | bytes 524320 | tf_op jit(solution)/shard_map/ppermute | solution.py:110
  30.8 2.2 %collective-permute-start.12 = (f32[512,256]{1,0:T(8,128)S(1)}, f32[512,256]{1,0:T(8,128)S(1)}, u32[]{:S(2)}, u32[]{:S(2)}) collective-permute-start(f32[512,256]{1,0:T(8,128)S(1)} %collective-permute-done.10.rest_12_), channel_id=1, source_target_pairs={{2,4},{3,5},{4,6},{5,7},{8,10},{9,11},{10,12},{11,13},{12,14},{13,... | collective-permute-start | bytes 1572872 | tf_op jit(solution)/shard_map/ppermute | solution.py:117
  33.0 1.2 collective-permute-done.8.rest_10_
  34.2 0.5 collective-permute-start.11
  34.7 0.1 collective-permute-start.9
  34.8 9.1 %collective-permute-done.5.rest_6_ = f32[512,256]{1,0:T(8,128)S(1)} collective-permute-done((f32[512,256]{1,0:T(8,128)S(1)}, f32[512,256]{1,0:T(8,128)S(1)}, u32[]{:S(2)}, u32[]{:S(2)}) %collective-permute-start.5) | collective-permute-done | bytes 524320 | tf_op jit(solution)/shard_map/ppermute | solution.py:116
  43.9 2.8 %collective-permute-done.12.rest_14_ = f32[512,256]{1,0:T(8,128)S(1)} collective-permute-done((f32[512,256]{1,0:T(8,128)S(1)}, f32[512,256]{1,0:T(8,128)S(1)}, u32[]{:S(2)}, u32[]{:S(2)}) %collective-permute-start.12) | collective-permute-done | bytes 524320 | tf_op jit(solution)/shard_map/ppermute | solution.py:117
  46.8 1.8 %collective-permute-done.13.rest_15_ = f32[512,256]{1,0:T(8,128)S(1)} collective-permute-done((f32[512,256]{1,0:T(8,128)S(1)}, f32[512,256]{1,0:T(8,128)S(1)}, u32[]{:S(2)}, u32[]{:S(2)}) %collective-permute-start.13) | collective-permute-done | bytes 524320 | tf_op jit(solution)/shard_map/ppermute | solution.py:106
  48.6 1.6 %solve.1 = (f32[832,256]{1,0:T(8,128)}, f32[96,256]{1,0:T(8,128)S(1)}, f32[96,256]{1,0:T(8,128)S(1)}, f32[256,256]{1,0:T(8,128)S(1)}, f32[256,256]{1,0:T(8,128)S(1)}) custom-call(s32[4]{0:T(128)S(1)} %pad_add_fusion.place, f32[1024,256]{1,0:T(8,128)S(1)} %copy-done.16, f32[512,256]{1,0:T(8,128)S(1)} %get-tuple-element.33.rest_0_, ...), custom_call_target="tpu_custom_call" | custom-call | flops 536870912 | bytes 8388608 | tf_op jit(solution)/shard_map/solve/pallas_call | solution.py:39
  50.4 0.7 collective-permute-start.14
  51.1 0.7 collective-permute-start.15
  51.8 1.3 collective-permute-start.16
  53.1 0.7 collective-permute-start.18
  53.8 1.3 collective-permute-start.19
  55.1 16.2 %collective-permute-done.16 = f32[256,256]{1,0:T(8,128)S(1)} collective-permute-done((f32[256,256]{1,0:T(8,128)S(1)}, f32[256,256]{1,0:T(8,128)S(1)}, u32[]{:S(2)}, u32[]{:S(2)}) %collective-permute-start.16) | collective-permute-done | bytes 262176 | tf_op jit(solution)/shard_map/ppermute | solution.py:391
  71.3 1.3 collective-permute-start.17
  72.6 0.7 collective-permute-start.22
  73.2 0.7 collective-permute-start.20
  73.9 1.2 copy-done.17
  75.2 1.0 prepare.1
  76.2 0.7 collective-permute-start.23
  76.9 0.7 collective-permute-start.21
  77.6 1.0 fusion
  78.6 1.3 collective-permute-start.25
  79.9 2.0 %collective-permute-start.24 = (f32[256,256]{1,0:T(8,128)S(1)}, f32[256,256]{1,0:T(8,128)}, u32[]{:S(2)}, u32[]{:S(2)}) collective-permute-start(f32[256,256]{1,0:T(8,128)S(1)} %fusion), channel_id=1, source_target_pairs={{0,96},{8,104},{16,112},{24,120},{1,97},{9,105},{17,113},{25,121},... | collective-permute-start | bytes 786440 | tf_op jit(solution)/shard_map/ppermute | solution.py:400
  81.9 0.5 combine.1
  82.5 0.7 collective-permute-start.30
  83.2 1.3 collective-permute-start.28
  84.5 0.7 collective-permute-start.29
  85.2 1.0 add_select_fusion.4
  86.2 1.3 collective-permute-start.27
  87.5 1.3 collective-permute-start.26
  88.9 10.4 %collective-permute-done.28 = f32[256,256]{1,0:T(8,128)S(1)} collective-permute-done((f32[256,256]{1,0:T(8,128)S(1)}, f32[256,256]{1,0:T(8,128)S(1)}, u32[]{:S(2)}, u32[]{:S(2)}) %collective-permute-start.28) | collective-permute-done | bytes 262176 | tf_op jit(solution)/shard_map/ppermute | solution.py:396
  99.3 0.1 add_select_fusion.2
  99.4 1.4 %collective-permute-start.32 = (f32[256,256]{1,0:T(8,128)S(1)}, f32[256,256]{1,0:T(8,128)S(1)}, u32[]{:S(2)}, u32[]{:S(2)}) collective-permute-start(f32[256,256]{1,0:T(8,128)S(1)} %add_select_fusion.2), channel_id=1, source_target_pairs={{0,160},{8,168},{16,176},{24,184},{1,161},{9,169},{17,177},{25,185... | collective-permute-start | bytes 786440 | tf_op jit(solution)/shard_map/ppermute | solution.py:401
  100.8 1.3 collective-permute-start.31
  102.2 0.1 add_select_fusion.3.rest_16_
  102.2 4.8 %collective-permute-start.35 = (f32[256,256]{1,0:T(8,128)S(1)}, f32[256,256]{1,0:T(8,128)S(1)}, u32[]{:S(2)}, u32[]{:S(2)}) collective-permute-start(f32[256,256]{1,0:T(8,128)S(1)} %add_select_fusion.3.rest_16_), channel_id=1, source_target_pairs={{0,8},{8,16},{16,24},{24,0},{32,40},{40,48},{48,56},{56,32},{64,72... | collective-permute-start | bytes 786440 | tf_op jit(solution)/shard_map/ppermute | solution.py:412
  107.1 0.1 add_select_fusion.1
  107.1 1.3 collective-permute-start.38
  108.4 1.3 collective-permute-start.37
  109.8 1.7 %collective-permute-done.35.rest_20_ = f32[256,256]{1,0:T(8,128)S(1)} collective-permute-done((f32[256,256]{1,0:T(8,128)S(1)}, f32[256,256]{1,0:T(8,128)S(1)}, u32[]{:S(2)}, u32[]{:S(2)}) %collective-permute-start.35) | collective-permute-done | bytes 262176 | tf_op jit(solution)/shard_map/ppermute | solution.py:412
  111.5 3.8 %collective-permute-start.36 = (f32[128,256]{1,0:T(8,128)S(1)}, f32[128,256]{1,0:T(8,128)S(1)}, u32[]{:S(2)}, u32[]{:S(2)}) collective-permute-start(f32[128,256]{1,0:T(8,128)S(1)} %slice.26), channel_id=1, source_target_pairs={{0,8},{8,16},{16,24},{24,0},{32,40},{40,48},{48,56},{56,32},{64,72... | collective-permute-start | bytes 393224 | tf_op jit(solution)/shard_map/ppermute | solution.py:416
  115.3 0.3 collective-permute-start.34
  115.6 0.1 add_select_fusion.rest_16_
  115.7 3.3 %collective-permute-start.40 = (f32[256,256]{1,0:T(8,128)S(1)}, f32[256,256]{1,0:T(8,128)S(1)}, u32[]{:S(2)}, u32[]{:S(2)}) collective-permute-start(f32[256,256]{1,0:T(8,128)S(1)} %add_select_fusion.rest_16_), channel_id=1, source_target_pairs={{0,8},{8,16},{16,24},{24,0},{32,40},{40,48},{48,56},{56,32},{64,72... | collective-permute-start | bytes 786440 | tf_op jit(solution)/shard_map/ppermute | solution.py:412
  119.0 0.2 collective-permute-done.36.rest_19_
  119.1 4.0 %collective-permute-done.34.rest_18_ = f32[128,256]{1,0:T(8,128)S(1)} collective-permute-done((f32[128,256]{1,0:T(8,128)S(1)}, f32[128,256]{1,0:T(8,128)S(1)}, u32[]{:S(2)}, u32[]{:S(2)}) %collective-permute-start.34) | collective-permute-done | bytes 131104 | tf_op jit(solution)/shard_map/ppermute | solution.py:416
  123.1 5.8 %update.1 = (f32[1024,256]{1,0:T(8,128)S(1)}, f32[2048,256]{1,0:T(8,128)}) custom-call(s32[4]{0:T(128)S(1)} %pad_add_fusion.place, f32[1024,256]{1,0:T(8,128)S(1)} %copy-done.18, f32[512,256]{1,0:T(8,128)} %copy-done, f32[512,256]{1,0:T(8,128)} %copy-done.4, f32[512,256]{1,0:T(8,128)} %copy-done.3, f32[512,256]{1,0:T(8,128)} %copy-done.11, ...), custom_call_target="tpu_custom_call" | custom-call | flops 16106127360 | bytes 8388608 | tf_op jit(solution)/shard_map/update/pallas_call | solution.py:39
  128.9 0.1 collective-permute-start.41
  129.0 3.2 %collective-permute-start.42 = (f32[128,256]{1,0:T(8,128)S(1)}, f32[128,256]{1,0:T(8,128)S(1)}, u32[]{:S(2)}, u32[]{:S(2)}) collective-permute-start(f32[128,256]{1,0:T(8,128)S(1)} %slice.23), channel_id=1, source_target_pairs={{0,8},{8,16},{16,24},{24,0},{32,40},{40,48},{48,56},{56,32},{64,72... | collective-permute-start | bytes 393224 | tf_op jit(solution)/shard_map/ppermute | solution.py:416
  132.2 4.7 %most.1 = (f32[1024,256]{1,0:T(8,128)S(1)}, f32[2048,256]{1,0:T(8,128)}, f32[1024,256]{1,0:T(8,128)S(1)}) custom-call(s32[4]{0:T(128)S(1)} %pad_add_fusion.place, f32[1024,256]{1,0:T(8,128)S(1)} %get-tuple-element.57.target, f32[512,256]{1,0:T(8,128)} %copy-done, f32[512,256]{1,0:T(8,128)} %copy-done.4, ...), custom_call_target="tpu_custom_call", output_to_operand_aliasing={{1}: (21, {})} | custom-call | flops 1610612736 | bytes 8388608 | tf_op jit(solution)/shard_map/most/pallas_call | solution.py:39
  137.0 2.5 %last.1 = (f32[1024,256]{1,0:T(8,128)}, f32[2048,256]{1,0:T(8,128)}) custom-call(s32[4]{0:T(128)S(1)} %pad_add_fusion.place, f32[1024,256]{1,0:T(8,128)S(1)} %get-tuple-element.61.target, f32[1024,256]{1,0:T(8,128)S(1)} %get-tuple-element.62.block, f32[128,256]{1,0:T(8,128)S(1)} %collective-permute-done.41.upper, ...), custom_call_target="tpu_custom_call", output_to_operand_aliasing={{1}: (5, {})} | custom-call | flops 536870912 | bytes 8388608 | tf_op jit(solution)/shard_map/last/pallas_call | solution.py:39
  (80 shorter events, 0.2 us)
Async XLA Ops:
  0.7 48.0 %copy-start.16 = (f32[1024,256]{1,0:T(8,128)S(1)}, f32[1024,256]{1,0:T(8,128)}, u32[]{:S(2)}) copy-start(f32[1024,256]{1,0:T(8,128)} %target.1) | copy-start | bytes 3145732
  0.7 1.3 copy-start.19
  2.7 47.6 %copy-start = (f32[512,256]{1,0:T(8,128)}, f32[512,256]{1,0:T(8,128)S(1)}, u32[]{:S(2)}) copy-start(f32[512,256]{1,0:T(8,128)S(1)} %get-tuple-element.33.rest_0_) | copy-start | bytes 1572868
  2.7 47.6 %copy-start.1 = (f32[512,256]{1,0:T(8,128)}, f32[512,256]{1,0:T(8,128)S(1)}, u32[]{:S(2)}) copy-start(f32[512,256]{1,0:T(8,128)S(1)} %get-tuple-element.34.rest_8_) | copy-start | bytes 1572868
  2.7 17.9 %collective-permute-start.3 = (f32[512,256]{1,0:T(8,128)S(1)}, f32[512,256]{1,0:T(8,128)S(1)}, u32[]{:S(2)}, u32[]{:S(2)}) collective-permute-start(f32[512,256]{1,0:T(8,128)S(1)} %get-tuple-element.33.rest_0_), channel_id=1, source_target_pairs={{0,2},{1,3},{8,10},{9,11},{10,12},{11,13},{12,14},{13,15},{14,8},{... | collective-permute-start | bytes 1572872 | tf_op jit(solution)/shard_map/ppermute | solution.py:110
  6.2 16.7 %collective-permute-start.1 = (f32[512,256]{1,0:T(8,128)S(1)}, f32[512,256]{1,0:T(8,128)S(1)}, u32[]{:S(2)}, u32[]{:S(2)}) collective-permute-start(f32[512,256]{1,0:T(8,128)S(1)} %get-tuple-element.33.rest_0_), channel_id=1, source_target_pairs={{0,6},{1,7},{8,14},{9,15},{10,8},{11,9},{12,10},{13,11},{14,12},{1... | collective-permute-start | bytes 1572872 | tf_op jit(solution)/shard_map/ppermute | solution.py:111
  9.8 13.2 %collective-permute-start = (f32[512,256]{1,0:T(8,128)S(1)}, f32[512,256]{1,0:T(8,128)S(1)}, u32[]{:S(2)}, u32[]{:S(2)}) collective-permute-start(f32[512,256]{1,0:T(8,128)S(1)} %get-tuple-element.33.rest_0_), channel_id=1, source_target_pairs={{0,1},{1,0},{2,3},{3,2},{4,5},{5,4},{6,7},{7,6},{8,9},{9,8},{10,11... | collective-permute-start | bytes 1572872 | tf_op jit(solution)/shard_map/ppermute | solution.py:106
  9.9 20.9 %collective-permute-start.10 = (f32[512,256]{1,0:T(8,128)S(1)}, f32[512,256]{1,0:T(8,128)S(1)}, u32[]{:S(2)}, u32[]{:S(2)}) collective-permute-start(f32[512,256]{1,0:T(8,128)S(1)} %get-tuple-element.34.rest_8_), channel_id=1, source_target_pairs={{0,2},{1,3},{2,4},{3,5},{8,10},{9,11},{10,12},{11,13},{12,14},{13,... | collective-permute-start | bytes 1572872 | tf_op jit(solution)/shard_map/ppermute | solution.py:110
  12.1 22.0 %collective-permute-start.8 = (f32[512,256]{1,0:T(8,128)S(1)}, f32[512,256]{1,0:T(8,128)S(1)}, u32[]{:S(2)}, u32[]{:S(2)}) collective-permute-start(f32[512,256]{1,0:T(8,128)S(1)} %get-tuple-element.34.rest_8_), channel_id=1, source_target_pairs={{0,6},{1,7},{2,0},{3,1},{8,14},{9,15},{10,8},{11,9},{12,10},{13,11... | collective-permute-start | bytes 1572872 | tf_op jit(solution)/shard_map/ppermute | solution.py:111
  20.6 29.7 %copy-start.2 = (f32[512,256]{1,0:T(8,128)}, f32[512,256]{1,0:T(8,128)S(1)}, u32[]{:S(2)}) copy-start(f32[512,256]{1,0:T(8,128)S(1)} %collective-permute-done.3.rest_4_) | copy-start | bytes 1572868
  20.6 13.6 %collective-permute-start.7 = (f32[512,256]{1,0:T(8,128)S(1)}, f32[512,256]{1,0:T(8,128)S(1)}, u32[]{:S(2)}, u32[]{:S(2)}) collective-permute-start(f32[512,256]{1,0:T(8,128)S(1)} %get-tuple-element.34.rest_8_), channel_id=1, source_target_pairs={{0,1},{1,0},{2,3},{3,2},{4,5},{5,4},{6,7},{7,6},{8,9},{9,8},{10,11... | collective-permute-start | bytes 1572872 | tf_op jit(solution)/shard_map/ppermute | solution.py:106
  22.9 27.4 %copy-start.3 = (f32[512,256]{1,0:T(8,128)}, f32[512,256]{1,0:T(8,128)S(1)}, u32[]{:S(2)}) copy-start(f32[512,256]{1,0:T(8,128)S(1)} %collective-permute-done.1.rest_2_) | copy-start | bytes 1572868
  22.9 11.8 %collective-permute-start.4 = (f32[512,256]{1,0:T(8,128)S(1)}, f32[512,256]{1,0:T(8,128)S(1)}, u32[]{:S(2)}, u32[]{:S(2)}) collective-permute-start(f32[512,256]{1,0:T(8,128)S(1)} %collective-permute-done.3.rest_4_), channel_id=1, source_target_pairs={{0,1},{1,0},{2,3},{3,2},{4,5},{5,4},{6,7},{7,6},{8,9},{9,8},{10,11... | collective-permute-start | bytes 1572872 | tf_op jit(solution)/shard_map/ppermute | solution.py:106
  22.9 27.4 %copy-start.4 = (f32[512,256]{1,0:T(8,128)}, f32[512,256]{1,0:T(8,128)S(1)}, u32[]{:S(2)}) copy-start(f32[512,256]{1,0:T(8,128)S(1)} %collective-permute-done.rest_1_) | copy-start | bytes 1572868
  22.9 21.0 %collective-permute-start.5 = (f32[512,256]{1,0:T(8,128)S(1)}, f32[512,256]{1,0:T(8,128)S(1)}, u32[]{:S(2)}, u32[]{:S(2)}) collective-permute-start(f32[512,256]{1,0:T(8,128)S(1)} %collective-permute-done.1.rest_2_), channel_id=1, source_target_pairs={{6,4},{7,5},{8,14},{9,15},{10,8},{11,9},{12,10},{13,11},{14,12},{1... | collective-permute-start | bytes 1572872 | tf_op jit(solution)/shard_map/ppermute | solution.py:116
  30.8 19.5 %copy-start.5 = (f32[512,256]{1,0:T(8,128)}, f32[512,256]{1,0:T(8,128)S(1)}, u32[]{:S(2)}) copy-start(f32[512,256]{1,0:T(8,128)S(1)} %collective-permute-done.10.rest_12_) | copy-start | bytes 1572868
  30.8 16.0 %collective-permute-start.12 = (f32[512,256]{1,0:T(8,128)S(1)}, f32[512,256]{1,0:T(8,128)S(1)}, u32[]{:S(2)}, u32[]{:S(2)}) collective-permute-start(f32[512,256]{1,0:T(8,128)S(1)} %collective-permute-done.10.rest_12_), channel_id=1, source_target_pairs={{2,4},{3,5},{4,6},{5,7},{8,10},{9,11},{10,12},{11,13},{12,14},{13,... | collective-permute-start | bytes 1572872 | tf_op jit(solution)/shard_map/ppermute | solution.py:117
  34.2 16.2 %copy-start.6 = (f32[512,256]{1,0:T(8,128)}, f32[512,256]{1,0:T(8,128)S(1)}, u32[]{:S(2)}) copy-start(f32[512,256]{1,0:T(8,128)S(1)} %collective-permute-done.8.rest_10_) | copy-start | bytes 1572868
  34.2 12.6 %collective-permute-start.2 = (f32[512,256]{1,0:T(8,128)S(1)}, f32[512,256]{1,0:T(8,128)S(1)}, u32[]{:S(2)}, u32[]{:S(2)}) collective-permute-start(f32[512,256]{1,0:T(8,128)S(1)} %collective-permute-done.1.rest_2_), channel_id=1, source_target_pairs={{0,1},{1,0},{2,3},{3,2},{4,5},{5,4},{6,7},{7,6},{8,9},{9,8},{10,11... | collective-permute-start | bytes 1572872 | tf_op jit(solution)/shard_map/ppermute | solution.py:106
  34.2 16.2 %copy-start.7 = (f32[512,256]{1,0:T(8,128)}, f32[512,256]{1,0:T(8,128)S(1)}, u32[]{:S(2)}) copy-start(f32[512,256]{1,0:T(8,128)S(1)} %collective-permute-done.7.rest_9_) | copy-start | bytes 1572868
  34.2 12.6 %collective-permute-start.11 = (f32[512,256]{1,0:T(8,128)S(1)}, f32[512,256]{1,0:T(8,128)S(1)}, u32[]{:S(2)}, u32[]{:S(2)}) collective-permute-start(f32[512,256]{1,0:T(8,128)S(1)} %collective-permute-done.10.rest_12_), channel_id=1, source_target_pairs={{0,1},{1,0},{2,3},{3,2},{4,5},{5,4},{6,7},{7,6},{8,9},{9,8},{10,11... | collective-permute-start | bytes 1572872 | tf_op jit(solution)/shard_map/ppermute | solution.py:106
  34.7 15.7 %copy-start.8 = (f32[512,256]{1,0:T(8,128)}, f32[512,256]{1,0:T(8,128)S(1)}, u32[]{:S(2)}) copy-start(f32[512,256]{1,0:T(8,128)S(1)} %collective-permute-done.4.rest_5_) | copy-start | bytes 1572868
  34.7 12.1 %collective-permute-start.9 = (f32[512,256]{1,0:T(8,128)S(1)}, f32[512,256]{1,0:T(8,128)S(1)}, u32[]{:S(2)}, u32[]{:S(2)}) collective-permute-start(f32[512,256]{1,0:T(8,128)S(1)} %collective-permute-done.8.rest_10_), channel_id=1, source_target_pairs={{0,1},{1,0},{2,3},{3,2},{4,5},{5,4},{6,7},{7,6},{8,9},{9,8},{10,11... | collective-permute-start | bytes 1572872 | tf_op jit(solution)/shard_map/ppermute | solution.py:106
  43.9 6.4 %copy-start.9 = (f32[512,256]{1,0:T(8,128)}, f32[512,256]{1,0:T(8,128)S(1)}, u32[]{:S(2)}) copy-start(f32[512,256]{1,0:T(8,128)S(1)} %collective-permute-done.5.rest_6_) | copy-start | bytes 1572868
  43.9 2.9 %collective-permute-start.6 = (f32[512,256]{1,0:T(8,128)S(1)}, f32[512,256]{1,0:T(8,128)S(1)}, u32[]{:S(2)}, u32[]{:S(2)}) collective-permute-start(f32[512,256]{1,0:T(8,128)S(1)} %collective-permute-done.5.rest_6_), channel_id=1, source_target_pairs={{0,1},{1,0},{2,3},{3,2},{4,5},{5,4},{6,7},{7,6},{8,9},{9,8},{10,11... | collective-permute-start | bytes 1572872 | tf_op jit(solution)/shard_map/ppermute | solution.py:106
  46.7 3.6 %copy-start.10 = (f32[512,256]{1,0:T(8,128)}, f32[512,256]{1,0:T(8,128)S(1)}, u32[]{:S(2)}) copy-start(f32[512,256]{1,0:T(8,128)S(1)} %collective-permute-done.12.rest_14_) | copy-start | bytes 1572868
  46.7 1.9 %collective-permute-start.13 = (f32[512,256]{1,0:T(8,128)S(1)}, f32[512,256]{1,0:T(8,128)S(1)}, u32[]{:S(2)}, u32[]{:S(2)}) collective-permute-start(f32[512,256]{1,0:T(8,128)S(1)} %collective-permute-done.12.rest_14_), channel_id=1, source_target_pairs={{0,1},{1,0},{2,3},{3,2},{4,5},{5,4},{6,7},{7,6},{8,9},{9,8},{10,11... | collective-permute-start | bytes 1572872 | tf_op jit(solution)/shard_map/ppermute | solution.py:106
  46.7 3.6 %copy-start.11 = (f32[512,256]{1,0:T(8,128)}, f32[512,256]{1,0:T(8,128)S(1)}, u32[]{:S(2)}) copy-start(f32[512,256]{1,0:T(8,128)S(1)} %collective-permute-done.2.rest_3_) | copy-start | bytes 1572868
  46.8 3.6 %copy-start.12 = (f32[512,256]{1,0:T(8,128)}, f32[512,256]{1,0:T(8,128)S(1)}, u32[]{:S(2)}) copy-start(f32[512,256]{1,0:T(8,128)S(1)} %collective-permute-done.11.rest_13_) | copy-start | bytes 1572868
  46.8 3.6 %copy-start.13 = (f32[512,256]{1,0:T(8,128)}, f32[512,256]{1,0:T(8,128)S(1)}, u32[]{:S(2)}) copy-start(f32[512,256]{1,0:T(8,128)S(1)} %collective-permute-done.9.rest_11_) | copy-start | bytes 1572868
  46.8 3.6 %copy-start.14 = (f32[512,256]{1,0:T(8,128)}, f32[512,256]{1,0:T(8,128)S(1)}, u32[]{:S(2)}) copy-start(f32[512,256]{1,0:T(8,128)S(1)} %collective-permute-done.6.rest_7_) | copy-start | bytes 1572868
  48.6 1.8 %copy-start.15 = (f32[512,256]{1,0:T(8,128)}, f32[512,256]{1,0:T(8,128)S(1)}, u32[]{:S(2)}) copy-start(f32[512,256]{1,0:T(8,128)S(1)} %collective-permute-done.13.rest_15_) | copy-start | bytes 1572868
  50.4 27.2 %collective-permute-start.14 = (f32[832,256]{1,0:T(8,128)}, f32[832,256]{1,0:T(8,128)S(1)}, u32[]{:S(2)}, u32[]{:S(2)}) collective-permute-start(f32[832,256]{1,0:T(8,128)} %get-tuple-element.35), channel_id=1, source_target_pairs={{0,8},{1,9},{2,10},{3,11},{4,12},{5,13},{6,14},{7,15}} | collective-permute-start | bytes 2555912 | tf_op jit(solution)/shard_map/ppermute | solution.py:446
  51.1 0.7 collective-permute-start.15
  51.8 19.4 %collective-permute-start.16 = (f32[256,256]{1,0:T(8,128)S(1)}, f32[256,256]{1,0:T(8,128)S(1)}, u32[]{:S(2)}, u32[]{:S(2)}) collective-permute-start(f32[256,256]{1,0:T(8,128)S(1)} %get-tuple-element.38), channel_id=1, source_target_pairs={{0,24},{1,25},{2,26},{3,27},{4,28},{5,29},{6,30},{7,31}} | collective-permute-start | bytes 786440 | tf_op jit(solution)/shard_map/ppermute | solution.py:391
  53.1 0.7 collective-permute-start.18
  53.8 23.8 %collective-permute-start.19 = (f32[256,256]{1,0:T(8,128)S(1)}, f32[256,256]{1,0:T(8,128)S(1)}, u32[]{:S(2)}, u32[]{:S(2)}) collective-permute-start(f32[256,256]{1,0:T(8,128)S(1)} %get-tuple-element.41), channel_id=1, source_target_pairs={{0,24},{1,25},{2,26},{3,27},{4,28},{5,29},{6,30},{7,31}} | collective-permute-start | bytes 786440 | tf_op jit(solution)/shard_map/ppermute | solution.py:392
  71.3 6.3 %collective-permute-start.17 = (f32[256,256]{1,0:T(8,128)S(1)}, f32[256,256]{1,0:T(8,128)S(1)}, u32[]{:S(2)}, u32[]{:S(2)}) collective-permute-start(f32[256,256]{1,0:T(8,128)S(1)} %collective-permute-done.16), channel_id=1, source_target_pairs={{24,16},{25,17},{26,18},{27,19},{28,20},{29,21},{30,22},{31,23}} | collective-permute-start | bytes 786440 | tf_op jit(solution)/shard_map/ppermute | solution.py:392
  72.6 3.6 %collective-permute-start.22 = (f32[96,256]{1,0:T(8,128)S(1)}, f32[96,256]{1,0:T(8,128)S(1)}, u32[]{:S(2)}, u32[]{:S(2)}) collective-permute-start(f32[96,256]{1,0:T(8,128)S(1)} %collective-permute-done.15), channel_id=1, source_target_pairs={{224,232},{225,233},{226,234},{227,235},{228,236},{229,237},{230,2... | collective-permute-start | bytes 294920 | tf_op jit(solution)/shard_map/ppermute | solution.py:445
  73.2 3.6 %collective-permute-start.20 = (f32[96,256]{1,0:T(8,128)S(1)}, f32[96,256]{1,0:T(8,128)S(1)}, u32[]{:S(2)}, u32[]{:S(2)}) collective-permute-start(f32[96,256]{1,0:T(8,128)S(1)} %collective-permute-done.18), channel_id=1, source_target_pairs={{32,40},{33,41},{34,42},{35,43},{36,44},{37,45},{38,46},{39,47}} | collective-permute-start | bytes 294920 | tf_op jit(solution)/shard_map/ppermute | solution.py:443
  73.9 1.2 copy-start.17
  76.2 2.4 %collective-permute-start.23 = (f32[96,256]{1,0:T(8,128)S(1)}, f32[96,256]{1,0:T(8,128)S(1)}, u32[]{:S(2)}, u32[]{:S(2)}) collective-permute-start(f32[96,256]{1,0:T(8,128)S(1)} %collective-permute-done.22), channel_id=1, source_target_pairs={{232,8},{233,9},{234,10},{235,11},{236,12},{237,13},{238,14},{239,... | collective-permute-start | bytes 294920 | tf_op jit(solution)/shard_map/ppermute | solution.py:445
  76.9 1.7 %collective-permute-start.21 = (f32[96,256]{1,0:T(8,128)S(1)}, f32[96,256]{1,0:T(8,128)S(1)}, u32[]{:S(2)}, u32[]{:S(2)}) collective-permute-start(f32[96,256]{1,0:T(8,128)S(1)} %collective-permute-done.20), channel_id=1, source_target_pairs={{40,8},{41,9},{42,10},{43,11},{44,12},{45,13},{46,14},{47,15}} | collective-permute-start | bytes 294920 | tf_op jit(solution)/shard_map/ppermute | solution.py:443
  78.6 6.6 %collective-permute-start.25 = (f32[256,256]{1,0:T(8,128)S(1)}, f32[256,256]{1,0:T(8,128)S(1)}, u32[]{:S(2)}, u32[]{:S(2)}) collective-permute-start(f32[256,256]{1,0:T(8,128)S(1)} %fusion), channel_id=1, source_target_pairs={{0,160},{8,168},{16,176},{24,184},{1,161},{9,169},{17,177},{25,185... | collective-permute-start | bytes 786440 | tf_op jit(solution)/shard_map/ppermute | solution.py:401
  79.9 5.3 %collective-permute-start.24 = (f32[256,256]{1,0:T(8,128)S(1)}, f32[256,256]{1,0:T(8,128)}, u32[]{:S(2)}, u32[]{:S(2)}) collective-permute-start(f32[256,256]{1,0:T(8,128)S(1)} %fusion), channel_id=1, source_target_pairs={{0,96},{8,104},{16,112},{24,120},{1,97},{9,105},{17,113},{25,121},... | collective-permute-start | bytes 786440 | tf_op jit(solution)/shard_map/ppermute | solution.py:400
  82.5 6.3 %collective-permute-start.30 = (f32[256,256]{1,0:T(8,128)S(1)}, f32[256,256]{1,0:T(8,128)S(1)}, u32[]{:S(2)}, u32[]{:S(2)}) collective-permute-start(f32[256,256]{1,0:T(8,128)S(1)} %get-tuple-element.47), channel_id=1, source_target_pairs={{8,16},{9,17},{10,18},{11,19},{12,20},{13,21},{14,22},{15,23}} | collective-permute-start | bytes 786440 | tf_op jit(solution)/shard_map/ppermute | solution.py:396
  83.2 16.1 %collective-permute-start.28 = (f32[256,256]{1,0:T(8,128)S(1)}, f32[256,256]{1,0:T(8,128)S(1)}, u32[]{:S(2)}, u32[]{:S(2)}) collective-permute-start(f32[256,256]{1,0:T(8,128)S(1)} %get-tuple-element.48), channel_id=1, source_target_pairs={{8,24},{9,25},{10,26},{11,27},{12,28},{13,29},{14,30},{15,31}} | collective-permute-start | bytes 786440 | tf_op jit(solution)/shard_map/ppermute | solution.py:396
  84.5 14.8 %collective-permute-start.29 = (f32[256,256]{1,0:T(8,128)S(1)}, f32[256,256]{1,0:T(8,128)S(1)}, u32[]{:S(2)}, u32[]{:S(2)}) collective-permute-start(f32[256,256]{1,0:T(8,128)S(1)} %get-tuple-element.49), channel_id=1, source_target_pairs={{8,0},{9,1},{10,2},{11,3},{12,4},{13,5},{14,6},{15,7}} | collective-permute-start | bytes 786440 | tf_op jit(solution)/shard_map/ppermute | solution.py:396
  86.2 15.9 %collective-permute-start.27 = (f32[256,256]{1,0:T(8,128)S(1)}, f32[256,256]{1,0:T(8,128)S(1)}, u32[]{:S(2)}, u32[]{:S(2)}) collective-permute-start(f32[256,256]{1,0:T(8,128)S(1)} %add_select_fusion.4), channel_id=1, source_target_pairs={{0,224},{8,232},{16,240},{24,248},{96,64},{104,72},{112,80},{120,8... | collective-permute-start | bytes 786440 | tf_op jit(solution)/shard_map/ppermute | solution.py:407
  87.5 14.6 %collective-permute-start.26 = (f32[256,256]{1,0:T(8,128)S(1)}, f32[256,256]{1,0:T(8,128)S(1)}, u32[]{:S(2)}, u32[]{:S(2)}) collective-permute-start(f32[256,256]{1,0:T(8,128)S(1)} %add_select_fusion.4), channel_id=1, source_target_pairs={{0,32},{8,40},{16,48},{24,56},{96,128},{104,136},{112,144},{120,15... | collective-permute-start | bytes 786440 | tf_op jit(solution)/shard_map/ppermute | solution.py:406
  99.3 23.8 %copy-start.18 = (f32[1024,256]{1,0:T(8,128)S(1)}, f32[1024,256]{1,0:T(8,128)}, u32[]{:S(2)}) copy-start(f32[1024,256]{1,0:T(8,128)} %target.1) | copy-start | bytes 3145732
  99.4 7.7 %collective-permute-start.32 = (f32[256,256]{1,0:T(8,128)S(1)}, f32[256,256]{1,0:T(8,128)S(1)}, u32[]{:S(2)}, u32[]{:S(2)}) collective-permute-start(f32[256,256]{1,0:T(8,128)S(1)} %add_select_fusion.2), channel_id=1, source_target_pairs={{0,160},{8,168},{16,176},{24,184},{1,161},{9,169},{17,177},{25,185... | collective-permute-start | bytes 786440 | tf_op jit(solution)/shard_map/ppermute | solution.py:401
  100.8 6.3 %collective-permute-start.31 = (f32[256,256]{1,0:T(8,128)S(1)}, f32[256,256]{1,0:T(8,128)S(1)}, u32[]{:S(2)}, u32[]{:S(2)}) collective-permute-start(f32[256,256]{1,0:T(8,128)S(1)} %add_select_fusion.2), channel_id=1, source_target_pairs={{0,96},{8,104},{16,112},{24,120},{1,97},{9,105},{17,113},{25,121},... | collective-permute-start | bytes 786440 | tf_op jit(solution)/shard_map/ppermute | solution.py:400
  102.2 9.3 %collective-permute-start.35 = (f32[256,256]{1,0:T(8,128)S(1)}, f32[256,256]{1,0:T(8,128)S(1)}, u32[]{:S(2)}, u32[]{:S(2)}) collective-permute-start(f32[256,256]{1,0:T(8,128)S(1)} %add_select_fusion.3.rest_16_), channel_id=1, source_target_pairs={{0,8},{8,16},{16,24},{24,0},{32,40},{40,48},{48,56},{56,32},{64,72... | collective-permute-start | bytes 786440 | tf_op jit(solution)/shard_map/ppermute | solution.py:412
  107.1 8.2 %collective-permute-start.33 = (f32[256,256]{1,0:T(8,128)S(1)}, f32[256,256]{1,0:T(8,128)S(1)}, u32[]{:S(2)}, u32[]{:S(2)}) collective-permute-start(f32[256,256]{1,0:T(8,128)S(1)} %add_select_fusion.3.rest_16_), channel_id=1, source_target_pairs={{8,0},{16,8},{24,16},{0,24},{40,32},{48,40},{56,48},{32,56},{72,64... | collective-permute-start | bytes 786440 | tf_op jit(solution)/shard_map/ppermute | solution.py:412
  107.1 8.5 %collective-permute-start.38 = (f32[256,256]{1,0:T(8,128)S(1)}, f32[256,256]{1,0:T(8,128)S(1)}, u32[]{:S(2)}, u32[]{:S(2)}) collective-permute-start(f32[256,256]{1,0:T(8,128)S(1)} %add_select_fusion.1), channel_id=1, source_target_pairs={{0,224},{8,232},{16,240},{24,248},{96,64},{104,72},{112,80},{120,8... | collective-permute-start | bytes 786440 | tf_op jit(solution)/shard_map/ppermute | solution.py:407
  108.4 7.2 %collective-permute-start.37 = (f32[256,256]{1,0:T(8,128)S(1)}, f32[256,256]{1,0:T(8,128)S(1)}, u32[]{:S(2)}, u32[]{:S(2)}) collective-permute-start(f32[256,256]{1,0:T(8,128)S(1)} %add_select_fusion.1), channel_id=1, source_target_pairs={{0,32},{8,40},{16,48},{24,56},{96,128},{104,136},{112,144},{120,15... | collective-permute-start | bytes 786440 | tf_op jit(solution)/shard_map/ppermute | solution.py:406
  111.5 7.7 %collective-permute-start.36 = (f32[128,256]{1,0:T(8,128)S(1)}, f32[128,256]{1,0:T(8,128)S(1)}, u32[]{:S(2)}, u32[]{:S(2)}) collective-permute-start(f32[128,256]{1,0:T(8,128)S(1)} %slice.26), channel_id=1, source_target_pairs={{0,8},{8,16},{16,24},{24,0},{32,40},{40,48},{48,56},{56,32},{64,72... | collective-permute-start | bytes 393224 | tf_op jit(solution)/shard_map/ppermute | solution.py:416
  115.3 7.8 %collective-permute-start.34 = (f32[128,256]{1,0:T(8,128)S(1)}, f32[128,256]{1,0:T(8,128)S(1)}, u32[]{:S(2)}, u32[]{:S(2)}) collective-permute-start(f32[128,256]{1,0:T(8,128)S(1)} %slice.25), channel_id=1, source_target_pairs={{8,0},{16,8},{24,16},{0,24},{40,32},{48,40},{56,48},{32,56},{72,64... | collective-permute-start | bytes 393224 | tf_op jit(solution)/shard_map/ppermute | solution.py:416
  115.7 13.2 %collective-permute-start.40 = (f32[256,256]{1,0:T(8,128)S(1)}, f32[256,256]{1,0:T(8,128)S(1)}, u32[]{:S(2)}, u32[]{:S(2)}) collective-permute-start(f32[256,256]{1,0:T(8,128)S(1)} %add_select_fusion.rest_16_), channel_id=1, source_target_pairs={{0,8},{8,16},{16,24},{24,0},{32,40},{40,48},{48,56},{56,32},{64,72... | collective-permute-start | bytes 786440 | tf_op jit(solution)/shard_map/ppermute | solution.py:412
  119.0 9.9 %collective-permute-start.39 = (f32[256,256]{1,0:T(8,128)S(1)}, f32[256,256]{1,0:T(8,128)S(1)}, u32[]{:S(2)}, u32[]{:S(2)}) collective-permute-start(f32[256,256]{1,0:T(8,128)S(1)} %add_select_fusion.rest_16_), channel_id=1, source_target_pairs={{8,0},{16,8},{24,16},{0,24},{40,32},{48,40},{56,48},{32,56},{72,64... | collective-permute-start | bytes 786440 | tf_op jit(solution)/shard_map/ppermute | solution.py:412
  128.9 8.1 %collective-permute-start.41 = (f32[128,256]{1,0:T(8,128)S(1)}, f32[128,256]{1,0:T(8,128)S(1)}, u32[]{:S(2)}, u32[]{:S(2)}) collective-permute-start(f32[128,256]{1,0:T(8,128)S(1)} %slice.22), channel_id=1, source_target_pairs={{8,0},{16,8},{24,16},{0,24},{40,32},{48,40},{56,48},{32,56},{72,64... | collective-permute-start | bytes 393224 | tf_op jit(solution)/shard_map/ppermute | solution.py:416
  129.0 8.0 %collective-permute-start.42 = (f32[128,256]{1,0:T(8,128)S(1)}, f32[128,256]{1,0:T(8,128)S(1)}, u32[]{:S(2)}, u32[]{:S(2)}) collective-permute-start(f32[128,256]{1,0:T(8,128)S(1)} %slice.23), channel_id=1, source_target_pairs={{0,8},{8,16},{16,24},{24,0},{32,40},{40,48},{48,56},{56,32},{64,72... | collective-permute-start | bytes 393224 | tf_op jit(solution)/shard_map/ppermute | solution.py:416
